TPU v7x, 32 devices: a whole 2x2x4 slice. The times are simulated.
32 devices in a mesh: dp: 8 (over z, x), tensor: 4 (over y, core).
Axes of the slice: x: 2, y: 2, z: 4, core: 2. Of those that a mesh axis runs over, the one named last changes fastest.
Arguments:
- queries: bfloat16 [2048, 4096], P('dp', 'tensor'), may hold values from -6 to 6
- span_keys: bfloat16 [2048, 1024], P('dp', 'tensor'), may hold values from -6 to 6
- span_values: bfloat16 [2048, 1024], P('dp', 'tensor'), may hold values from -6 to 6
- cache_keys: bfloat16 [2048, 1024], P(None, 'tensor'), may hold values from -6 to 6
- cache_values: bfloat16 [2048, 1024], P(None, 'tensor'), may hold values from -6 to 6
- out_proj: bfloat16 [4096, 8192], P('tensor'), may hold values from -0.09375 to 0.09375
- out_grad: bfloat16 [2048, 8192], P('dp', 'tensor'), may hold values from -6 to 6
- doc_ids: int32 [8, 256], P('dp'), may hold values from 0 to 15, never falling along the last dimension, each value on 1 to 128 neighbouring positions
Outputs:
- attended: bfloat16 [2048, 4096], P('dp', 'tensor')
- new_keys: float32 [2048, 1024], P('dp', 'tensor')
- new_values: float32 [2048, 1024], P('dp', 'tensor')
All inputs are finite; a program needn't handle non-finite values.
Results may differ from a plain program's by a relative error of at most 0.0055.
Values may be sent and summed in bfloat16 or wider, within the bound.
No kernel may reach another device: no remote copies, remote signals or barrier semaphores. Data moves between devices by JAX's collectives and lax.ppermute only.
A program may use at most 192 MiB of HBM per device.

v0:
```python
import math

import jax
import jax.numpy as jnp
from jax import lax
from jax.sharding import PartitionSpec as P

HD = 128
KVH = 8
SLOTS = 2048


step_rate = 0.25
epsilon = 1e-06


def seq_terms(query_rows, span_k, span_v, seq_docs, cache_k, cache_v, grad_att):
    length = query_rows.shape[0]
    slots = cache_k.shape[0]
    kv_heads = cache_k.shape[1] // HD
    group = query_rows.shape[1] // (kv_heads * HD)
    scale_factor = 1.0 / math.sqrt(HD)
    query_four = query_rows.reshape(length, kv_heads, group, HD)
    all_keys = jnp.concatenate([cache_k, span_k], 0).reshape(slots + length, kv_heads, HD)
    all_vals = jnp.concatenate([cache_v, span_v], 0).reshape(slots + length, kv_heads, HD)
    scores = (
        jnp.einsum("tgjd,kgd->gjtk", query_four, all_keys, preferred_element_type=jnp.float32)
        * scale_factor
    )
    places = jnp.arange(length)
    span_ok = (seq_docs[None, :] == seq_docs[:, None]) & (places[None, :] <= places[:, None])
    allowed = jnp.concatenate([jnp.ones((length, slots), bool), span_ok], 1)
    scores = jnp.where(allowed, scores, -1e30)
    highest = jnp.max(scores, -1, keepdims=True)
    expo = jnp.exp(scores - highest)
    probs = expo / jnp.sum(expo, -1, keepdims=True)
    probs_b = probs.astype(jnp.bfloat16)
    attended = jnp.einsum(
        "gjtk,kgd->tgjd", probs_b, all_vals, preferred_element_type=jnp.float32
    ).astype(jnp.bfloat16)
    grad_four = grad_att.reshape(length, kv_heads, group, HD)
    grad_probs = jnp.einsum(
        "tgjd,kgd->gjtk", grad_four, all_vals, preferred_element_type=jnp.float32
    )
    row_dot = jnp.sum(grad_four.astype(jnp.float32) * attended.astype(jnp.float32), -1).transpose(
        1, 2, 0
    )
    grad_scores = (probs * (grad_probs - row_dot[..., None])).astype(jnp.bfloat16)
    grad_keys = (
        jnp.einsum(
            "gjtk,tgjd->kgd",
            grad_scores[..., :slots],
            query_four,
            preferred_element_type=jnp.float32,
        )
        * scale_factor
    )
    grad_vals = jnp.einsum(
        "gjtk,tgjd->kgd", probs_b[..., :slots], grad_four, preferred_element_type=jnp.float32
    )
    return (
        attended.reshape(length, -1),
        grad_keys.reshape(slots, -1),
        grad_vals.reshape(slots, -1),
    )


def body(queries, span_keys, span_values, cache_keys, cache_values, out_proj, out_grad, doc_ids):
    grad_att = lax.dot_general(
        lax.all_gather(out_grad, "tensor", axis=1, tiled=True),
        out_proj,
        (((1,), (1,)), ((), ())),
        preferred_element_type=jnp.float32,
    ).astype(jnp.bfloat16)
    attended, grad_keys, grad_vals = seq_terms(
        queries, span_keys, span_values, doc_ids[0], cache_keys, cache_values, grad_att
    )
    count = 2 * SLOTS * KVH * HD
    share_rows = cache_keys.shape[0] // lax.axis_size("dp")
    offset = lax.axis_index("dp") * share_rows
    own_keys = lax.dynamic_slice_in_dim(cache_keys, offset, share_rows, 0).astype(jnp.float32)
    own_vals = lax.dynamic_slice_in_dim(cache_values, offset, share_rows, 0).astype(jnp.float32)
    grad_keys, grad_vals = (
        lax.psum(grad_keys.astype(jnp.bfloat16), "dp").astype(jnp.float32),
        lax.psum(grad_vals.astype(jnp.bfloat16), "dp").astype(jnp.float32),
    )
    local_squares = jnp.sum(grad_keys * grad_keys) + jnp.sum(grad_vals * grad_vals)
    total = lax.psum(local_squares, "tensor")
    share_keys = lax.dynamic_slice_in_dim(grad_keys, offset, share_rows, 0)
    share_vals = lax.dynamic_slice_in_dim(grad_vals, offset, share_rows, 0)
    rms_value = jnp.sqrt(total / count + epsilon)
    new_keys = own_keys - step_rate * share_keys / rms_value
    new_values = own_vals - step_rate * share_vals / rms_value
    return (attended, new_keys, new_values)


def solution(mesh):
    placed = (
        P("dp", "tensor"),
        P("dp", "tensor"),
        P("dp", "tensor"),
        P(None, "tensor"),
        P(None, "tensor"),
        P("tensor", None),
        P("dp", "tensor"),
        P("dp", None),
    )
    return jax.shard_map(
        body,
        mesh=mesh,
        in_specs=placed,
        out_specs=(P("dp", "tensor"), P("dp", "tensor"), P("dp", "tensor")),
        check_vma=False,
    )
```

profile of v0, /device:TPU:0, one launch (start us, length us, event | category | flops | bytes accessed | tf_op | source)
XLA Modules:
  0.0 219.6 jit_solution(8408911809954539206)
XLA Ops:
  7.2 0.0 copy-start.3
  7.2 0.0 copy-start.4
  7.2 0.0 all-gather.2.cloned.1.call-start
  7.2 0.7 all-gather.2.cloned.1.call-update
  7.9 0.0 all-reduce.4.cloned.1.call-start
  8.0 1.0 copy.23
  9.0 2.0 copy.43
  11.0 1.5 copy.22
  12.5 0.0 copy-done.3
  12.5 1.0 pad_maximum_fusion
  13.5 0.7 copy.21
  14.2 0.0 copy-done.4
  14.3 0.1 fusion.27
  14.4 1.0 concatenate.10
  15.3 0.1 pad_maximum_fusion.1
  15.4 12.0 %fusion.31 = (f32[2,4,256]{2,1,0:T(4,128)S(1)}, f32[2,4,256,2304]{2,3,1,0:T(8,128)}) fusion(bf16[2304,2,128,1]{0,2,3,1:T(8,128)(2,1)S(1)} %bitcast.70, bf16[256,2,4,128]{0,3,2,1:T(8,128)(2,1)} %bitcast.67, pred[256,2304]{0,1:T(8,128)(4,1)} %concatenate.10), kind=kOutput, calls=%fused_computation.35 | convolution fusion | flops 1226836224 | bytes 21176320 | tf_op jit(solution)/shard_map/sub | solution.py:35
  27.4 16.4 %fusion.30 = (bf16[2,4,256,2304]{2,3,1,0:T(8,128)(2,1)}, f32[2,4,256,2304]{2,3,1,0:T(8,128)}) fusion(f32[2,4,256,2304]{2,3,1,0:T(8,128)} %get-tuple-element.14, f32[2,4,256]{2,1,0:T(4,128)S(1)} %get-tuple-element.13), kind=kLoop, calls=%fused_computation.34 | loop fusion | flops 9437184 | bytes 47194112 | tf_op jit(solution)/shard_map/convert_element_type | solution.py:37
  43.8 3.0 %all-gather.2.cloned.1.call-done = bf16[256,8192]{1,0:T(8,128)(2,1)} async-done(((bf16[256,2048]{1,0:T(8,128)(2,1)}), bf16[256,8192]{1,0:T(8,128)(2,1)}) %all-gather.2.cloned.1.call-update) | async-done | bytes 4194320 | tf_op jit(solution)/shard_map/all_gather | solution.py:70
  46.8 11.6 %convolution_convert_fusion.1 = bf16[256,1024]{1,0:T(8,128)(2,1)S(1)} fusion(bf16[256,8192]{1,0:T(8,128)(2,1)} %all-gather.2.cloned.1.call-done, bf16[1024,8192]{1,0:T(8,128)(2,1)} %param.13), kind=kOutput, calls=%fused_computation.24 | convolution fusion | flops 4295229440 | bytes 21495808 | tf_op jit(solution)/shard_map/dot_general | solution.py:69
  58.4 0.2 copy.27
  58.6 0.0 copy-start
  58.6 5.2 %multiply_reduce_fusion.2 = (f32[256,2,4]{0,2,1:T(4,128)S(1)}, bf16[2,128,4,256]{3,1,2,0:T(8,128)(2,1)S(1)}) fusion(bf16[256,1024]{0,1:T(8,128)(2,1)S(1)} %copy.27, bf16[2304,2,128,1]{0,2,3,1:T(8,128)(2,1)S(1)} %bitcast.62, bf16[2,4,256,2304]{2,3,1,0:T(8,128)(2,1)} %get-tuple-element.11), kind=kOutput, calls=%fused_computation.27 | convolution fusion | flops 1209268224 | bytes 11673600 | tf_op jit(solution)/shard_map/gjtk,kgd->tgjd/dot_general | solution.py:38
  63.8 1.1 copy-done
  64.9 3.8 %fusion.24 = bf16[2,128,2048]{2,1,0:T(8,128)(2,1)} fusion(bf16[256,2,4,128]{0,3,2,1:T(8,128)(2,1)S(1)} %bitcast.64, bf16[2,4,256,2304]{2,3,1,0:T(8,128)(2,1)S(1)} %copy-done), kind=kOutput, calls=%fused_computation.20 | convolution fusion | flops 1074266112 | bytes 9961472 | tf_op jit(solution)/shard_map/gjtk,tgjd->kgd/dot_general | solution.py:58
  68.7 0.0 copy-start.2
  68.7 7.9 %convolution_bitcast_fusion = f32[2,4,256,2304]{2,3,1,0:T(8,128)} fusion(bf16[2304,2,128,1]{0,2,3,1:T(8,128)(2,1)S(1)} %bitcast.63, bf16[256,2,4,128]{0,3,2,1:T(8,128)(2,1)S(1)} %bitcast.65), kind=kOutput, calls=%fused_computation.8 | convolution fusion | flops 1207959552 | bytes 20578304 | tf_op jit(solution)/shard_map/tgjd,kgd->gjtk/dot_general | solution.py:42
  76.6 2.3 %copy.32 = bf16[2048,256]{1,0:T(8,128)(2,1)} copy(bf16[2048,256]{0,1:T(8,128)(2,1)} %bitcast.71) | data formatting | bytes 2097152 | tf_op jit(solution)/shard_map/convert_element_type | solution.py:85
  78.9 0.0 copy-done.2
  78.9 12.3 %fusion.21 = bf16[2,2048,128]{1,2,0:T(8,128)(2,1)S(1)} fusion(bf16[256,2,4,128]{0,3,2,1:T(8,128)(2,1)S(1)} %bitcast.68, f32[2,4,256,2304]{2,3,1,0:T(8,128)} %get-tuple-element.12, f32[2,4,256,2304]{2,3,1,0:T(8,128)} %convolution_bitcast_fusion, f32[2,4,256]{2,1,0:T(4,128)S(1)} %bitcast.72), kind=kOutput, calls=%fused_computation.19 | convolution fusion | flops 1087373312 | bytes 35135488 | tf_op jit(solution)/shard_map/gjtk,tgjd->kgd/dot_general | solution.py:50
  91.2 1.3 copy.30
  92.6 0.0 all-reduce.4.cloned.1.call-update
  92.6 1.0 copy.33
  93.6 101.3 %all-reduce.4.cloned.1.call-done = (bf16[2048,256]{1,0:T(8,128)(2,1)}, bf16[2048,256]{1,0:T(8,128)(2,1)}) async-done(((bf16[2048,256]{1,0:T(8,128)(2,1)}, bf16[2048,256]{1,0:T(8,128)(2,1)}), (bf16[2048,256]{1,0:T(8,128)(2,1)}, bf16[2048,256]{1,0:T(8,128)(2,1)})) %all-reduce.4.cloned.1.call-update) | async-done | bytes 2097168 | tf_op jit(solution)/shard_map/psum | solution.py:84
  194.9 0.0 copy-start.1
  194.9 1.5 convert_element_type.62
  196.4 2.7 %multiply_reduce_fusion = (f32[]{:T(128)}, f32[]{:T(128)}) fusion(bf16[2048,256]{1,0:T(8,128)(2,1)} %get-tuple-element.10, bf16[2048,256]{1,0:T(8,128)(2,1)} %get-tuple-element.9), kind=kLoop, calls=%fused_computation.21 | loop fusion | flops 3145726 | bytes 2097160 | tf_op jit(solution)/shard_map/reduce_sum | solution.py:87
  200.4 0.0 copy-done.1
  200.4 1.5 convert_element_type.66
  201.9 6.8 %psum.23 = f32[]{:T(128)} all-reduce(f32[]{:T(128)S(6)} %add.19), channel_id=1, replica_groups=mesh['dp'=8,'tensor'=4] {'tensor'}, use_global_device_ids=true, to_apply=%region_7.8 | all-reduce | flops 1 | bytes 8 | tf_op jit(solution)/shard_map/psum | solution.py:88
  209.4 1.7 divide_subtract_fusion.1
  211.0 1.7 divide_subtract_fusion
Async XLA Ops:
  7.2 5.3 %copy-start.3 = (bf16[2048,256]{1,0:T(8,128)(2,1)S(1)}, bf16[2048,256]{1,0:T(8,128)(2,1)}, u32[]{:S(2)}) copy-start(bf16[2048,256]{1,0:T(8,128)(2,1)} %param.12) | copy-start | bytes 3145732
  7.2 7.1 %copy-start.4 = (s32[1,256]{1,0:T(1,128)S(1)}, s32[1,256]{1,0:T(1,128)}, u32[]{:S(2)}) copy-start(s32[1,256]{1,0:T(1,128)} %param.15) | copy-start | bytes 3076
  7.2 39.6 %all-gather.2.cloned.1.call-start = ((), (), s32[]{:S(2)}) async-start(), calls=%async_computation | async-start | bytes 5242880 | tf_op jit(solution)/shard_map/all_gather | solution.py:70
  7.9 187.0 %all-reduce.4.cloned.1.call-start = ((), (), s32[]{:S(2)}) async-start(), calls=%async_computation.1 | async-start | bytes 4194304 | tf_op jit(solution)/shard_map/psum | solution.py:84
  58.6 6.4 %copy-start = (bf16[2,4,256,2304]{2,3,1,0:T(8,128)(2,1)S(1)}, bf16[2,4,256,2304]{2,3,1,0:T(8,128)(2,1)}, u32[]{:S(2)}) copy-start(bf16[2,4,256,2304]{2,3,1,0:T(8,128)(2,1)} %get-tuple-element.11) | copy-start | bytes 28311556
  68.7 10.2 %copy-start.2 = (bf16[256,1024]{0,1:T(8,128)(2,1)S(1)}, bf16[256,1024]{0,1:T(8,128)(2,1)}, u32[]{:S(2)}) copy-start(bf16[256,1024]{0,1:T(8,128)(2,1)} %copy.43) | copy-start | bytes 1572868
  194.9 5.5 %copy-start.1 = (bf16[2048,256]{1,0:T(8,128)(2,1)S(1)}, bf16[2048,256]{1,0:T(8,128)(2,1)}, u32[]{:S(2)}) copy-start(bf16[2048,256]{1,0:T(8,128)(2,1)} %get-tuple-element.10) | copy-start | bytes 3145732
Sparse Core Ops, SparseCore 0:
  9.6 37.1 all-gather.1
  92.7 102.1 all-reduce.3
where the time goes:
time: 220 us
  waiting for transfers between devices  105 us (48%)
  matrix products  52.8 us (24%)
  other arithmetic  26.6 us (12%)
  between operations  16.2 us (7%)
  local copies, waits for them, and re-layouts  12.2 us (6%)
  blocking collectives  6.81 us (3%)
    psum x1, waiting for transfers between devices, body(): lax.psum(grad_keys.astype(jnp.bfloat16), 'dp').astype(jnp.float32)  101 us
    convert_element_type x1, other arithmetic, seq_terms(): probs_b = probs.astype(jnp.bfloat16)  16.4 us
    dot_general x1, matrix products, seq_terms(): jnp.einsum('gjtk,tgjd->kgd', grad_scores[..., :slots], query_four, prefer...  12.3 us
    sub x1, matrix products, seq_terms(): expo = jnp.exp(scores - highest)  12 us
    dot_general x1, matrix products, body(): lax.dot_general(lax.all_gather(out_grad, 'tensor', axis=1, tiled=True), o...  11.6 us
    dot_general x1, matrix products, seq_terms(): jnp.einsum('tgjd,kgd->gjtk', grad_four, all_vals, preferred_element_type=...  7.89 us
    psum x1, blocking collectives, body(): total = lax.psum(local_squares, 'tensor')  6.81 us
    dot_general x1, matrix products, seq_terms(): jnp.einsum('gjtk,kgd->tgjd', probs_b, all_vals, preferred_element_type=jn...  5.24 us
  transfers between devices with their start and end apart: 2, of which 2 were waited for; matrix products, arithmetic and copies ran while one was open for 17% of the time, Pallas kernels for 0%

commit v1 on v0

v1 whole, which is shorter than its diff:
```python
import functools
import math

import jax
import jax.numpy as jnp
from jax import lax
from jax.experimental import pallas as pl
from jax.experimental.pallas import tpu as pltpu
from jax.sharding import PartitionSpec as P

HD = 128
KVH = 8
SLOTS = 2048

step_rate = 0.25
epsilon = 1e-06

F32 = jnp.float32
BF16 = jnp.bfloat16
NT = (((1,), (1,)), ((), ()))
NN = (((1,), (0,)), ((), ()))
TN = (((0,), (0,)), ((), ()))
MIB = 1 << 20


def mm(a, b, dims):
    return lax.dot_general(a, b, dims, preferred_element_type=F32)


def bit_orders(n, heads):
    bits = max(1, n.bit_length() - 1)
    first = list(range(bits))
    if n == 1:
        return [[] for _ in range(heads)]
    second = first[:]
    if bits > 1:
        second[0], second[1] = second[1], second[0]
    return [first if head % 2 == 0 else second for head in range(heads)]


def place_of(rel, order):
    place = 0
    for step, bit in enumerate(order):
        place = place + (((rel >> bit) & 1) << (len(order) - 1 - step))
    return place


def block_at(place, order):
    rel = 0
    for step, bit in enumerate(order):
        rel = rel + (((place >> (len(order) - 1 - step)) & 1) << bit)
    return rel


def per_head(g, orders, fn):
    even = fn(orders[0])
    if len(orders) == 1:
        return even
    return jnp.where(g % 2 == 0, even, fn(orders[1]))


def forward_kernel(orders, n, me_ref, q_ref, k_ref, ks_ref, v_ref, vs_ref, bias_ref, p_ref, att_ref, att_t_ref, s_ref):
    g = pl.program_id(0)
    me = me_ref[0]
    slots = k_ref.shape[0]
    length = q_ref.shape[0]
    share = slots // n
    chunk = 256
    scale = math.log2(math.e) / math.sqrt(HD)
    q = q_ref[...]
    steps = [(k_ref, v_ref, c, c, chunk) for c in range(0, slots, chunk)]
    steps.append((ks_ref, vs_ref, 0, slots, length))
    high = None
    for keys, _, at, row, size in steps:
        s = mm(keys[at : at + size, :], q, NT) * scale
        if keys is ks_ref:
            s = s + bias_ref[...]
        s_ref[row : row + size, :] = s
        top = jnp.max(s.reshape(size // 8, 8, length), axis=0)
        high = top if high is None else jnp.maximum(high, top)
    high = jnp.max(high, axis=0, keepdims=True)
    total = None
    for _, _, _, row, size in steps:
        e = jnp.exp2(s_ref[row : row + size, :] - high)
        s_ref[row : row + size, :] = e
        part = jnp.sum(e.reshape(size // 8, 8, length), axis=0)
        total = part if total is None else total + part
    inverse = 1.0 / jnp.sum(total, axis=0, keepdims=True)
    att = None
    for keys, values, at, row, size in steps:
        p = (s_ref[row : row + size, :] * inverse).astype(BF16)
        if keys is k_ref:
            piece = min(share, size)
            for b in range(0, size, piece):
                block, inside = (at + b) // share, (at + b) % share
                place = per_head(g, orders, functools.partial(place_of, block ^ me))
                start = pl.multiple_of(place * share + inside, piece)
                p_ref[0, 0, pl.ds(start, piece), :] = p[b : b + piece, :]
        part = mm(values[at : at + size, :], p, TN)
        att = part if att is None else att + part
    att_t_ref[...] = att.astype(BF16)
    att_ref[...] = att.T.astype(BF16)


def forward(me, queries, cache_k, span_k, cache_v, span_v, bias, orders, n):
    length, width = queries.shape
    slots, kv_width = cache_k.shape
    kv = kv_width // HD
    group = width // kv_width
    spec = pltpu.PrefetchScalarGridSpec(
        num_scalar_prefetch=1,
        grid=(kv, group),
        in_specs=[
            pl.BlockSpec((length, HD), lambda g, j, me: (0, g * group + j)),
            pl.BlockSpec((slots, HD), lambda g, j, me: (0, g)),
            pl.BlockSpec((length, HD), lambda g, j, me: (0, g)),
            pl.BlockSpec((slots, HD), lambda g, j, me: (0, g)),
            pl.BlockSpec((length, HD), lambda g, j, me: (0, g)),
            pl.BlockSpec((length, length), lambda g, j, me: (0, 0)),
        ],
        out_specs=[
            pl.BlockSpec((1, 1, slots, length), lambda g, j, me: (g, j, 0, 0)),
            pl.BlockSpec((length, HD), lambda g, j, me: (0, g * group + j)),
            pl.BlockSpec((HD, length), lambda g, j, me: (g * group + j, 0)),
        ],
        scratch_shapes=[pltpu.VMEM((slots + length, length), F32)],
    )
    return pl.pallas_call(
        functools.partial(forward_kernel, orders, n),
        grid_spec=spec,
        out_shape=[
            jax.ShapeDtypeStruct((kv, group, slots, length), BF16),
            jax.ShapeDtypeStruct((length, width), BF16),
            jax.ShapeDtypeStruct((width, length), BF16),
        ],
        compiler_params=pltpu.CompilerParams(vmem_limit_bytes=32 * MIB),
        cost_estimate=pl.CostEstimate(
            flops=4 * width * length * (slots + length),
            bytes_accessed=2 * width // HD * length * slots,
            transcendentals=width // HD * length * (slots + length),
        ),
        name="forward",
    )(me, queries, cache_k, span_k, cache_v, span_v, bias)


def project_kernel(first, shard_ref, w_ref, g_ref, *refs):
    out_ref = refs[-1]
    total = mm(w_ref[...], g_ref[...], NT)
    if not first:
        total = total + refs[0][...]
    out_ref[...] = total.astype(out_ref.dtype)


def project(shard, out_proj, grad, acc, dtype):
    rows = out_proj.shape[0]
    length, features = grad.shape
    block = min(256, rows)
    in_specs = [
        pl.BlockSpec((block, features), lambda m, shard: (m, shard[0])),
        pl.BlockSpec((length, features), lambda m, shard: (0, 0)),
    ]
    args = [out_proj, grad]
    if acc is not None:
        in_specs.append(pl.BlockSpec((block, length), lambda m, shard: (m, 0)))
        args.append(acc)
    return pl.pallas_call(
        functools.partial(project_kernel, acc is None),
        grid_spec=pltpu.PrefetchScalarGridSpec(
            num_scalar_prefetch=1,
            grid=(rows // block,),
            in_specs=in_specs,
            out_specs=pl.BlockSpec((block, length), lambda m, shard: (m, 0)),
        ),
        out_shape=jax.ShapeDtypeStruct((rows, length), dtype),
        compiler_params=pltpu.CompilerParams(vmem_limit_bytes=32 * MIB),
        cost_estimate=pl.CostEstimate(
            flops=2 * rows * length * features,
            bytes_accessed=2 * rows * features,
            transcendentals=0,
        ),
        name="project",
    )(shard.reshape(1), *args)


def values_kernel(p_ref, da_ref, out_ref):
    total = None
    for j in range(p_ref.shape[1]):
        part = mm(p_ref[0, j], da_ref[j * HD : (j + 1) * HD, :], NT)
        total = part if total is None else total + part
    out_ref[...] = total.astype(BF16)


def value_grads(head, probs, grad_att_t):
    _, group, slots, length = probs.shape
    rows = 512
    return pl.pallas_call(
        values_kernel,
        grid=(slots // rows,),
        in_specs=[
            pl.BlockSpec((1, group, rows, length), lambda i: (head, 0, i, 0)),
            pl.BlockSpec((group * HD, length), lambda i: (head, 0)),
        ],
        out_specs=pl.BlockSpec((rows, HD), lambda i: (i, 0)),
        out_shape=jax.ShapeDtypeStruct((slots, HD), BF16),
        compiler_params=pltpu.CompilerParams(vmem_limit_bytes=32 * MIB),
        cost_estimate=pl.CostEstimate(
            flops=2 * slots * length * group * HD,
            bytes_accessed=2 * slots * length * group,
            transcendentals=0,
        ),
        name="value_grads",
    )(probs, grad_att_t)


def keys_kernel(order, n, me_ref, p_ref, v_ref, da_ref, att_ref, q_ref, out_ref, dot_ref):
    i = pl.program_id(0)
    me = me_ref[0]
    group, rows = p_ref.shape[1], p_ref.shape[2]
    share = v_ref.shape[0] // n
    piece = min(share, rows)

    @pl.when(i == 0)
    def _():
        for j in range(group):
            cut = slice(j * HD, (j + 1) * HD)
            product = da_ref[cut, :].astype(F32) * att_ref[cut, :].astype(F32)
            dot_ref[j : j + 1, :] = jnp.sum(product, axis=0, keepdims=True)

    for b in range(0, rows, piece):
        row = i * rows + b
        place, inside = row // share, row % share
        block = block_at(place, order) ^ me
        start = pl.multiple_of(block * share + inside, piece)
        values = v_ref[pl.ds(start, piece), :]
        total = None
        for j in range(group):
            grad_p = mm(values, da_ref[j * HD : (j + 1) * HD, :], NN)
            p = p_ref[0, j, b : b + piece, :].astype(F32)
            grad_s = (p * (grad_p - dot_ref[j : j + 1, :])).astype(BF16)
            part = mm(grad_s, q_ref[:, j * HD : (j + 1) * HD], NN)
            total = part if total is None else total + part
        out_ref[b : b + piece, :] = (total * (1.0 / math.sqrt(HD))).astype(BF16)


def key_grads(head, me, probs, cache_v, grad_att_t, att_t, queries, order, n):
    _, group, slots, length = probs.shape
    rows = 512
    return pl.pallas_call(
        functools.partial(keys_kernel, order, n),
        grid_spec=pltpu.PrefetchScalarGridSpec(
            num_scalar_prefetch=1,
            grid=(slots // rows,),
            in_specs=[
                pl.BlockSpec((1, group, rows, length), lambda i, me: (head, 0, i, 0)),
                pl.BlockSpec((slots, HD), lambda i, me: (0, head)),
                pl.BlockSpec((group * HD, length), lambda i, me: (head, 0)),
                pl.BlockSpec((group * HD, length), lambda i, me: (head, 0)),
                pl.BlockSpec((length, group * HD), lambda i, me: (0, head)),
            ],
            out_specs=pl.BlockSpec((rows, HD), lambda i, me: (i, 0)),
            scratch_shapes=[pltpu.VMEM((max(8, group), length), F32)],
        ),
        out_shape=jax.ShapeDtypeStruct((slots, HD), BF16),
        compiler_params=pltpu.CompilerParams(vmem_limit_bytes=32 * MIB),
        cost_estimate=pl.CostEstimate(
            flops=4 * slots * length * group * HD,
            bytes_accessed=2 * slots * length * group,
            transcendentals=0,
        ),
        name="key_grads",
    )(me, probs, cache_v, grad_att_t, att_t, queries)


def exchange(value, axis, size, flip):
    return lax.ppermute(value, axis, [(i, i ^ flip) for i in range(size)])


def reduce_halving(part, order, n):
    for bit in order:
        half = part.shape[0] // 2
        got = exchange(part[half:], "dp", n, 1 << bit)
        total = part[:half].astype(F32) + got.astype(F32)
        part = total.astype(BF16)
    return total if order else part.astype(F32)


def body(queries, span_keys, span_values, cache_keys, cache_values, out_proj, out_grad, doc_ids):
    n = lax.axis_size("dp")
    t = lax.axis_size("tensor")
    mine = lax.axis_index("dp")
    shard = lax.axis_index("tensor")
    me = mine.astype(jnp.int32).reshape(1)
    length = queries.shape[0]
    kv = cache_keys.shape[1] // HD
    share = cache_keys.shape[0] // n
    orders = bit_orders(n, kv)

    far = [(exchange(out_grad, "tensor", t, 2 * s), 2 * s) for s in range(1, t // 2)]
    near = exchange(out_grad, "tensor", t, 1)

    docs = doc_ids[0]
    places = jnp.arange(length)
    span_ok = (docs[None, :] == docs[:, None]) & (places[:, None] <= places[None, :])
    bias = jnp.where(span_ok, 0.0, -1e30).astype(F32)
    probs, attended, att_t = forward(
        me, queries, cache_keys, span_keys, cache_values, span_values, bias, orders, n
    )

    acc = project(shard, out_proj, out_grad, None, F32)
    acc = project(shard ^ 1, out_proj, near, acc, F32)
    later = [(exchange(got, "tensor", t, 1), flip + 1) for got, flip in far]
    pieces = [pair for both in zip(far, later) for pair in both]
    for place, (got, flip) in enumerate(pieces):
        last = place == len(pieces) - 1
        acc = project(shard ^ flip, out_proj, got, acc, BF16 if last else F32)

    grads_v = [
        reduce_halving(value_grads(h, probs, acc), orders[h], n) for h in range(kv)
    ]
    grads_k = [
        reduce_halving(
            key_grads(h, me, probs, cache_values, acc, att_t, queries, orders[h], n), orders[h], n
        )
        for h in range(kv)
    ]
    share_keys = jnp.concatenate(grads_k, axis=1)
    share_vals = jnp.concatenate(grads_v, axis=1)
    squares = jnp.sum(share_keys * share_keys) + jnp.sum(share_vals * share_vals)
    spread = jnp.broadcast_to(squares, (n * t, 8, 128))
    spread = lax.all_to_all(spread, ("dp", "tensor"), split_axis=0, concat_axis=0, tiled=True)
    total = jnp.sum(spread[:, 0, 0])
    count = 2 * SLOTS * KVH * HD
    rms_value = jnp.sqrt(total / count + epsilon)
    offset = mine * share
    own_keys = lax.dynamic_slice_in_dim(cache_keys, offset, share, 0).astype(F32)
    own_vals = lax.dynamic_slice_in_dim(cache_values, offset, share, 0).astype(F32)
    new_keys = own_keys - step_rate * share_keys / rms_value
    new_values = own_vals - step_rate * share_vals / rms_value
    return (attended, new_keys, new_values)


def solution(mesh):
    placed = (
        P("dp", "tensor"),
        P("dp", "tensor"),
        P("dp", "tensor"),
        P(None, "tensor"),
        P(None, "tensor"),
        P("tensor", None),
        P("dp", "tensor"),
        P("dp", None),
    )
    return jax.shard_map(
        body,
        mesh=mesh,
        in_specs=placed,
        out_specs=(P("dp", "tensor"), P("dp", "tensor"), P("dp", "tensor")),
        check_vma=False,
    )
```

time: 220 us -> 126 us (0.57)
  waiting for transfers between devices: 105 us -> 43.7 us
  matrix products: 52.8 us -> 0 us
  Pallas kernels: 0 us -> 38.4 us
  starting transfers between devices: 0.08 us -> 22.7 us
  other arithmetic: 26.6 us -> 4.42 us
  between operations: 16.2 us -> 2.99 us
  blocking collectives: 6.81 us -> 0 us
    psum x1 -> x0, waiting for transfers between devices: 101 us -> none  [body(): lax.psum(grad_keys.astype(jnp.bfloat16), 'dp').astype(jnp.float32)]
    dot_general x5 -> x0, matrix products: 40.8 us -> none  [the longest x1 12.3 us: seq_terms(): jnp.einsum('gjtk,tgjd->kgd', grad_scores[..., :slots], query_four, prefer...]
    pallas_call x0 -> x9, Pallas kernels: none -> 38.4 us  [the longest x1 14.5 us: forward(): pl.pallas_call(functools.partial(forward_kernel, orders, n), grid_spec=sp...]
    ppermute x0 -> x15, waiting for transfers between devices: none -> 35.5 us  [exchange(): return lax.ppermute(value, axis, [(i, i ^ flip) for i in range(size)])]
    convert_element_type x3 -> x8, other arithmetic: 19.4 us -> 0.44 us  [reduce_halving(): part = total.astype(BF16)]
    ppermute x0 -> x15, starting transfers between devices: none -> 18.8 us  [exchange(): return lax.ppermute(value, axis, [(i, i ^ flip) for i in range(size)])]
    sub x1 -> x0, matrix products: 12 us -> none  [seq_terms(): expo = jnp.exp(scores - highest)]
    all_to_all x0 -> x1, waiting for transfers between devices: none -> 8.23 us  [body(): lax.all_to_all(spread, ('dp', 'tensor'), split_axis=0, concat_axis=0, til...]
  transfers between devices with their start and end apart: 2 -> 16, of which waited for: 2 -> 7; matrix products, arithmetic and copies ran while one was open for 17% -> 1% of each run, Pallas kernels for 0% -> 25%
where the time goes in v1:
time: 126 us
  waiting for transfers between devices  43.7 us (35%)
  Pallas kernels  38.4 us (30%)
  starting transfers between devices  22.7 us (18%)
  local copies, waits for them, and re-layouts  13.6 us (11%)
  other arithmetic  4.42 us (4%)
  between operations  2.99 us (2%)
    ppermute x15, waiting for transfers between devices, exchange(): return lax.ppermute(value, axis, [(i, i ^ flip) for i in range(size)])  35.5 us
    ppermute x15, starting transfers between devices, exchange(): return lax.ppermute(value, axis, [(i, i ^ flip) for i in range(size)])  18.8 us
    pallas_call x1, Pallas kernels, forward(): pl.pallas_call(functools.partial(forward_kernel, orders, n), grid_spec=sp...  14.5 us
    unnamed x18, local copies, waits for them, and re-layouts  12.8 us
    pallas_call x4, Pallas kernels, project(): pl.pallas_call(functools.partial(project_kernel, acc is None), grid_spec=...  10.1 us
    pallas_call x2, Pallas kernels, key_grads(): pl.pallas_call(functools.partial(keys_kernel, order, n), grid_spec=pltpu....  9.65 us
    all_to_all x1, waiting for transfers between devices, body(): lax.all_to_all(spread, ('dp', 'tensor'), split_axis=0, concat_axis=0, til...  8.23 us
    pallas_call x2, Pallas kernels, value_grads(): pl.pallas_call(values_kernel, grid=(slots // rows,), in_specs=[pl.BlockSp...  4.18 us
  transfers between devices with their start and end apart: 16, of which 7 were waited for; matrix products, arithmetic and copies ran while one was open for 1% of the time, Pallas kernels for 25%

profile of v1, /device:TPU:0, one launch (start us, length us, event | category | flops | bytes accessed | tf_op | source)
XLA Modules:
  0.0 125.9 jit_solution(11127892693248344027)
XLA Ops:
  0.6 3.0 %collective-permute-start = (bf16[256,2048]{1,0:T(8,128)(2,1)}, bf16[256,2048]{1,0:T(8,128)(2,1)S(1)}, u32[]{:S(2)}, u32[]{:S(2)}) collective-permute-start(bf16[256,2048]{1,0:T(8,128)(2,1)} %g_ref.1), channel_id=1, source_target_pairs={{0,2},{1,3},{2,0},{3,1},{4,6},{5,7},{6,4},{7,5},{8,10},{9,11},{10,... | collective-permute-start | bytes 3145736 | tf_op jit(solution)/shard_map/ppermute | solution.py:275
  3.7 23.4 %collective-permute-done.g_ref = bf16[256,2048]{1,0:T(8,128)(2,1)S(1)} collective-permute-done((bf16[256,2048]{1,0:T(8,128)(2,1)}, bf16[256,2048]{1,0:T(8,128)(2,1)S(1)}, u32[]{:S(2)}, u32[]{:S(2)}) %collective-permute-start) | collective-permute-done | bytes 1048608 | tf_op jit(solution)/shard_map/ppermute | solution.py:275
  27.0 0.0 collective-permute-start.1
  27.0 5.8 %copy-done = bf16[1024,8192]{1,0:T(8,128)(2,1)S(1)} copy-done((bf16[1024,8192]{1,0:T(8,128)(2,1)S(1)}, bf16[1024,8192]{1,0:T(8,128)(2,1)}, u32[]{:S(2)}) %copy-start) | copy-done | bytes 16777240
  32.8 1.2 copy-done.4
  34.1 2.2 %project.4.refs_0_ = f32[1024,256]{1,0:T(8,128)S(1)} custom-call(s32[1]{0:T(128)} %bitcast.5.shard_ref, bf16[1024,8192]{1,0:T(8,128)(2,1)S(1)} %copy-done, bf16[256,2048]{1,0:T(8,128)(2,1)S(1)} %copy-done.4), custom_call_target="tpu_custom_call" | custom-call | flops 1073741824 | bytes 4194304 | tf_op jit(solution)/shard_map/project/pallas_call | solution.py:166
  36.3 0.1 fusion.1.bias_ref
  36.5 14.5 %forward.1 = (bf16[2,4,2048,256]{3,2,1,0:T(8,128)(2,1)S(1)}, bf16[256,1024]{1,0:T(8,128)(2,1)}, bf16[1024,256]{1,0:T(8,128)(2,1)S(1)}) custom-call(s32[1]{0:T(128)} %bitcast.me_ref, bf16[256,1024]{1,0:T(8,128)(2,1)S(1)} %copy-done.3, bf16[2048,256]{1,0:T(8,128)(2,1)S(1)} %copy-done.5, bf16[256,256]{1,0:T(8,128)(2,1)S(1)} %copy-done.6, ...), custom_call_target="tpu_custom_call" | custom-call | flops 2415919104 | bytes 8388608 | tf_op jit(solution)/shard_map/forward/pallas_call | solution.py:128
  51.0 0.0 collective-permute-done.2.g_ref
  51.0 5.8 %copy-done.1 = bf16[1024,8192]{1,0:T(8,128)(2,1)S(1)} copy-done((bf16[1024,8192]{1,0:T(8,128)(2,1)S(1)}, bf16[1024,8192]{1,0:T(8,128)(2,1)}, u32[]{:S(2)}) %copy-start.1) | copy-done | bytes 16777240
  56.7 3.4 %project.5.refs_0_ = f32[1024,256]{1,0:T(8,128)S(1)} custom-call(s32[1]{0:T(128)} %bitcast.4.shard_ref, bf16[1024,8192]{1,0:T(8,128)(2,1)S(1)} %copy-done.1, bf16[256,2048]{1,0:T(8,128)(2,1)} %collective-permute-done.2.g_ref, f32[1024,256]{1,0:T(8,128)S(1)} %project.4.refs_0_), custom_call_target="tpu_custom_call" | custom-call | flops 1073741824 | bytes 4194304 | tf_op jit(solution)/shard_map/project/pallas_call | solution.py:166
  60.1 2.2 %project.6.refs_0_ = f32[1024,256]{1,0:T(8,128)S(1)} custom-call(s32[1]{0:T(128)} %bitcast.3.shard_ref, bf16[1024,8192]{1,0:T(8,128)(2,1)S(1)} %copy-done.1, bf16[256,2048]{1,0:T(8,128)(2,1)S(1)} %collective-permute-done.g_ref, f32[1024,256]{1,0:T(8,128)S(1)} %project.5.refs_0_), custom_call_target="tpu_custom_call" | custom-call | flops 1073741824 | bytes 4194304 | tf_op jit(solution)/shard_map/project/pallas_call | solution.py:166
  62.4 0.0 collective-permute-done.1.g_ref
  62.4 2.2 %project.7.da_ref = bf16[1024,256]{1,0:T(8,128)(2,1)S(1)} custom-call(s32[1]{0:T(128)} %bitcast.2.shard_ref, bf16[1024,8192]{1,0:T(8,128)(2,1)S(1)} %copy-done.1, bf16[256,2048]{1,0:T(8,128)(2,1)S(1)} %collective-permute-done.1.g_ref, f32[1024,256]{1,0:T(8,128)S(1)} %project.6.refs_0_), custom_call_target="tpu_custom_call" | custom-call | flops 1073741824 | bytes 4194304 | tf_op jit(solution)/shard_map/project/pallas_call | solution.py:166
  64.6 4.8 %key_grads.3 = bf16[2048,128]{1,0:T(8,128)(2,1)S(1)} custom-call(s32[1]{0:T(128)} %bitcast.me_ref, bf16[2,4,2048,256]{3,2,1,0:T(8,128)(2,1)S(1)} %get-tuple-element.7.p_ref, bf16[2048,256]{1,0:T(8,128)(2,1)S(1)} %copy-done.2, bf16[1024,256]{1,0:T(8,128)(2,1)S(1)} %project.7.da_ref, bf16[1024,256]{1,0:T(8,128)(2,1)S(1)} %get-tuple-element.8.att_ref, ...), custom_call_target="tpu_custom_call" | custom-call | flops 1073741824 | bytes 4194304 | tf_op jit(solution)/shard_map/key_grads/pallas_call | solution.py:248
  69.5 1.9 %collective-permute-start.6 = (bf16[1024,128]{1,0:T(8,128)(2,1)S(1)}, bf16[1024,128]{1,0:T(8,128)(2,1)S(1)}, u32[]{:S(2)}, u32[]{:S(2)}) collective-permute-start(bf16[1024,128]{1,0:T(8,128)(2,1)S(1)} %slice.107), channel_id=1, source_target_pairs={{0,8},{4,12},{8,0},{12,4},{16,24},{20,28},{24,16},{28,20},{1,9},{5... | collective-permute-start | bytes 786440 | tf_op jit(solution)/shard_map/ppermute | solution.py:275
  71.4 4.8 %key_grads.2 = bf16[2048,128]{1,0:T(8,128)(2,1)S(1)} custom-call(s32[1]{0:T(128)} %bitcast.me_ref, bf16[2,4,2048,256]{3,2,1,0:T(8,128)(2,1)S(1)} %get-tuple-element.7.p_ref, bf16[2048,256]{1,0:T(8,128)(2,1)S(1)} %copy-done.2, bf16[1024,256]{1,0:T(8,128)(2,1)S(1)} %project.7.da_ref, bf16[1024,256]{1,0:T(8,128)(2,1)S(1)} %get-tuple-element.8.att_ref, ...), custom_call_target="tpu_custom_call" | custom-call | flops 1073741824 | bytes 4194304 | tf_op jit(solution)/shard_map/key_grads/pallas_call | solution.py:248
  76.2 1.6 %collective-permute-start.3 = (bf16[1024,128]{1,0:T(8,128)(2,1)S(1)}, bf16[1024,128]{1,0:T(8,128)(2,1)S(1)}, u32[]{:S(2)}, u32[]{:S(2)}) collective-permute-start(bf16[1024,128]{1,0:T(8,128)(2,1)S(1)} %slice.101), channel_id=1, source_target_pairs={{0,4},{4,0},{8,12},{12,8},{16,20},{20,16},{24,28},{28,24},{1,5},{5... | collective-permute-start | bytes 786440 | tf_op jit(solution)/shard_map/ppermute | solution.py:275
  77.8 2.1 %value_grads.3 = bf16[2048,128]{1,0:T(8,128)(2,1)S(1)} custom-call(bf16[2,4,2048,256]{3,2,1,0:T(8,128)(2,1)S(1)} %get-tuple-element.7.p_ref, bf16[1024,256]{1,0:T(8,128)(2,1)S(1)} %project.7.da_ref), custom_call_target="tpu_custom_call" | custom-call | flops 536870912 | bytes 4194304 | tf_op jit(solution)/shard_map/value_grads/pallas_call | solution.py:196
  79.9 2.1 %value_grads.2 = bf16[2048,128]{1,0:T(8,128)(2,1)S(1)} custom-call(bf16[2,4,2048,256]{3,2,1,0:T(8,128)(2,1)S(1)} %get-tuple-element.7.p_ref, bf16[1024,256]{1,0:T(8,128)(2,1)S(1)} %project.7.da_ref), custom_call_target="tpu_custom_call" | custom-call | flops 536870912 | bytes 4194304 | tf_op jit(solution)/shard_map/value_grads/pallas_call | solution.py:196
  82.0 0.5 collective-permute-start.12
  82.5 0.3 collective-permute-start.9
  82.8 0.1 add_convert_fusion.2
  82.9 1.8 %collective-permute-start.7 = (bf16[512,128]{1,0:T(8,128)(2,1)S(1)}, bf16[512,128]{1,0:T(8,128)(2,1)S(1)}, u32[]{:S(2)}, u32[]{:S(2)}) collective-permute-start(bf16[512,128]{1,0:T(8,128)(2,1)S(1)} %slice.109), channel_id=1, source_target_pairs={{0,4},{4,0},{8,12},{12,8},{16,20},{20,16},{24,28},{28,24},{1,5},{5... | collective-permute-start | bytes 393224 | tf_op jit(solution)/shard_map/ppermute | solution.py:275
  84.7 0.0 collective-permute-done.3
  84.7 0.1 add_convert_fusion.3
  84.8 1.6 %collective-permute-start.4 = (bf16[512,128]{1,0:T(8,128)(2,1)S(1)}, bf16[512,128]{1,0:T(8,128)(2,1)S(1)}, u32[]{:S(2)}, u32[]{:S(2)}) collective-permute-start(bf16[512,128]{1,0:T(8,128)(2,1)S(1)} %slice.103), channel_id=1, source_target_pairs={{0,8},{4,12},{8,0},{12,4},{16,24},{20,28},{24,16},{28,20},{1,9},{5... | collective-permute-start | bytes 393224 | tf_op jit(solution)/shard_map/ppermute | solution.py:275
  86.5 4.8 %collective-permute-done.12 = bf16[1024,128]{1,0:T(8,128)(2,1)S(1)} collective-permute-done((bf16[1024,128]{1,0:T(8,128)(2,1)S(1)}, bf16[1024,128]{1,0:T(8,128)(2,1)S(1)}, u32[]{:S(2)}, u32[]{:S(2)}) %collective-permute-start.12) | collective-permute-done | bytes 262176 | tf_op jit(solution)/shard_map/ppermute | solution.py:275
  91.3 0.1 add_convert_fusion
  91.4 0.6 collective-permute-start.13
  92.0 0.1 add_convert_fusion.1
  92.1 1.4 %collective-permute-start.10 = (bf16[512,128]{1,0:T(8,128)(2,1)S(1)}, bf16[512,128]{1,0:T(8,128)(2,1)S(1)}, u32[]{:S(2)}, u32[]{:S(2)}) collective-permute-start(bf16[512,128]{1,0:T(8,128)(2,1)S(1)} %slice.115), channel_id=1, source_target_pairs={{0,8},{4,12},{8,0},{12,4},{16,24},{20,28},{24,16},{28,20},{1,9},{5... | collective-permute-start | bytes 393224 | tf_op jit(solution)/shard_map/ppermute | solution.py:275
  93.5 0.8 collective-permute-done.7
  94.3 2.7 %collective-permute-start.8 = (bf16[256,128]{1,0:T(8,128)(2,1)S(1)}, bf16[256,128]{1,0:T(8,128)(2,1)S(1)}, u32[]{:S(2)}, u32[]{:S(2)}) collective-permute-start(bf16[256,128]{1,0:T(8,128)(2,1)S(1)} %slice.111), channel_id=1, source_target_pairs={{0,16},{4,20},{8,24},{12,28},{16,0},{20,4},{24,8},{28,12},{1,17},{... | collective-permute-start | bytes 196616 | tf_op jit(solution)/shard_map/ppermute | solution.py:275
  97.1 0.4 collective-permute-start.5
  97.5 2.7 %collective-permute-start.14 = (bf16[256,128]{1,0:T(8,128)(2,1)S(1)}, bf16[256,128]{1,0:T(8,128)(2,1)S(1)}, u32[]{:S(2)}, u32[]{:S(2)}) collective-permute-start(bf16[256,128]{1,0:T(8,128)(2,1)S(1)} %slice.123), channel_id=1, source_target_pairs={{0,16},{4,20},{8,24},{12,28},{16,0},{20,4},{24,8},{28,12},{1,17},{... | collective-permute-start | bytes 196616 | tf_op jit(solution)/shard_map/ppermute | solution.py:275
  100.2 0.4 collective-permute-start.11
  100.6 3.8 %collective-permute-done.8 = bf16[256,128]{1,0:T(8,128)(2,1)S(1)} collective-permute-done((bf16[256,128]{1,0:T(8,128)(2,1)S(1)}, bf16[256,128]{1,0:T(8,128)(2,1)S(1)}, u32[]{:S(2)}, u32[]{:S(2)}) %collective-permute-start.8) | collective-permute-done | bytes 65568 | tf_op jit(solution)/shard_map/ppermute | solution.py:275
  104.5 1.3 %collective-permute-done.5 = bf16[256,128]{1,0:T(8,128)(2,1)S(1)} collective-permute-done((bf16[256,128]{1,0:T(8,128)(2,1)S(1)}, bf16[256,128]{1,0:T(8,128)(2,1)S(1)}, u32[]{:S(2)}, u32[]{:S(2)}) %collective-permute-start.5) | collective-permute-done | bytes 65568 | tf_op jit(solution)/shard_map/ppermute | solution.py:275
  105.8 1.4 %collective-permute-done.14 = bf16[256,128]{1,0:T(8,128)(2,1)S(1)} collective-permute-done((bf16[256,128]{1,0:T(8,128)(2,1)S(1)}, bf16[256,128]{1,0:T(8,128)(2,1)S(1)}, u32[]{:S(2)}, u32[]{:S(2)}) %collective-permute-start.14) | collective-permute-done | bytes 65568 | tf_op jit(solution)/shard_map/ppermute | solution.py:275
  107.2 0.7 multiply_reduce_fusion.1
  107.9 0.0 collective-permute-done.11
  107.9 0.7 multiply_reduce_fusion
  110.0 0.7 broadcast_in_dim.15
  110.6 3.9 %all-to-all-start = ((f32[32,8,128]{2,1,0:T(8,128)}), f32[32,8,128]{2,1,0:T(8,128)S(1)}, u32[]{:S(2)}, u32[]{:S(2)}) async-start(f32[32,8,128]{2,1,0:T(8,128)} %broadcast_in_dim.15), calls=%async_computation | async-start | bytes 262144 | tf_op jit(solution)/shard_map/all_to_all | solution.py:330
  114.5 8.2 %all-to-all-done = f32[32,8,128]{2,1,0:T(8,128)S(1)} async-done(((f32[32,8,128]{2,1,0:T(8,128)}), f32[32,8,128]{2,1,0:T(8,128)S(1)}, u32[]{:S(2)}, u32[]{:S(2)}) %all-to-all-start) | async-done | bytes 131104 | tf_op jit(solution)/shard_map/all_to_all | solution.py:330
  122.8 0.6 slice_reduce_fusion
  124.1 1.8 %divide_subtract_fusion = (f32[256,256]{1,0:T(8,128)}, f32[256,256]{1,0:T(8,128)}) fusion(f32[256,128]{1,0:T(8,128)S(1)} %convert_add_fusion, f32[256,128]{1,0:T(8,128)S(1)} %convert_add_fusion.1, bf16[2048,256]{1,0:T(8,128)(2,1)S(1)} %copy-done.2, s32[]{:T(128)S(6)} %select_n.9, f32[]{:T(128)S(6)} %sqrt.3, f32[256,128]{1,0:T(8,128)S(1)} %convert_add_fusion.2, ...), kind=kLoop, calls=%fused_computation.6 | loop fusion | flops 655360 | bytes 1310728 | tf_op jit(solution)/shard_map/sub | solution.py:338
  (41 shorter events, 0.4 us)
Async XLA Ops:
  0.6 35.7 %copy-start.8 = (s32[1,256]{1,0:T(1,128)S(1)}, s32[1,256]{1,0:T(1,128)}, u32[]{:S(2)}) copy-start(s32[1,256]{1,0:T(1,128)} %param.15) | copy-start | bytes 3076
  0.6 26.4 %collective-permute-start = (bf16[256,2048]{1,0:T(8,128)(2,1)}, bf16[256,2048]{1,0:T(8,128)(2,1)S(1)}, u32[]{:S(2)}, u32[]{:S(2)}) collective-permute-start(bf16[256,2048]{1,0:T(8,128)(2,1)} %g_ref.1), channel_id=1, source_target_pairs={{0,2},{1,3},{2,0},{3,1},{4,6},{5,7},{6,4},{7,5},{8,10},{9,11},{10,... | collective-permute-start | bytes 3145736 | tf_op jit(solution)/shard_map/ppermute | solution.py:275
  3.7 47.3 %collective-permute-start.2 = (bf16[256,2048]{1,0:T(8,128)(2,1)}, bf16[256,2048]{1,0:T(8,128)(2,1)}, u32[]{:S(2)}, u32[]{:S(2)}) collective-permute-start(bf16[256,2048]{1,0:T(8,128)(2,1)} %g_ref.1), channel_id=1, source_target_pairs={{0,1},{1,0},{2,3},{3,2},{4,5},{5,4},{6,7},{7,6},{8,9},{9,8},{10,11... | collective-permute-start | bytes 3145736 | tf_op jit(solution)/shard_map/ppermute | solution.py:275
  27.0 35.3 %collective-permute-start.1 = (bf16[256,2048]{1,0:T(8,128)(2,1)S(1)}, bf16[256,2048]{1,0:T(8,128)(2,1)S(1)}, u32[]{:S(2)}, u32[]{:S(2)}) collective-permute-start(bf16[256,2048]{1,0:T(8,128)(2,1)S(1)} %collective-permute-done.g_ref), channel_id=1, source_target_pairs={{0,1},{1,0},{2,3},{3,2},{4,5},{5,4},{6,7},{7,6},{8,9},{9,8},{10,11... | collective-permute-start | bytes 3145736 | tf_op jit(solution)/shard_map/ppermute | solution.py:275
  27.0 5.8 %copy-start = (bf16[1024,8192]{1,0:T(8,128)(2,1)S(1)}, bf16[1024,8192]{1,0:T(8,128)(2,1)}, u32[]{:S(2)}) copy-start(bf16[1024,8192]{1,0:T(8,128)(2,1)} %w_ref.7) | copy-start | bytes 50331652
  32.8 1.2 copy-start.4
  34.0 2.4 %copy-start.2 = (bf16[2048,256]{1,0:T(8,128)(2,1)S(1)}, bf16[2048,256]{1,0:T(8,128)(2,1)}, u32[]{:S(2)}) copy-start(bf16[2048,256]{1,0:T(8,128)(2,1)} %v_ref.5) | copy-start | bytes 3145732
  34.0 2.4 %copy-start.3 = (bf16[256,1024]{1,0:T(8,128)(2,1)S(1)}, bf16[256,1024]{1,0:T(8,128)(2,1)}, u32[]{:S(2)}) copy-start(bf16[256,1024]{1,0:T(8,128)(2,1)} %q_ref.5) | copy-start | bytes 1572868
  34.0 2.4 %copy-start.5 = (bf16[2048,256]{1,0:T(8,128)(2,1)S(1)}, bf16[2048,256]{1,0:T(8,128)(2,1)}, u32[]{:S(2)}) copy-start(bf16[2048,256]{1,0:T(8,128)(2,1)} %k_ref.1) | copy-start | bytes 3145732
  34.0 2.4 %copy-start.6 = (bf16[256,256]{1,0:T(8,128)(2,1)S(1)}, bf16[256,256]{1,0:T(8,128)(2,1)}, u32[]{:S(2)}) copy-start(bf16[256,256]{1,0:T(8,128)(2,1)} %ks_ref.1) | copy-start | bytes 393220
  34.1 2.4 %copy-start.7 = (bf16[256,256]{1,0:T(8,128)(2,1)S(1)}, bf16[256,256]{1,0:T(8,128)(2,1)}, u32[]{:S(2)}) copy-start(bf16[256,256]{1,0:T(8,128)(2,1)} %vs_ref.1) | copy-start | bytes 393220
  51.0 5.8 %copy-start.1 = (bf16[1024,8192]{1,0:T(8,128)(2,1)S(1)}, bf16[1024,8192]{1,0:T(8,128)(2,1)}, u32[]{:S(2)}) copy-start(bf16[1024,8192]{1,0:T(8,128)(2,1)} %w_ref.7) | copy-start | bytes 50331652
  69.5 13.3 %collective-permute-start.6 = (bf16[1024,128]{1,0:T(8,128)(2,1)S(1)}, bf16[1024,128]{1,0:T(8,128)(2,1)S(1)}, u32[]{:S(2)}, u32[]{:S(2)}) collective-permute-start(bf16[1024,128]{1,0:T(8,128)(2,1)S(1)} %slice.107), channel_id=1, source_target_pairs={{0,8},{4,12},{8,0},{12,4},{16,24},{20,28},{24,16},{28,20},{1,9},{5... | collective-permute-start | bytes 786440 | tf_op jit(solution)/shard_map/ppermute | solution.py:275
  76.2 8.5 %collective-permute-start.3 = (bf16[1024,128]{1,0:T(8,128)(2,1)S(1)}, bf16[1024,128]{1,0:T(8,128)(2,1)S(1)}, u32[]{:S(2)}, u32[]{:S(2)}) collective-permute-start(bf16[1024,128]{1,0:T(8,128)(2,1)S(1)} %slice.101), channel_id=1, source_target_pairs={{0,4},{4,0},{8,12},{12,8},{16,20},{20,16},{24,28},{28,24},{1,5},{5... | collective-permute-start | bytes 786440 | tf_op jit(solution)/shard_map/ppermute | solution.py:275
  82.0 9.2 %collective-permute-start.12 = (bf16[1024,128]{1,0:T(8,128)(2,1)S(1)}, bf16[1024,128]{1,0:T(8,128)(2,1)S(1)}, u32[]{:S(2)}, u32[]{:S(2)}) collective-permute-start(bf16[1024,128]{1,0:T(8,128)(2,1)S(1)} %slice.119), channel_id=1, source_target_pairs={{0,8},{4,12},{8,0},{12,4},{16,24},{20,28},{24,16},{28,20},{1,9},{5... | collective-permute-start | bytes 786440 | tf_op jit(solution)/shard_map/ppermute | solution.py:275
  82.5 9.4 %collective-permute-start.9 = (bf16[1024,128]{1,0:T(8,128)(2,1)S(1)}, bf16[1024,128]{1,0:T(8,128)(2,1)S(1)}, u32[]{:S(2)}, u32[]{:S(2)}) collective-permute-start(bf16[1024,128]{1,0:T(8,128)(2,1)S(1)} %slice.113), channel_id=1, source_target_pairs={{0,4},{4,0},{8,12},{12,8},{16,20},{20,16},{24,28},{28,24},{1,5},{5... | collective-permute-start | bytes 786440 | tf_op jit(solution)/shard_map/ppermute | solution.py:275
  82.9 11.3 %collective-permute-start.7 = (bf16[512,128]{1,0:T(8,128)(2,1)S(1)}, bf16[512,128]{1,0:T(8,128)(2,1)S(1)}, u32[]{:S(2)}, u32[]{:S(2)}) collective-permute-start(bf16[512,128]{1,0:T(8,128)(2,1)S(1)} %slice.109), channel_id=1, source_target_pairs={{0,4},{4,0},{8,12},{12,8},{16,20},{20,16},{24,28},{28,24},{1,5},{5... | collective-permute-start | bytes 393224 | tf_op jit(solution)/shard_map/ppermute | solution.py:275
  84.8 12.2 %collective-permute-start.4 = (bf16[512,128]{1,0:T(8,128)(2,1)S(1)}, bf16[512,128]{1,0:T(8,128)(2,1)S(1)}, u32[]{:S(2)}, u32[]{:S(2)}) collective-permute-start(bf16[512,128]{1,0:T(8,128)(2,1)S(1)} %slice.103), channel_id=1, source_target_pairs={{0,8},{4,12},{8,0},{12,4},{16,24},{20,28},{24,16},{28,20},{1,9},{5... | collective-permute-start | bytes 393224 | tf_op jit(solution)/shard_map/ppermute | solution.py:275
  91.4 6.1 %collective-permute-start.13 = (bf16[512,128]{1,0:T(8,128)(2,1)S(1)}, bf16[512,128]{1,0:T(8,128)(2,1)S(1)}, u32[]{:S(2)}, u32[]{:S(2)}) collective-permute-start(bf16[512,128]{1,0:T(8,128)(2,1)S(1)} %slice.121), channel_id=1, source_target_pairs={{0,4},{4,0},{8,12},{12,8},{16,20},{20,16},{24,28},{28,24},{1,5},{5... | collective-permute-start | bytes 393224 | tf_op jit(solution)/shard_map/ppermute | solution.py:275
  92.1 8.1 %collective-permute-start.10 = (bf16[512,128]{1,0:T(8,128)(2,1)S(1)}, bf16[512,128]{1,0:T(8,128)(2,1)S(1)}, u32[]{:S(2)}, u32[]{:S(2)}) collective-permute-start(bf16[512,128]{1,0:T(8,128)(2,1)S(1)} %slice.115), channel_id=1, source_target_pairs={{0,8},{4,12},{8,0},{12,4},{16,24},{20,28},{24,16},{28,20},{1,9},{5... | collective-permute-start | bytes 393224 | tf_op jit(solution)/shard_map/ppermute | solution.py:275
  94.3 10.1 %collective-permute-start.8 = (bf16[256,128]{1,0:T(8,128)(2,1)S(1)}, bf16[256,128]{1,0:T(8,128)(2,1)S(1)}, u32[]{:S(2)}, u32[]{:S(2)}) collective-permute-start(bf16[256,128]{1,0:T(8,128)(2,1)S(1)} %slice.111), channel_id=1, source_target_pairs={{0,16},{4,20},{8,24},{12,28},{16,0},{20,4},{24,8},{28,12},{1,17},{... | collective-permute-start | bytes 196616 | tf_op jit(solution)/shard_map/ppermute | solution.py:275
  97.1 8.7 %collective-permute-start.5 = (bf16[256,128]{1,0:T(8,128)(2,1)S(1)}, bf16[256,128]{1,0:T(8,128)(2,1)S(1)}, u32[]{:S(2)}, u32[]{:S(2)}) collective-permute-start(bf16[256,128]{1,0:T(8,128)(2,1)S(1)} %slice.105), channel_id=1, source_target_pairs={{0,16},{4,20},{8,24},{12,28},{16,0},{20,4},{24,8},{28,12},{1,17},{... | collective-permute-start | bytes 196616 | tf_op jit(solution)/shard_map/ppermute | solution.py:275
  97.5 9.7 %collective-permute-start.14 = (bf16[256,128]{1,0:T(8,128)(2,1)S(1)}, bf16[256,128]{1,0:T(8,128)(2,1)S(1)}, u32[]{:S(2)}, u32[]{:S(2)}) collective-permute-start(bf16[256,128]{1,0:T(8,128)(2,1)S(1)} %slice.123), channel_id=1, source_target_pairs={{0,16},{4,20},{8,24},{12,28},{16,0},{20,4},{24,8},{28,12},{1,17},{... | collective-permute-start | bytes 196616 | tf_op jit(solution)/shard_map/ppermute | solution.py:275
  100.2 7.6 %collective-permute-start.11 = (bf16[256,128]{1,0:T(8,128)(2,1)S(1)}, bf16[256,128]{1,0:T(8,128)(2,1)S(1)}, u32[]{:S(2)}, u32[]{:S(2)}) collective-permute-start(bf16[256,128]{1,0:T(8,128)(2,1)S(1)} %slice.117), channel_id=1, source_target_pairs={{0,16},{4,20},{8,24},{12,28},{16,0},{20,4},{24,8},{28,12},{1,17},{... | collective-permute-start | bytes 196616 | tf_op jit(solution)/shard_map/ppermute | solution.py:275
  110.6 12.1 %all-to-all-start = ((f32[32,8,128]{2,1,0:T(8,128)}), f32[32,8,128]{2,1,0:T(8,128)S(1)}, u32[]{:S(2)}, u32[]{:S(2)}) async-start(f32[32,8,128]{2,1,0:T(8,128)} %broadcast_in_dim.15), calls=%async_computation | async-start | bytes 262144 | tf_op jit(solution)/shard_map/all_to_all | solution.py:330

commit v2 on v1

v2 whole, which is shorter than its diff:
```python
import functools
import math

import jax
import jax.numpy as jnp
from jax import lax
from jax.experimental import pallas as pl
from jax.experimental.pallas import tpu as pltpu
from jax.sharding import PartitionSpec as P

HD = 128
KVH = 8
SLOTS = 2048

step_rate = 0.25
epsilon = 1e-06

F32 = jnp.float32
BF16 = jnp.bfloat16
NT = (((1,), (1,)), ((), ()))
NN = (((1,), (0,)), ((), ()))
TN = (((0,), (0,)), ((), ()))
MIB = 1 << 20


def mm(a, b, dims):
    return lax.dot_general(a, b, dims, preferred_element_type=F32)


def bit_orders(n, heads):
    bits = max(1, n.bit_length() - 1)
    first = list(range(bits))
    if n == 1:
        return [[] for _ in range(heads)]
    second = first[:]
    if bits > 1:
        second[0], second[1] = second[1], second[0]
    return [first if head % 2 == 0 else second for head in range(heads)]


def place_of(rel, order):
    place = 0
    for step, bit in enumerate(order):
        place = place + (((rel >> bit) & 1) << (len(order) - 1 - step))
    return place


def block_at(place, order):
    rel = 0
    for step, bit in enumerate(order):
        rel = rel + (((place >> (len(order) - 1 - step)) & 1) << bit)
    return rel


def per_head(g, orders, fn):
    even = fn(orders[0])
    if len(orders) == 1:
        return even
    return jnp.where(g % 2 == 0, even, fn(orders[1]))


def forward_kernel(
    orders, n, me_ref, q_ref, k_ref, ks_ref, v_ref, vs_ref, bias_ref, w_ref,
    p_ref, att_ref, att_t_ref, held_ref, s_ref, sems,
):
    g, j = pl.program_id(0), pl.program_id(1)
    cut = w_ref.shape[0] // 4
    copies = [
        pltpu.make_async_copy(
            w_ref.at[c * cut : (c + 1) * cut], held_ref.at[c * cut : (c + 1) * cut], sems.at[c]
        )
        for c in range(4)
    ]

    @pl.when((g == 0) & (j == 0))
    def _():
        for copy in copies:
            copy.start()

    me = me_ref[0]
    slots = k_ref.shape[0]
    length = q_ref.shape[0]
    share = slots // n
    chunk = 256
    scale = math.log2(math.e) / math.sqrt(HD)
    q = q_ref[...]
    steps = [(k_ref, v_ref, c, c, chunk) for c in range(0, slots, chunk)]
    steps.append((ks_ref, vs_ref, 0, slots, length))
    high = None
    for keys, _, at, row, size in steps:
        s = mm(keys[at : at + size, :], q, NT) * scale
        if keys is ks_ref:
            s = s + bias_ref[...]
        s_ref[row : row + size, :] = s
        top = jnp.max(s.reshape(size // 8, 8, length), axis=0)
        high = top if high is None else jnp.maximum(high, top)
    high = jnp.max(high, axis=0, keepdims=True)
    total = None
    for _, _, _, row, size in steps:
        e = jnp.exp2(s_ref[row : row + size, :] - high)
        s_ref[row : row + size, :] = e
        part = jnp.sum(e.reshape(size // 8, 8, length), axis=0)
        total = part if total is None else total + part
    inverse = 1.0 / jnp.sum(total, axis=0, keepdims=True)
    att = None
    for keys, values, at, row, size in steps:
        p = (s_ref[row : row + size, :] * inverse).astype(BF16)
        if keys is k_ref:
            piece = min(share, size)
            for b in range(0, size, piece):
                block, inside = (at + b) // share, (at + b) % share
                place = per_head(g, orders, functools.partial(place_of, block ^ me))
                start = pl.multiple_of(place * share + inside, piece)
                p_ref[0, pl.ds(start, piece), :] = p[b : b + piece, :]
        part = mm(values[at : at + size, :], p, TN)
        att = part if att is None else att + part
    att_t_ref[0] = att.astype(BF16)
    att_ref[...] = att.T.astype(BF16)

    @pl.when((g == pl.num_programs(0) - 1) & (j == pl.num_programs(1) - 1))
    def _():
        for copy in copies:
            copy.wait()


def forward(me, queries, cache_k, span_k, cache_v, span_v, bias, weights, orders, n):
    length, width = queries.shape
    slots, kv_width = cache_k.shape
    kv = kv_width // HD
    group = width // kv_width
    spec = pltpu.PrefetchScalarGridSpec(
        num_scalar_prefetch=1,
        grid=(kv, group),
        in_specs=[
            pl.BlockSpec((length, HD), lambda g, j, me: (0, g * group + j)),
            pl.BlockSpec((slots, HD), lambda g, j, me: (0, g)),
            pl.BlockSpec((length, HD), lambda g, j, me: (0, g)),
            pl.BlockSpec((slots, HD), lambda g, j, me: (0, g)),
            pl.BlockSpec((length, HD), lambda g, j, me: (0, g)),
            pl.BlockSpec((length, length), lambda g, j, me: (0, 0)),
            pl.BlockSpec(memory_space=pl.ANY),
        ],
        out_specs=[
            pl.BlockSpec((1, slots, length), lambda g, j, me: (g, 0, j)),
            pl.BlockSpec((length, HD), lambda g, j, me: (0, g * group + j)),
            pl.BlockSpec((1, HD, length), lambda g, j, me: (g, 0, j)),
            pl.BlockSpec(memory_space=pltpu.VMEM),
        ],
        scratch_shapes=[pltpu.VMEM((slots + length, length), F32), pltpu.SemaphoreType.DMA((4,))],
    )
    return pl.pallas_call(
        functools.partial(forward_kernel, orders, n),
        grid_spec=spec,
        out_shape=[
            jax.ShapeDtypeStruct((kv, slots, group * length), BF16),
            jax.ShapeDtypeStruct((length, width), BF16),
            jax.ShapeDtypeStruct((kv, HD, group * length), BF16),
            jax.ShapeDtypeStruct(weights.shape, BF16),
        ],
        compiler_params=pltpu.CompilerParams(vmem_limit_bytes=16 * MIB),
        cost_estimate=pl.CostEstimate(
            flops=4 * width * length * (slots + length),
            bytes_accessed=2 * width // HD * length * slots,
            transcendentals=width // HD * length * (slots + length),
        ),
        name="forward",
    )(me, queries, cache_k, span_k, cache_v, span_v, bias, weights)


def project_kernel(adds, heads, shard_ref, w_ref, g_ref, *refs):
    acc_ref, out_ref = refs if adds else (None, refs[0])
    rows, features = w_ref.shape[0], g_ref.shape[1]
    block = min(256, rows)
    columns = pl.ds(pl.multiple_of(shard_ref[0] * features, features), features)
    for m in range(0, rows, block):
        total = mm(w_ref[m : m + block, columns], g_ref[...], NT)
        if adds:
            total = total + acc_ref[m : m + block, :]
        if not heads:
            out_ref[m : m + block, :] = total
            continue
        length = total.shape[1]
        for b in range(0, block, HD):
            head = (m + b) // HD
            at = head % heads * length
            out_ref[head // heads, :, at : at + length] = total[b : b + HD, :].astype(BF16)


def project(shard, out_proj, grad, acc=None, heads=0):
    rows = out_proj.shape[0]
    length, features = grad.shape
    vmem = pl.BlockSpec(memory_space=pltpu.VMEM)
    args = [shard, out_proj, grad] + ([] if acc is None else [acc])
    if heads:
        out = jax.ShapeDtypeStruct((rows // HD // heads, HD, heads * length), BF16)
    else:
        out = jax.ShapeDtypeStruct((rows, length), F32)
    return pl.pallas_call(
        functools.partial(project_kernel, acc is not None, heads),
        in_specs=[pl.BlockSpec(memory_space=pltpu.SMEM)] + [vmem] * (len(args) - 1),
        out_specs=vmem,
        out_shape=out,
        compiler_params=pltpu.CompilerParams(vmem_limit_bytes=8 * MIB),
        cost_estimate=pl.CostEstimate(
            flops=2 * rows * length * features,
            bytes_accessed=2 * rows * features,
            transcendentals=0,
        ),
        name="project",
    )(*args)


def values_kernel(head, p_ref, da_ref, out_ref):
    rows = 256
    da = da_ref[head]
    for at in range(0, p_ref.shape[1], rows):
        out_ref[at : at + rows, :] = mm(p_ref[head, at : at + rows, :], da, NT).astype(BF16)


def value_grads(head, probs, grad_att_t):
    _, slots, wide = probs.shape
    vmem = pl.BlockSpec(memory_space=pltpu.VMEM)
    return pl.pallas_call(
        functools.partial(values_kernel, head),
        in_specs=[vmem, vmem],
        out_specs=vmem,
        out_shape=jax.ShapeDtypeStruct((slots, HD), BF16),
        compiler_params=pltpu.CompilerParams(vmem_limit_bytes=14 * MIB),
        cost_estimate=pl.CostEstimate(
            flops=2 * slots * wide, bytes_accessed=2 * slots * HD, transcendentals=0
        ),
        name="value_grads",
    )(probs, grad_att_t)


def keys_kernel(head, order, n, me_ref, p_ref, v_ref, da_ref, att_ref, q_ref, out_ref):
    me = me_ref[0]
    slots = p_ref.shape[1]
    share = slots // n
    length = q_ref.shape[0]
    group = p_ref.shape[2] // length
    piece = min(share, 256)
    da = da_ref[head]
    dot = jnp.sum(da.astype(F32) * att_ref[head].astype(F32), axis=0, keepdims=True)
    first = head * group * HD
    q = jnp.concatenate(
        [q_ref[:, first + j * HD : first + (j + 1) * HD] for j in range(group)], axis=0
    )
    for row in range(0, slots, piece):
        block = block_at(row // share, order) ^ me
        start = pl.multiple_of(block * share + row % share, piece)
        values = v_ref[pl.ds(start, piece), head * HD : (head + 1) * HD]
        grad_p = mm(values, da, NN)
        p = p_ref[head, row : row + piece, :].astype(F32)
        grad_s = (p * (grad_p - dot)).astype(BF16)
        total = mm(grad_s, q, NN) * (1.0 / math.sqrt(HD))
        out_ref[row : row + piece, :] = total.astype(BF16)


def key_grads(head, me, probs, cache_v, grad_att_t, att_t, queries, order, n):
    _, slots, wide = probs.shape
    vmem = pl.BlockSpec(memory_space=pltpu.VMEM)
    return pl.pallas_call(
        functools.partial(keys_kernel, head, order, n),
        in_specs=[pl.BlockSpec(memory_space=pltpu.SMEM)] + [vmem] * 5,
        out_specs=vmem,
        out_shape=jax.ShapeDtypeStruct((slots, HD), BF16),
        compiler_params=pltpu.CompilerParams(vmem_limit_bytes=14 * MIB),
        cost_estimate=pl.CostEstimate(
            flops=4 * slots * wide, bytes_accessed=2 * slots * HD, transcendentals=0
        ),
        name="key_grads",
    )(me, probs, cache_v, grad_att_t, att_t, queries)


def squares_kernel(count, *refs):
    parts, (keys_ref, vals_ref, sum_ref) = refs[: 2 * count], refs[2 * count :]
    half = count // 2
    square = None
    for at in range(count):
        own_ref, got_ref = parts[2 * at], parts[2 * at + 1]
        total = own_ref[: got_ref.shape[0], :].astype(F32) + got_ref[...].astype(F32)
        out_ref, head = (vals_ref, at) if at < half else (keys_ref, at - half)
        out_ref[:, head * HD : (head + 1) * HD] = total
        here = jnp.sum((total * total).reshape(-1, 8, HD), axis=0)
        square = here if square is None else square + here
    sum_ref[...] = jnp.broadcast_to(jnp.sum(square, keepdims=True), sum_ref.shape)


def squares(parts, devices):
    flat = [term for pair in parts for term in pair]
    share = flat[1].shape[0]
    count = len(parts)
    vmem = pl.BlockSpec(memory_space=pltpu.VMEM)
    grads = jax.ShapeDtypeStruct((share, count // 2 * HD), F32)
    return pl.pallas_call(
        functools.partial(squares_kernel, count),
        in_specs=[vmem] * len(flat),
        out_specs=[vmem] * 3,
        out_shape=[grads, grads, jax.ShapeDtypeStruct((devices, 128), F32)],
        compiler_params=pltpu.CompilerParams(vmem_limit_bytes=8 * MIB),
        cost_estimate=pl.CostEstimate(
            flops=6 * count * share * HD, bytes_accessed=8 * count * share * HD, transcendentals=0
        ),
        name="squares",
    )(*flat)


def update_kernel(sums_ref, keys_ref, vals_ref, grad_k_ref, grad_v_ref, new_k_ref, new_v_ref):
    total = jnp.sum(sums_ref[...], axis=0, keepdims=True)[:, :1]
    rms = jnp.sqrt(total / (2 * SLOTS * KVH * HD) + epsilon)
    factor = step_rate / rms
    new_k_ref[...] = keys_ref[...].astype(F32) - factor * grad_k_ref[...]
    new_v_ref[...] = vals_ref[...].astype(F32) - factor * grad_v_ref[...]


def update(sums, own_keys, own_vals, grad_k, grad_v):
    vmem = pl.BlockSpec(memory_space=pltpu.VMEM)
    return pl.pallas_call(
        update_kernel,
        in_specs=[vmem] * 5,
        out_specs=[vmem] * 2,
        out_shape=[jax.ShapeDtypeStruct(grad_k.shape, F32)] * 2,
        compiler_params=pltpu.CompilerParams(vmem_limit_bytes=8 * MIB),
        cost_estimate=pl.CostEstimate(
            flops=4 * grad_k.size, bytes_accessed=20 * grad_k.size, transcendentals=0
        ),
        name="update",
    )(sums, own_keys, own_vals, grad_k, grad_v)


def exchange(value, axis, size, flip):
    return lax.ppermute(value, axis, [(i, i ^ flip) for i in range(size)])


def first_halving(part, order, n):
    if not order:
        return part, jnp.zeros_like(part)
    return part, exchange(part[part.shape[0] // 2 :], "dp", n, 1 << order[0])


def rest_halving(part, got, order, n):
    for bit in order[1:]:
        half = got.shape[0]
        part = (part[:half].astype(F32) + got.astype(F32)).astype(BF16)
        got = exchange(part[half // 2 :], "dp", n, 1 << bit)
    return part, got


def body(queries, span_keys, span_values, cache_keys, cache_values, out_proj, out_grad, doc_ids):
    n = lax.axis_size("dp")
    t = lax.axis_size("tensor")
    mine = lax.axis_index("dp")
    shard = lax.axis_index("tensor")
    me = mine.astype(jnp.int32).reshape(1)
    length = queries.shape[0]
    kv = cache_keys.shape[1] // HD
    group = queries.shape[1] // HD // kv
    share = cache_keys.shape[0] // n
    orders = bit_orders(n, kv)

    flips = [2 * s for s in range(1, t // 2)]
    far = [exchange(out_grad, "tensor", t, flip) for flip in flips]
    near = exchange(out_grad, "tensor", t, 1)

    docs = doc_ids[0]
    places = jnp.arange(length)
    span_ok = (docs[None, :] == docs[:, None]) & (places[:, None] <= places[None, :])
    bias = jnp.where(span_ok, 0.0, -1e30).astype(F32)
    probs, attended, att_t, held = forward(
        me, queries, cache_keys, span_keys, cache_values, span_values, bias, out_proj, orders, n
    )
    shard = shard.astype(jnp.int32).reshape(1)
    acc = project(shard, held, out_grad)
    acc = project(shard ^ 1, held, near, acc)
    far, acc = lax.optimization_barrier((far, acc))
    later = [exchange(got, "tensor", t, 1) for got in far]
    for flip, got in zip(flips, far):
        acc = project(shard ^ flip, held, got, acc)
    for flip, got in zip(flips, later):
        acc = project(shard ^ (flip + 1), held, got, acc, group if flip == flips[-1] else 0)

    kernels = [functools.partial(value_grads, h, probs) for h in range(kv)]
    kernels += [
        lambda acc, h=h: key_grads(
            h, me, probs, cache_values, acc, att_t, queries, orders[h], n
        )
        for h in range(kv)
    ]
    parts = []
    for at, kernel in enumerate(kernels):
        grad = kernel(acc)
        if at < len(kernels) - 1:
            acc, grad = lax.optimization_barrier((acc, grad))
        parts.append(first_halving(grad, orders[at % kv], n))
    grads = [rest_halving(*part, orders[at % kv], n) for at, part in enumerate(parts)]
    grad_k, grad_v, sums = squares(grads, n * t)
    sums = lax.all_to_all(sums, ("dp", "tensor"), split_axis=0, concat_axis=0, tiled=True)
    own_keys = lax.dynamic_slice_in_dim(cache_keys, mine * share, share, 0)
    own_vals = lax.dynamic_slice_in_dim(cache_values, mine * share, share, 0)
    new_keys, new_values = update(sums, own_keys, own_vals, grad_k, grad_v)
    return (attended, new_keys, new_values)


def solution(mesh):
    placed = (
        P("dp", "tensor"),
        P("dp", "tensor"),
        P("dp", "tensor"),
        P(None, "tensor"),
        P(None, "tensor"),
        P("tensor", None),
        P("dp", "tensor"),
        P("dp", None),
    )
    return jax.shard_map(
        body,
        mesh=mesh,
        in_specs=placed,
        out_specs=(P("dp", "tensor"), P("dp", "tensor"), P("dp", "tensor")),
        check_vma=False,
    )
```

time: 126 us -> 85.2 us (0.68)
  waiting for transfers between devices: 43.7 us -> 22.1 us
  Pallas kernels: 38.4 us -> 30.1 us
  local copies, waits for them, and re-layouts: 13.6 us -> 7.27 us
  other arithmetic: 4.42 us -> 1.29 us
  between operations: 2.99 us -> 0.87 us
    ppermute x15, waiting for transfers between devices: 35.5 us -> 15.9 us  [exchange(): return lax.ppermute(value, axis, [(i, i ^ flip) for i in range(size)])]
    pallas_call x8 -> x10, Pallas kernels: 23.9 us -> 14.3 us  [the longest x4 5.27 us: project(): pl.pallas_call(functools.partial(project_kernel, acc is not None, heads),...]
    unnamed x18 -> x12, local copies, waits for them, and re-layouts: 12.8 us -> 5.3 us
    all_to_all x1, waiting for transfers between devices: 8.23 us -> 6.15 us  [body(): lax.all_to_all(sums, ('dp', 'tensor'), split_axis=0, concat_axis=0, tiled...]
    reduce_sum x3 -> x0, other arithmetic: 2.04 us -> none  [the longest x1 0.74 us: body(): jnp.sum(share_vals * share_vals)]
    dynamic_slice x0 -> x2, local copies, waits for them, and re-layouts: none -> 1.83 us  [the longest x1 0.92 us: body(): own_keys = lax.dynamic_slice_in_dim(cache_keys, mine * share, share, 0)]
    sub x1 -> x0, other arithmetic: 1.77 us -> none  [body(): new_values = own_vals - step_rate * share_vals / rms_value]
    pallas_call x1, Pallas kernels: 14.5 us -> 15.8 us  [forward(): pl.pallas_call(functools.partial(forward_kernel, orders, n), grid_spec=sp...]
  transfers between devices with their start and end apart: 16 -> 16, of which waited for: 7 -> 9; matrix products, arithmetic and copies ran while one was open for 1% -> 4% of each run, Pallas kernels for 25% -> 23%
where the time goes in v2:
time: 85.2 us; the launch traced here: 84.9 us
  Pallas kernels  30.1 us (35%)
  starting transfers between devices  23.3 us (27%)
  waiting for transfers between devices  22.1 us (26%)
  local copies, waits for them, and re-layouts  7.27 us (9%)
  other arithmetic  1.29 us (2%)
  between operations  0.87 us (1%)
    ppermute x15, starting transfers between devices, exchange(): return lax.ppermute(value, axis, [(i, i ^ flip) for i in range(size)])  20.1 us
    ppermute x15, waiting for transfers between devices, exchange(): return lax.ppermute(value, axis, [(i, i ^ flip) for i in range(size)])  15.9 us
    pallas_call x1, Pallas kernels, forward(): pl.pallas_call(functools.partial(forward_kernel, orders, n), grid_spec=sp...  15.8 us
    all_to_all x1, waiting for transfers between devices, body(): lax.all_to_all(sums, ('dp', 'tensor'), split_axis=0, concat_axis=0, tiled...  6.15 us
    unnamed x12, local copies, waits for them, and re-layouts  5.3 us
    pallas_call x4, Pallas kernels, project(): pl.pallas_call(functools.partial(project_kernel, acc is not None, heads),...  5.27 us
    pallas_call x2, Pallas kernels, key_grads(): pl.pallas_call(functools.partial(keys_kernel, head, order, n), in_specs=[...  4.76 us
    all_to_all x1, starting transfers between devices, body(): lax.all_to_all(sums, ('dp', 'tensor'), split_axis=0, concat_axis=0, tiled...  3.22 us
  transfers between devices with their start and end apart: 16, of which 9 were waited for; matrix products, arithmetic and copies ran while one was open for 4% of the time, Pallas kernels for 23%

profile of v2, /device:TPU:0, one launch (start us, length us, event | category | flops | bytes accessed | tf_op | source)
XLA Modules:
  0.0 84.9 jit_solution(8661823396775652443)
XLA Ops:
  0.6 0.5 collective-permute-start.1
  1.1 2.6 %collective-permute-start = (bf16[256,2048]{1,0:T(8,128)(2,1)}, bf16[256,2048]{1,0:T(8,128)(2,1)S(1)}, u32[]{:S(2)}, u32[]{:S(2)}) collective-permute-start(bf16[256,2048]{1,0:T(8,128)(2,1)} %g_ref.1), channel_id=1, source_target_pairs={{0,2},{1,3},{2,0},{3,1},{4,6},{5,7},{6,4},{7,5},{8,10},{9,11},{10,... | collective-permute-start | bytes 3145736 | tf_op jit(solution)/shard_map/ppermute | solution.py:333
  3.7 0.8 %fusion.1.bias_ref = f32[256,256]{1,0:T(8,128)S(1)} fusion(s32[256]{0:T(256)} %bitcast.8), kind=kLoop, calls=%fused_computation.10 | loop fusion | flops 262144 | bytes 263168 | tf_op jit(solution)/shard_map/jit(_where)/select_n | solution.py:369
  4.6 1.2 %copy-done = bf16[2048,256]{1,0:T(8,128)(2,1)S(1)} copy-done((bf16[2048,256]{1,0:T(8,128)(2,1)S(1)}, bf16[2048,256]{1,0:T(8,128)(2,1)}, u32[]{:S(2)}) %copy-start) | copy-done | bytes 1048600
  5.8 1.0 %copy-done.1 = bf16[256,1024]{1,0:T(8,128)(2,1)S(1)} copy-done((bf16[256,1024]{1,0:T(8,128)(2,1)S(1)}, bf16[256,1024]{1,0:T(8,128)(2,1)}, u32[]{:S(2)}) %copy-start.1) | copy-done | bytes 524312
  6.9 1.2 %copy-done.2 = bf16[2048,256]{1,0:T(8,128)(2,1)S(1)} copy-done((bf16[2048,256]{1,0:T(8,128)(2,1)S(1)}, bf16[2048,256]{1,0:T(8,128)(2,1)}, u32[]{:S(2)}) %copy-start.2) | copy-done | bytes 1048600
  8.1 0.9 %copy-done.4 = bf16[256,256]{1,0:T(8,128)(2,1)S(1)} copy-done((bf16[256,256]{1,0:T(8,128)(2,1)S(1)}, bf16[256,256]{1,0:T(8,128)(2,1)}, u32[]{:S(2)}) %copy-start.4) | copy-done | bytes 131096
  9.0 0.9 %copy-done.5 = bf16[256,256]{1,0:T(8,128)(2,1)S(1)} copy-done((bf16[256,256]{1,0:T(8,128)(2,1)S(1)}, bf16[256,256]{1,0:T(8,128)(2,1)}, u32[]{:S(2)}) %copy-start.5) | copy-done | bytes 131096
  9.9 15.8 %forward.1 = (bf16[2,2048,1024]{2,1,0:T(8,128)(2,1)S(1)}, bf16[256,1024]{1,0:T(8,128)(2,1)}, bf16[2,128,1024]{2,1,0:T(8,128)(2,1)S(1)}, bf16[1024,8192]{1,0:T(8,128)(2,1)S(1)}) custom-call(s32[1]{0:T(128)} %bitcast.me_ref, bf16[256,1024]{1,0:T(8,128)(2,1)S(1)} %copy-done.1, bf16[2048,256]{1,0:T(8,128)(2,1)S(1)} %copy-done.2, bf16[256,256]{1,0:T(8,128)(2,1)S(1)} %copy-done.4, ...), custom_call_target="tpu_custom_call" | custom-call | flops 2415919104 | bytes 8388608 | tf_op jit(solution)/shard_map/forward/pallas_call | solution.py:151
  25.7 1.3 %project.4.refs_0_ = f32[1024,256]{1,0:T(8,128)S(1)} custom-call(s32[1]{0:T(128)} %bitcast.2.shard_ref, bf16[1024,8192]{1,0:T(8,128)(2,1)S(1)} %get-tuple-element.21.w_ref, bf16[256,2048]{1,0:T(8,128)(2,1)S(1)} %copy-done.3), custom_call_target="tpu_custom_call" | custom-call | flops 1073741824 | bytes 4194304 | tf_op jit(solution)/shard_map/project/pallas_call | solution.py:198
  27.0 1.3 %project.5.refs_0_ = f32[1024,256]{1,0:T(8,128)S(1)} custom-call(s32[1]{0:T(128)S(6)} %xor.10.shard_ref, bf16[1024,8192]{1,0:T(8,128)(2,1)S(1)} %get-tuple-element.21.w_ref, bf16[256,2048]{1,0:T(8,128)(2,1)S(1)} %collective-permute-done.1.g_ref, f32[1024,256]{1,0:T(8,128)S(1)} %project.4.refs_0_), custom_call_target="tpu_custom_call" | custom-call | flops 1073741824 | bytes 4194304 | tf_op jit(solution)/shard_map/project/pallas_call | solution.py:198
  28.4 0.2 collective-permute-start.2
  28.6 1.3 %project.6.refs_0_ = f32[1024,256]{1,0:T(8,128)S(1)} custom-call(s32[1]{0:T(128)S(6)} %xor.11.shard_ref, bf16[1024,8192]{1,0:T(8,128)(2,1)S(1)} %get-tuple-element.21.w_ref, bf16[256,2048]{1,0:T(8,128)(2,1)S(1)} %collective-permute-done.g_ref, f32[1024,256]{1,0:T(8,128)S(1)} %project.5.refs_0_), custom_call_target="tpu_custom_call" | custom-call | flops 1073741824 | bytes 4194304 | tf_op jit(solution)/shard_map/project/pallas_call | solution.py:198
  29.9 1.2 %collective-permute-done.2.g_ref = bf16[256,2048]{1,0:T(8,128)(2,1)S(1)} collective-permute-done((bf16[256,2048]{1,0:T(8,128)(2,1)S(1)}, bf16[256,2048]{1,0:T(8,128)(2,1)S(1)}, u32[]{:S(2)}, u32[]{:S(2)}) %collective-permute-start.2) | collective-permute-done | bytes 1048608 | tf_op jit(solution)/shard_map/ppermute | solution.py:333
  31.1 1.3 %project.7.da_ref = bf16[2,128,1024]{2,1,0:T(8,128)(2,1)S(1)} custom-call(s32[1]{0:T(128)S(6)} %xor.9.shard_ref, bf16[1024,8192]{1,0:T(8,128)(2,1)S(1)} %get-tuple-element.21.w_ref, bf16[256,2048]{1,0:T(8,128)(2,1)S(1)} %collective-permute-done.2.g_ref, f32[1024,256]{1,0:T(8,128)S(1)} %project.6.refs_0_), custom_call_target="tpu_custom_call" | custom-call | flops 1073741824 | bytes 4194304 | tf_op jit(solution)/shard_map/project/pallas_call | solution.py:198
  32.4 1.2 %value_grads.2 = bf16[2048,128]{1,0:T(8,128)(2,1)S(1)} custom-call(bf16[2,2048,1024]{2,1,0:T(8,128)(2,1)S(1)} %get-tuple-element.24.p_ref, bf16[2,128,1024]{2,1,0:T(8,128)(2,1)S(1)} %project.7.da_ref), custom_call_target="tpu_custom_call" | custom-call | flops 4194304 | bytes 524288 | tf_op jit(solution)/shard_map/value_grads/pallas_call | solution.py:223
  33.7 1.2 %value_grads.3 = bf16[2048,128]{1,0:T(8,128)(2,1)S(1)} custom-call(bf16[2,2048,1024]{2,1,0:T(8,128)(2,1)S(1)} %get-tuple-element.24.p_ref, bf16[2,128,1024]{2,1,0:T(8,128)(2,1)S(1)} %project.7.da_ref), custom_call_target="tpu_custom_call" | custom-call | flops 4194304 | bytes 524288 | tf_op jit(solution)/shard_map/value_grads/pallas_call | solution.py:223
  34.9 2.4 %key_grads.2 = bf16[2048,128]{1,0:T(8,128)(2,1)S(1)} custom-call(s32[1]{0:T(128)} %bitcast.me_ref, bf16[2,2048,1024]{2,1,0:T(8,128)(2,1)S(1)} %get-tuple-element.24.p_ref, bf16[2048,256]{1,0:T(8,128)(2,1)S(1)} %copy-done, bf16[2,128,1024]{2,1,0:T(8,128)(2,1)S(1)} %project.7.da_ref, bf16[2,128,1024]{2,1,0:T(8,128)(2,1)S(1)} %get-tuple-element.29.att_ref, ...), custom_call_target="tpu_custom_call" | custom-call | flops 8388608 | bytes 524288 | tf_op jit(solution)/shard_map/key_grads/pallas_call | solution.py:263
  37.3 2.4 %key_grads.3 = bf16[2048,128]{1,0:T(8,128)(2,1)S(1)} custom-call(s32[1]{0:T(128)} %bitcast.me_ref, bf16[2,2048,1024]{2,1,0:T(8,128)(2,1)S(1)} %get-tuple-element.24.p_ref, bf16[2048,256]{1,0:T(8,128)(2,1)S(1)} %copy-done, bf16[2,128,1024]{2,1,0:T(8,128)(2,1)S(1)} %project.7.da_ref, bf16[2,128,1024]{2,1,0:T(8,128)(2,1)S(1)} %get-tuple-element.29.att_ref, ...), custom_call_target="tpu_custom_call" | custom-call | flops 8388608 | bytes 524288 | tf_op jit(solution)/shard_map/key_grads/pallas_call | solution.py:263
  39.7 1.6 %collective-permute-start.12 = (bf16[1024,128]{1,0:T(8,128)(2,1)S(1)}, bf16[1024,128]{1,0:T(8,128)(2,1)S(1)}, u32[]{:S(2)}, u32[]{:S(2)}) collective-permute-start(bf16[1024,128]{1,0:T(8,128)(2,1)S(1)} %slice.90), channel_id=1, source_target_pairs={{0,8},{4,12},{8,0},{12,4},{16,24},{20,28},{24,16},{28,20},{1,9},{5... | collective-permute-start | bytes 786440 | tf_op jit(solution)/shard_map/ppermute | solution.py:333
  41.4 1.6 %collective-permute-start.9 = (bf16[1024,128]{1,0:T(8,128)(2,1)S(1)}, bf16[1024,128]{1,0:T(8,128)(2,1)S(1)}, u32[]{:S(2)}, u32[]{:S(2)}) collective-permute-start(bf16[1024,128]{1,0:T(8,128)(2,1)S(1)} %slice.71), channel_id=1, source_target_pairs={{0,4},{4,0},{8,12},{12,8},{16,20},{20,16},{24,28},{28,24},{1,5},{5... | collective-permute-start | bytes 786440 | tf_op jit(solution)/shard_map/ppermute | solution.py:333
  43.0 0.5 collective-permute-start.6
  43.5 0.6 collective-permute-start.3
  44.1 4.8 %collective-permute-done.12 = bf16[1024,128]{1,0:T(8,128)(2,1)S(1)} collective-permute-done((bf16[1024,128]{1,0:T(8,128)(2,1)S(1)}, bf16[1024,128]{1,0:T(8,128)(2,1)S(1)}, u32[]{:S(2)}, u32[]{:S(2)}) %collective-permute-start.12) | collective-permute-done | bytes 262176 | tf_op jit(solution)/shard_map/ppermute | solution.py:333
  48.9 0.1 add_convert_fusion
  49.0 1.6 %collective-permute-start.13 = (bf16[512,128]{1,0:T(8,128)(2,1)S(1)}, bf16[512,128]{1,0:T(8,128)(2,1)S(1)}, u32[]{:S(2)}, u32[]{:S(2)}) collective-permute-start(bf16[512,128]{1,0:T(8,128)(2,1)S(1)} %slice.92), channel_id=1, source_target_pairs={{0,4},{4,0},{8,12},{12,8},{16,20},{20,16},{24,28},{28,24},{1,5},{5... | collective-permute-start | bytes 393224 | tf_op jit(solution)/shard_map/ppermute | solution.py:333
  50.6 0.1 add_convert_fusion.1
  50.7 1.6 %collective-permute-start.10 = (bf16[512,128]{1,0:T(8,128)(2,1)S(1)}, bf16[512,128]{1,0:T(8,128)(2,1)S(1)}, u32[]{:S(2)}, u32[]{:S(2)}) collective-permute-start(bf16[512,128]{1,0:T(8,128)(2,1)S(1)} %slice.87), channel_id=1, source_target_pairs={{0,8},{4,12},{8,0},{12,4},{16,24},{20,28},{24,16},{28,20},{1,9},{5... | collective-permute-start | bytes 393224 | tf_op jit(solution)/shard_map/ppermute | solution.py:333
  52.3 2.2 %collective-permute-done.6 = bf16[1024,128]{1,0:T(8,128)(2,1)S(1)} collective-permute-done((bf16[1024,128]{1,0:T(8,128)(2,1)S(1)}, bf16[1024,128]{1,0:T(8,128)(2,1)S(1)}, u32[]{:S(2)}, u32[]{:S(2)}) %collective-permute-start.6) | collective-permute-done | bytes 262176 | tf_op jit(solution)/shard_map/ppermute | solution.py:333
  54.6 0.1 add_convert_fusion.2
  54.7 1.6 %collective-permute-start.7 = (bf16[512,128]{1,0:T(8,128)(2,1)S(1)}, bf16[512,128]{1,0:T(8,128)(2,1)S(1)}, u32[]{:S(2)}, u32[]{:S(2)}) collective-permute-start(bf16[512,128]{1,0:T(8,128)(2,1)S(1)} %slice.84), channel_id=1, source_target_pairs={{0,4},{4,0},{8,12},{12,8},{16,20},{20,16},{24,28},{28,24},{1,5},{5... | collective-permute-start | bytes 393224 | tf_op jit(solution)/shard_map/ppermute | solution.py:333
  56.3 0.1 add_convert_fusion.3
  56.3 1.6 %collective-permute-start.4 = (bf16[512,128]{1,0:T(8,128)(2,1)S(1)}, bf16[512,128]{1,0:T(8,128)(2,1)S(1)}, u32[]{:S(2)}, u32[]{:S(2)}) collective-permute-start(bf16[512,128]{1,0:T(8,128)(2,1)S(1)} %slice.81), channel_id=1, source_target_pairs={{0,8},{4,12},{8,0},{12,4},{16,24},{20,28},{24,16},{28,20},{1,9},{5... | collective-permute-start | bytes 393224 | tf_op jit(solution)/shard_map/ppermute | solution.py:333
  57.9 1.1 %collective-permute-done.13 = bf16[512,128]{1,0:T(8,128)(2,1)S(1)} collective-permute-done((bf16[512,128]{1,0:T(8,128)(2,1)S(1)}, bf16[512,128]{1,0:T(8,128)(2,1)S(1)}, u32[]{:S(2)}, u32[]{:S(2)}) %collective-permute-start.13) | collective-permute-done | bytes 131104 | tf_op jit(solution)/shard_map/ppermute | solution.py:333
  59.1 2.7 %collective-permute-start.14 = (bf16[256,128]{1,0:T(8,128)(2,1)S(1)}, bf16[256,128]{1,0:T(8,128)(2,1)S(1)}, u32[]{:S(2)}, u32[]{:S(2)}) collective-permute-start(bf16[256,128]{1,0:T(8,128)(2,1)S(1)} %slice.93), channel_id=1, source_target_pairs={{0,16},{4,20},{8,24},{12,28},{16,0},{20,4},{24,8},{28,12},{1,17},{... | collective-permute-start | bytes 196616 | tf_op jit(solution)/shard_map/ppermute | solution.py:333
  61.8 0.4 collective-permute-start.11
  62.3 2.6 %collective-permute-start.8 = (bf16[256,128]{1,0:T(8,128)(2,1)S(1)}, bf16[256,128]{1,0:T(8,128)(2,1)S(1)}, u32[]{:S(2)}, u32[]{:S(2)}) collective-permute-start(bf16[256,128]{1,0:T(8,128)(2,1)S(1)} %slice.85), channel_id=1, source_target_pairs={{0,16},{4,20},{8,24},{12,28},{16,0},{20,4},{24,8},{28,12},{1,17},{... | collective-permute-start | bytes 196616 | tf_op jit(solution)/shard_map/ppermute | solution.py:333
  65.0 0.4 collective-permute-start.5
  65.4 0.9 %constant_dynamic-slice_fusion.vals_ref = bf16[256,256]{1,0:T(8,128)(2,1)S(1)} fusion(bf16[2048,256]{1,0:T(8,128)(2,1)} %v_ref.5, s32[]{:T(128)S(6)} %select_n.9), kind=kLoop, calls=%fused_computation.11 | loop fusion | bytes 262148 | tf_op jit(solution)/shard_map/dynamic_slice | solution.py:400
  66.3 2.6 %collective-permute-done.14.refs_7_ = bf16[256,128]{1,0:T(8,128)(2,1)S(1)} collective-permute-done((bf16[256,128]{1,0:T(8,128)(2,1)S(1)}, bf16[256,128]{1,0:T(8,128)(2,1)S(1)}, u32[]{:S(2)}, u32[]{:S(2)}) %collective-permute-start.14) | collective-permute-done | bytes 65568 | tf_op jit(solution)/shard_map/ppermute | solution.py:333
  68.9 2.1 %collective-permute-done.11.refs_5_ = bf16[256,128]{1,0:T(8,128)(2,1)S(1)} collective-permute-done((bf16[256,128]{1,0:T(8,128)(2,1)S(1)}, bf16[256,128]{1,0:T(8,128)(2,1)S(1)}, u32[]{:S(2)}, u32[]{:S(2)}) %collective-permute-start.11) | collective-permute-done | bytes 65568 | tf_op jit(solution)/shard_map/ppermute | solution.py:333
  71.0 1.1 %collective-permute-done.8.refs_3_ = bf16[256,128]{1,0:T(8,128)(2,1)S(1)} collective-permute-done((bf16[256,128]{1,0:T(8,128)(2,1)S(1)}, bf16[256,128]{1,0:T(8,128)(2,1)S(1)}, u32[]{:S(2)}, u32[]{:S(2)}) %collective-permute-start.8) | collective-permute-done | bytes 65568 | tf_op jit(solution)/shard_map/ppermute | solution.py:333
  72.1 0.7 collective-permute-done.5.refs_1_
  72.8 0.8 squares.1
  73.6 3.2 %all-to-all-start = ((f32[32,1,128]{2,1,0:T(1,128)}), f32[32,1,128]{2,1,0:T(1,128)S(1)}, u32[]{:S(2)}, u32[]{:S(2)}) async-start(f32[32,1,128]{2,1,0:T(1,128)} %bitcast.4), calls=%async_computation | async-start | bytes 32768 | tf_op jit(solution)/shard_map/all_to_all | solution.py:398
  76.9 0.9 %constant_dynamic-slice_fusion.1.keys_ref = bf16[256,256]{1,0:T(8,128)(2,1)S(1)} fusion(bf16[2048,256]{1,0:T(8,128)(2,1)} %k_ref.1, s32[]{:T(128)S(6)} %select_n.9), kind=kLoop, calls=%fused_computation.12 | loop fusion | bytes 262148 | tf_op jit(solution)/shard_map/dynamic_slice | solution.py:399
  77.8 6.1 %all-to-all-done = f32[32,1,128]{2,1,0:T(1,128)S(1)} async-done(((f32[32,1,128]{2,1,0:T(1,128)}), f32[32,1,128]{2,1,0:T(1,128)S(1)}, u32[]{:S(2)}, u32[]{:S(2)}) %all-to-all-start) | async-done | bytes 16416 | tf_op jit(solution)/shard_map/all_to_all | solution.py:398
  84.0 0.9 %update.1 = (f32[256,256]{1,0:T(8,128)}, f32[256,256]{1,0:T(8,128)}) custom-call(f32[32,128]{1,0:T(8,128)S(1)} %bitcast.7, bf16[256,256]{1,0:T(8,128)(2,1)S(1)} %constant_dynamic-slice_fusion.1.keys_ref, bf16[256,256]{1,0:T(8,128)(2,1)S(1)} %constant_dynamic-slice_fusion.vals_ref, f32[256,256]{1,0:T(8,128)S(1)} %get-tuple-element.33.grad_k_ref, ...), custom_call_target="tpu_custom_call" | custom-call | flops 262144 | bytes 1310720 | tf_op jit(solution)/shard_map/update/pallas_call | solution.py:319
  (30 shorter events, 0.4 us)
Async XLA Ops:
  0.6 26.4 %collective-permute-start.1 = (bf16[256,2048]{1,0:T(8,128)(2,1)}, bf16[256,2048]{1,0:T(8,128)(2,1)S(1)}, u32[]{:S(2)}, u32[]{:S(2)}) collective-permute-start(bf16[256,2048]{1,0:T(8,128)(2,1)} %g_ref.1), channel_id=1, source_target_pairs={{0,1},{1,0},{2,3},{3,2},{4,5},{5,4},{6,7},{7,6},{8,9},{9,8},{10,11... | collective-permute-start | bytes 3145736 | tf_op jit(solution)/shard_map/ppermute | solution.py:333
  1.1 27.2 %collective-permute-start = (bf16[256,2048]{1,0:T(8,128)(2,1)}, bf16[256,2048]{1,0:T(8,128)(2,1)S(1)}, u32[]{:S(2)}, u32[]{:S(2)}) collective-permute-start(bf16[256,2048]{1,0:T(8,128)(2,1)} %g_ref.1), channel_id=1, source_target_pairs={{0,2},{1,3},{2,0},{3,1},{4,6},{5,7},{6,4},{7,5},{8,10},{9,11},{10,... | collective-permute-start | bytes 3145736 | tf_op jit(solution)/shard_map/ppermute | solution.py:333
  4.6 1.2 %copy-start = (bf16[2048,256]{1,0:T(8,128)(2,1)S(1)}, bf16[2048,256]{1,0:T(8,128)(2,1)}, u32[]{:S(2)}) copy-start(bf16[2048,256]{1,0:T(8,128)(2,1)} %v_ref.5) | copy-start | bytes 3145732
  5.8 1.0 %copy-start.1 = (bf16[256,1024]{1,0:T(8,128)(2,1)S(1)}, bf16[256,1024]{1,0:T(8,128)(2,1)}, u32[]{:S(2)}) copy-start(bf16[256,1024]{1,0:T(8,128)(2,1)} %q_ref.5) | copy-start | bytes 1572868
  6.9 1.2 %copy-start.2 = (bf16[2048,256]{1,0:T(8,128)(2,1)S(1)}, bf16[2048,256]{1,0:T(8,128)(2,1)}, u32[]{:S(2)}) copy-start(bf16[2048,256]{1,0:T(8,128)(2,1)} %k_ref.1) | copy-start | bytes 3145732
  8.1 0.9 %copy-start.4 = (bf16[256,256]{1,0:T(8,128)(2,1)S(1)}, bf16[256,256]{1,0:T(8,128)(2,1)}, u32[]{:S(2)}) copy-start(bf16[256,256]{1,0:T(8,128)(2,1)} %ks_ref.1) | copy-start | bytes 393220
  9.0 0.9 %copy-start.5 = (bf16[256,256]{1,0:T(8,128)(2,1)S(1)}, bf16[256,256]{1,0:T(8,128)(2,1)}, u32[]{:S(2)}) copy-start(bf16[256,256]{1,0:T(8,128)(2,1)} %vs_ref.1) | copy-start | bytes 393220
  9.9 15.8 %copy-start.3 = (bf16[256,2048]{1,0:T(8,128)(2,1)S(1)}, bf16[256,2048]{1,0:T(8,128)(2,1)}, u32[]{:S(2)}) copy-start(bf16[256,2048]{1,0:T(8,128)(2,1)} %g_ref.1) | copy-start | bytes 3145732
  28.4 2.7 %collective-permute-start.2 = (bf16[256,2048]{1,0:T(8,128)(2,1)S(1)}, bf16[256,2048]{1,0:T(8,128)(2,1)S(1)}, u32[]{:S(2)}, u32[]{:S(2)}) collective-permute-start(bf16[256,2048]{1,0:T(8,128)(2,1)S(1)} %collective-permute-done.g_ref), channel_id=1, source_target_pairs={{0,1},{1,0},{2,3},{3,2},{4,5},{5,4},{6,7},{7,6},{8,9},{9,8},{10,11... | collective-permute-start | bytes 3145736 | tf_op jit(solution)/shard_map/ppermute | solution.py:333
  39.7 9.2 %collective-permute-start.12 = (bf16[1024,128]{1,0:T(8,128)(2,1)S(1)}, bf16[1024,128]{1,0:T(8,128)(2,1)S(1)}, u32[]{:S(2)}, u32[]{:S(2)}) collective-permute-start(bf16[1024,128]{1,0:T(8,128)(2,1)S(1)} %slice.90), channel_id=1, source_target_pairs={{0,8},{4,12},{8,0},{12,4},{16,24},{20,28},{24,16},{28,20},{1,9},{5... | collective-permute-start | bytes 786440 | tf_op jit(solution)/shard_map/ppermute | solution.py:333
  41.4 9.3 %collective-permute-start.9 = (bf16[1024,128]{1,0:T(8,128)(2,1)S(1)}, bf16[1024,128]{1,0:T(8,128)(2,1)S(1)}, u32[]{:S(2)}, u32[]{:S(2)}) collective-permute-start(bf16[1024,128]{1,0:T(8,128)(2,1)S(1)} %slice.71), channel_id=1, source_target_pairs={{0,4},{4,0},{8,12},{12,8},{16,20},{20,16},{24,28},{28,24},{1,5},{5... | collective-permute-start | bytes 786440 | tf_op jit(solution)/shard_map/ppermute | solution.py:333
  43.0 11.6 %collective-permute-start.6 = (bf16[1024,128]{1,0:T(8,128)(2,1)S(1)}, bf16[1024,128]{1,0:T(8,128)(2,1)S(1)}, u32[]{:S(2)}, u32[]{:S(2)}) collective-permute-start(bf16[1024,128]{1,0:T(8,128)(2,1)S(1)} %slice.66), channel_id=1, source_target_pairs={{0,8},{4,12},{8,0},{12,4},{16,24},{20,28},{24,16},{28,20},{1,9},{5... | collective-permute-start | bytes 786440 | tf_op jit(solution)/shard_map/ppermute | solution.py:333
  43.5 12.8 %collective-permute-start.3 = (bf16[1024,128]{1,0:T(8,128)(2,1)S(1)}, bf16[1024,128]{1,0:T(8,128)(2,1)S(1)}, u32[]{:S(2)}, u32[]{:S(2)}) collective-permute-start(bf16[1024,128]{1,0:T(8,128)(2,1)S(1)} %slice.61), channel_id=1, source_target_pairs={{0,4},{4,0},{8,12},{12,8},{16,20},{20,16},{24,28},{28,24},{1,5},{5... | collective-permute-start | bytes 786440 | tf_op jit(solution)/shard_map/ppermute | solution.py:333
  49.0 10.0 %collective-permute-start.13 = (bf16[512,128]{1,0:T(8,128)(2,1)S(1)}, bf16[512,128]{1,0:T(8,128)(2,1)S(1)}, u32[]{:S(2)}, u32[]{:S(2)}) collective-permute-start(bf16[512,128]{1,0:T(8,128)(2,1)S(1)} %slice.92), channel_id=1, source_target_pairs={{0,4},{4,0},{8,12},{12,8},{16,20},{20,16},{24,28},{28,24},{1,5},{5... | collective-permute-start | bytes 393224 | tf_op jit(solution)/shard_map/ppermute | solution.py:333
  50.7 11.0 %collective-permute-start.10 = (bf16[512,128]{1,0:T(8,128)(2,1)S(1)}, bf16[512,128]{1,0:T(8,128)(2,1)S(1)}, u32[]{:S(2)}, u32[]{:S(2)}) collective-permute-start(bf16[512,128]{1,0:T(8,128)(2,1)S(1)} %slice.87), channel_id=1, source_target_pairs={{0,8},{4,12},{8,0},{12,4},{16,24},{20,28},{24,16},{28,20},{1,9},{5... | collective-permute-start | bytes 393224 | tf_op jit(solution)/shard_map/ppermute | solution.py:333
  54.7 7.6 %collective-permute-start.7 = (bf16[512,128]{1,0:T(8,128)(2,1)S(1)}, bf16[512,128]{1,0:T(8,128)(2,1)S(1)}, u32[]{:S(2)}, u32[]{:S(2)}) collective-permute-start(bf16[512,128]{1,0:T(8,128)(2,1)S(1)} %slice.84), channel_id=1, source_target_pairs={{0,4},{4,0},{8,12},{12,8},{16,20},{20,16},{24,28},{28,24},{1,5},{5... | collective-permute-start | bytes 393224 | tf_op jit(solution)/shard_map/ppermute | solution.py:333
  56.3 8.6 %collective-permute-start.4 = (bf16[512,128]{1,0:T(8,128)(2,1)S(1)}, bf16[512,128]{1,0:T(8,128)(2,1)S(1)}, u32[]{:S(2)}, u32[]{:S(2)}) collective-permute-start(bf16[512,128]{1,0:T(8,128)(2,1)S(1)} %slice.81), channel_id=1, source_target_pairs={{0,8},{4,12},{8,0},{12,4},{16,24},{20,28},{24,16},{28,20},{1,9},{5... | collective-permute-start | bytes 393224 | tf_op jit(solution)/shard_map/ppermute | solution.py:333
  59.1 9.8 %collective-permute-start.14 = (bf16[256,128]{1,0:T(8,128)(2,1)S(1)}, bf16[256,128]{1,0:T(8,128)(2,1)S(1)}, u32[]{:S(2)}, u32[]{:S(2)}) collective-permute-start(bf16[256,128]{1,0:T(8,128)(2,1)S(1)} %slice.93), channel_id=1, source_target_pairs={{0,16},{4,20},{8,24},{12,28},{16,0},{20,4},{24,8},{28,12},{1,17},{... | collective-permute-start | bytes 196616 | tf_op jit(solution)/shard_map/ppermute | solution.py:333
  61.8 9.2 %collective-permute-start.11 = (bf16[256,128]{1,0:T(8,128)(2,1)S(1)}, bf16[256,128]{1,0:T(8,128)(2,1)S(1)}, u32[]{:S(2)}, u32[]{:S(2)}) collective-permute-start(bf16[256,128]{1,0:T(8,128)(2,1)S(1)} %slice.88), channel_id=1, source_target_pairs={{0,16},{4,20},{8,24},{12,28},{16,0},{20,4},{24,8},{28,12},{1,17},{... | collective-permute-start | bytes 196616 | tf_op jit(solution)/shard_map/ppermute | solution.py:333
  62.3 9.8 %collective-permute-start.8 = (bf16[256,128]{1,0:T(8,128)(2,1)S(1)}, bf16[256,128]{1,0:T(8,128)(2,1)S(1)}, u32[]{:S(2)}, u32[]{:S(2)}) collective-permute-start(bf16[256,128]{1,0:T(8,128)(2,1)S(1)} %slice.85), channel_id=1, source_target_pairs={{0,16},{4,20},{8,24},{12,28},{16,0},{20,4},{24,8},{28,12},{1,17},{... | collective-permute-start | bytes 196616 | tf_op jit(solution)/shard_map/ppermute | solution.py:333
  65.0 7.8 %collective-permute-start.5 = (bf16[256,128]{1,0:T(8,128)(2,1)S(1)}, bf16[256,128]{1,0:T(8,128)(2,1)S(1)}, u32[]{:S(2)}, u32[]{:S(2)}) collective-permute-start(bf16[256,128]{1,0:T(8,128)(2,1)S(1)} %slice.82), channel_id=1, source_target_pairs={{0,16},{4,20},{8,24},{12,28},{16,0},{20,4},{24,8},{28,12},{1,17},{... | collective-permute-start | bytes 196616 | tf_op jit(solution)/shard_map/ppermute | solution.py:333
  73.6 10.3 %all-to-all-start = ((f32[32,1,128]{2,1,0:T(1,128)}), f32[32,1,128]{2,1,0:T(1,128)S(1)}, u32[]{:S(2)}, u32[]{:S(2)}) async-start(f32[32,1,128]{2,1,0:T(1,128)} %bitcast.4), calls=%async_computation | async-start | bytes 32768 | tf_op jit(solution)/shard_map/all_to_all | solution.py:398

commit v3 on v2

--- a/solution.py
+++ b/solution.py
@@ -27,15 +27,9 @@
     return lax.dot_general(a, b, dims, preferred_element_type=F32)
 
 
-def bit_orders(n, heads):
-    bits = max(1, n.bit_length() - 1)
-    first = list(range(bits))
-    if n == 1:
-        return [[] for _ in range(heads)]
-    second = first[:]
-    if bits > 1:
-        second[0], second[1] = second[1], second[0]
-    return [first if head % 2 == 0 else second for head in range(heads)]
+def bit_orders(n):
+    first = list(range(n.bit_length() - 1))
+    return first, first[1::-1] + first[2:]
 
 
 def place_of(rel, order):
@@ -52,15 +46,8 @@
     return rel
 
 
-def per_head(g, orders, fn):
-    even = fn(orders[0])
-    if len(orders) == 1:
-        return even
-    return jnp.where(g % 2 == 0, even, fn(orders[1]))
-
-
 def forward_kernel(
-    orders, n, me_ref, q_ref, k_ref, ks_ref, v_ref, vs_ref, bias_ref, w_ref,
+    order, n, me_ref, q_ref, k_ref, ks_ref, v_ref, vs_ref, bias_ref, w_ref,
     p_ref, att_ref, att_t_ref, held_ref, s_ref, sems,
 ):
     g, j = pl.program_id(0), pl.program_id(1)
@@ -83,6 +70,7 @@
     share = slots // n
     chunk = 256
     scale = math.log2(math.e) / math.sqrt(HD)
+    columns = pl.ds(pl.multiple_of(j * length, length), length)
     q = q_ref[...]
     steps = [(k_ref, v_ref, c, c, chunk) for c in range(0, slots, chunk)]
     steps.append((ks_ref, vs_ref, 0, slots, length))
@@ -109,9 +97,9 @@
             piece = min(share, size)
             for b in range(0, size, piece):
                 block, inside = (at + b) // share, (at + b) % share
-                place = per_head(g, orders, functools.partial(place_of, block ^ me))
+                place = place_of(block ^ me, order)
                 start = pl.multiple_of(place * share + inside, piece)
-                p_ref[0, pl.ds(start, piece), :] = p[b : b + piece, :]
+                p_ref[g, pl.ds(start, piece), columns] = p[b : b + piece, :]
         part = mm(values[at : at + size, :], p, TN)
         att = part if att is None else att + part
     att_t_ref[0] = att.astype(BF16)
@@ -123,7 +111,7 @@
             copy.wait()
 
 
-def forward(me, queries, cache_k, span_k, cache_v, span_v, bias, weights, orders, n):
+def forward(me, queries, cache_k, span_k, cache_v, span_v, bias, weights, order, n):
     length, width = queries.shape
     slots, kv_width = cache_k.shape
     kv = kv_width // HD
@@ -141,7 +129,7 @@
             pl.BlockSpec(memory_space=pl.ANY),
         ],
         out_specs=[
-            pl.BlockSpec((1, slots, length), lambda g, j, me: (g, 0, j)),
+            pl.BlockSpec(memory_space=pltpu.VMEM),
             pl.BlockSpec((length, HD), lambda g, j, me: (0, g * group + j)),
             pl.BlockSpec((1, HD, length), lambda g, j, me: (g, 0, j)),
             pl.BlockSpec(memory_space=pltpu.VMEM),
@@ -149,7 +137,7 @@
         scratch_shapes=[pltpu.VMEM((slots + length, length), F32), pltpu.SemaphoreType.DMA((4,))],
     )
     return pl.pallas_call(
-        functools.partial(forward_kernel, orders, n),
+        functools.partial(forward_kernel, order, n),
         grid_spec=spec,
         out_shape=[
             jax.ShapeDtypeStruct((kv, slots, group * length), BF16),
@@ -165,6 +153,36 @@
         ),
         name="forward",
     )(me, queries, cache_k, span_k, cache_v, span_v, bias, weights)
+
+
+def streamed_kernel(shard_ref, w_ref, g_ref, out_ref):
+    out_ref[...] = mm(w_ref[...], g_ref[...], NT)
+
+
+def project_streamed(shard, out_proj, grad):
+    rows = out_proj.shape[0]
+    length, features = grad.shape
+    block = min(256, rows)
+    return pl.pallas_call(
+        streamed_kernel,
+        grid_spec=pltpu.PrefetchScalarGridSpec(
+            num_scalar_prefetch=1,
+            grid=(rows // block,),
+            in_specs=[
+                pl.BlockSpec((block, features), lambda m, shard: (m, shard[0])),
+                pl.BlockSpec((length, features), lambda m, shard: (0, 0)),
+            ],
+            out_specs=pl.BlockSpec((block, length), lambda m, shard: (m, 0)),
+        ),
+        out_shape=jax.ShapeDtypeStruct((rows, length), F32),
+        compiler_params=pltpu.CompilerParams(vmem_limit_bytes=46 * MIB),
+        cost_estimate=pl.CostEstimate(
+            flops=2 * rows * length * features,
+            bytes_accessed=2 * rows * features,
+            transcendentals=0,
+        ),
+        name="project_streamed",
+    )(shard, out_proj, grad)
 
 
 def project_kernel(adds, heads, shard_ref, w_ref, g_ref, *refs):
@@ -210,18 +228,25 @@
     )(*args)
 
 
-def values_kernel(head, p_ref, da_ref, out_ref):
-    rows = 256
+def row_pieces(slots, n, base, order):
+    share = slots // n
+    size = min(share, 256)
+    for row in range(0, slots, size):
+        away = block_at(row // share, base)
+        yield row, place_of(away, order) * share + row % share, size, away
+
+
+def values_kernel(head, orders, n, p_ref, da_ref, out_ref):
     da = da_ref[head]
-    for at in range(0, p_ref.shape[1], rows):
-        out_ref[at : at + rows, :] = mm(p_ref[head, at : at + rows, :], da, NT).astype(BF16)
-
-
-def value_grads(head, probs, grad_att_t):
+    for row, to, size, _ in row_pieces(p_ref.shape[1], n, *orders):
+        out_ref[to : to + size, :] = mm(p_ref[head, row : row + size, :], da, NT).astype(BF16)
+
+
+def value_grads(head, probs, grad_att_t, orders, n):
     _, slots, wide = probs.shape
     vmem = pl.BlockSpec(memory_space=pltpu.VMEM)
     return pl.pallas_call(
-        functools.partial(values_kernel, head),
+        functools.partial(values_kernel, head, orders, n),
         in_specs=[vmem, vmem],
         out_specs=vmem,
         out_shape=jax.ShapeDtypeStruct((slots, HD), BF16),
@@ -233,35 +258,33 @@
     )(probs, grad_att_t)
 
 
-def keys_kernel(head, order, n, me_ref, p_ref, v_ref, da_ref, att_ref, q_ref, out_ref):
+def keys_kernel(head, orders, n, me_ref, p_ref, v_ref, da_ref, att_ref, q_ref, out_ref):
     me = me_ref[0]
     slots = p_ref.shape[1]
     share = slots // n
     length = q_ref.shape[0]
     group = p_ref.shape[2] // length
-    piece = min(share, 256)
     da = da_ref[head]
     dot = jnp.sum(da.astype(F32) * att_ref[head].astype(F32), axis=0, keepdims=True)
     first = head * group * HD
     q = jnp.concatenate(
         [q_ref[:, first + j * HD : first + (j + 1) * HD] for j in range(group)], axis=0
     )
-    for row in range(0, slots, piece):
-        block = block_at(row // share, order) ^ me
-        start = pl.multiple_of(block * share + row % share, piece)
-        values = v_ref[pl.ds(start, piece), head * HD : (head + 1) * HD]
+    for row, to, size, away in row_pieces(slots, n, *orders):
+        start = pl.multiple_of((away ^ me) * share + row % share, size)
+        values = v_ref[pl.ds(start, size), head * HD : (head + 1) * HD]
         grad_p = mm(values, da, NN)
-        p = p_ref[head, row : row + piece, :].astype(F32)
+        p = p_ref[head, row : row + size, :].astype(F32)
         grad_s = (p * (grad_p - dot)).astype(BF16)
         total = mm(grad_s, q, NN) * (1.0 / math.sqrt(HD))
-        out_ref[row : row + piece, :] = total.astype(BF16)
-
-
-def key_grads(head, me, probs, cache_v, grad_att_t, att_t, queries, order, n):
+        out_ref[to : to + size, :] = total.astype(BF16)
+
+
+def key_grads(head, me, probs, cache_v, grad_att_t, att_t, queries, orders, n):
     _, slots, wide = probs.shape
     vmem = pl.BlockSpec(memory_space=pltpu.VMEM)
     return pl.pallas_call(
-        functools.partial(keys_kernel, head, order, n),
+        functools.partial(keys_kernel, head, orders, n),
         in_specs=[pl.BlockSpec(memory_space=pltpu.SMEM)] + [vmem] * 5,
         out_specs=vmem,
         out_shape=jax.ShapeDtypeStruct((slots, HD), BF16),
@@ -280,7 +303,7 @@
     for at in range(count):
         own_ref, got_ref = parts[2 * at], parts[2 * at + 1]
         total = own_ref[: got_ref.shape[0], :].astype(F32) + got_ref[...].astype(F32)
-        out_ref, head = (vals_ref, at) if at < half else (keys_ref, at - half)
+        out_ref, head = (keys_ref, at) if at < half else (vals_ref, at - half)
         out_ref[:, head * HD : (head + 1) * HD] = total
         here = jnp.sum((total * total).reshape(-1, 8, HD), axis=0)
         square = here if square is None else square + here
@@ -306,7 +329,7 @@
     )(*flat)
 
 
-def update_kernel(sums_ref, keys_ref, vals_ref, grad_k_ref, grad_v_ref, new_k_ref, new_v_ref):
+def update_kernel(me_ref, sums_ref, keys_ref, vals_ref, grad_k_ref, grad_v_ref, new_k_ref, new_v_ref):
     total = jnp.sum(sums_ref[...], axis=0, keepdims=True)[:, :1]
     rms = jnp.sqrt(total / (2 * SLOTS * KVH * HD) + epsilon)
     factor = step_rate / rms
@@ -314,19 +337,25 @@
     new_v_ref[...] = vals_ref[...].astype(F32) - factor * grad_v_ref[...]
 
 
-def update(sums, own_keys, own_vals, grad_k, grad_v):
-    vmem = pl.BlockSpec(memory_space=pltpu.VMEM)
+def update(me, sums, cache_k, cache_v, grad_k, grad_v):
+    share, width = grad_k.shape
+    own = pl.BlockSpec((share, width), lambda i, me: (me[0], 0))
+    whole = pl.BlockSpec((share, width), lambda i, me: (0, 0))
     return pl.pallas_call(
         update_kernel,
-        in_specs=[vmem] * 5,
-        out_specs=[vmem] * 2,
+        grid_spec=pltpu.PrefetchScalarGridSpec(
+            num_scalar_prefetch=1,
+            grid=(1,),
+            in_specs=[pl.BlockSpec(sums.shape, lambda i, me: (0, 0)), own, own, whole, whole],
+            out_specs=[whole, whole],
+        ),
         out_shape=[jax.ShapeDtypeStruct(grad_k.shape, F32)] * 2,
         compiler_params=pltpu.CompilerParams(vmem_limit_bytes=8 * MIB),
         cost_estimate=pl.CostEstimate(
             flops=4 * grad_k.size, bytes_accessed=20 * grad_k.size, transcendentals=0
         ),
         name="update",
-    )(sums, own_keys, own_vals, grad_k, grad_v)
+    )(me, sums, cache_k, cache_v, grad_k, grad_v)
 
 
 def exchange(value, axis, size, flip):
@@ -339,25 +368,34 @@
     return part, exchange(part[part.shape[0] // 2 :], "dp", n, 1 << order[0])
 
 
-def rest_halving(part, got, order, n):
-    for bit in order[1:]:
-        half = got.shape[0]
-        part = (part[:half].astype(F32) + got.astype(F32)).astype(BF16)
-        got = exchange(part[half // 2 :], "dp", n, 1 << bit)
-    return part, got
+def next_halving(part, bit, n):
+    rows, got = part
+    half = got.shape[0]
+    rows = (rows[:half].astype(F32) + got.astype(F32)).astype(BF16)
+    return rows, exchange(rows[half // 2 :], "dp", n, 1 << bit)
+
+
+def in_order(value, part):
+    rows, got = part
+    if isinstance(value, tuple):
+        value_rows, value_got = value
+        value_got, got = lax.optimization_barrier((value_got, got))
+        return (value_rows, value_got), (rows, got)
+    value, got = lax.optimization_barrier((value, got))
+    return value, (rows, got)
 
 
 def body(queries, span_keys, span_values, cache_keys, cache_values, out_proj, out_grad, doc_ids):
     n = lax.axis_size("dp")
     t = lax.axis_size("tensor")
     mine = lax.axis_index("dp")
-    shard = lax.axis_index("tensor")
+    shard = lax.axis_index("tensor").astype(jnp.int32).reshape(1)
     me = mine.astype(jnp.int32).reshape(1)
+    out_grad, me, shard = lax.optimization_barrier((out_grad, me, shard))
     length = queries.shape[0]
     kv = cache_keys.shape[1] // HD
     group = queries.shape[1] // HD // kv
-    share = cache_keys.shape[0] // n
-    orders = bit_orders(n, kv)
+    base, other = bit_orders(n)
 
     flips = [2 * s for s in range(1, t // 2)]
     far = [exchange(out_grad, "tensor", t, flip) for flip in flips]
@@ -367,11 +405,11 @@
     places = jnp.arange(length)
     span_ok = (docs[None, :] == docs[:, None]) & (places[:, None] <= places[None, :])
     bias = jnp.where(span_ok, 0.0, -1e30).astype(F32)
+    acc = project_streamed(shard, out_proj, out_grad)
+    me, acc = lax.optimization_barrier((me, acc))
     probs, attended, att_t, held = forward(
-        me, queries, cache_keys, span_keys, cache_values, span_values, bias, out_proj, orders, n
+        me, queries, cache_keys, span_keys, cache_values, span_values, bias, out_proj, base, n
     )
-    shard = shard.astype(jnp.int32).reshape(1)
-    acc = project(shard, held, out_grad)
     acc = project(shard ^ 1, held, near, acc)
     far, acc = lax.optimization_barrier((far, acc))
     later = [exchange(got, "tensor", t, 1) for got in far]
@@ -380,25 +418,29 @@
     for flip, got in zip(flips, later):
         acc = project(shard ^ (flip + 1), held, got, acc, group if flip == flips[-1] else 0)
 
-    kernels = [functools.partial(value_grads, h, probs) for h in range(kv)]
-    kernels += [
-        lambda acc, h=h: key_grads(
-            h, me, probs, cache_values, acc, att_t, queries, orders[h], n
-        )
-        for h in range(kv)
-    ]
+    def values(h, acc, order):
+        return value_grads(h, probs, acc, (base, order), n)
+
+    def keys(h, acc, order):
+        return key_grads(h, me, probs, cache_values, acc, att_t, queries, (base, order), n)
+
+    kernels = [functools.partial(values, h) for h in range(kv)]
+    kernels += [functools.partial(keys, h) for h in range(kv)]
+    orders = ([base, other, other, base] if kv == 2 else [base] * len(kernels))
     parts = []
-    for at, kernel in enumerate(kernels):
-        grad = kernel(acc)
-        if at < len(kernels) - 1:
-            acc, grad = lax.optimization_barrier((acc, grad))
-        parts.append(first_halving(grad, orders[at % kv], n))
-    grads = [rest_halving(*part, orders[at % kv], n) for at, part in enumerate(parts)]
+    for at, (kernel, order) in enumerate(zip(kernels, orders)):
+        final = at == len(kernels) - 1
+        grad = kernel(acc, order)
+        if final:
+            grad, parts[0] = in_order(grad, parts[0])
+        parts.append(first_halving(grad, order, n))
+    for step in range(1, len(base)):
+        for at, order in enumerate(orders):
+            parts[at] = next_halving(parts[at], order[step], n)
+    grads = parts[kv:] + parts[:kv]
     grad_k, grad_v, sums = squares(grads, n * t)
     sums = lax.all_to_all(sums, ("dp", "tensor"), split_axis=0, concat_axis=0, tiled=True)
-    own_keys = lax.dynamic_slice_in_dim(cache_keys, mine * share, share, 0)
-    own_vals = lax.dynamic_slice_in_dim(cache_values, mine * share, share, 0)
-    new_keys, new_values = update(sums, own_keys, own_vals, grad_k, grad_v)
+    new_keys, new_values = update(me, sums, cache_keys, cache_values, grad_k, grad_v)
     return (attended, new_keys, new_values)
 
 

time: 85.2 us -> 79.8 us (0.937)
  blocking collectives: 0 us -> 12.2 us
  waiting for transfers between devices: 22.1 us -> 12.7 us
  local copies, waits for them, and re-layouts: 7.27 us -> 1.42 us
  starting transfers between devices: 23.3 us -> 20.4 us
  Pallas kernels: 30.1 us -> 31.3 us
    all_to_all x0 -> x1, blocking collectives: none -> 12.2 us  [body(): lax.all_to_all(sums, ('dp', 'tensor'), split_axis=0, concat_axis=0, tiled...]
    all_to_all x1 -> x0, waiting for transfers between devices: 6.15 us -> none  [body(): lax.all_to_all(sums, ('dp', 'tensor'), split_axis=0, concat_axis=0, tiled...]
    unnamed x12 -> x14, local copies, waits for them, and re-layouts: 5.3 us -> 1.28 us
    pallas_call x6 -> x7, Pallas kernels: 23.9 us -> 27.2 us  [the longest x1 15.1 us: forward(): pl.pallas_call(functools.partial(forward_kernel, order, n), grid_spec=spe...]
    all_to_all x1 -> x0, starting transfers between devices: 3.22 us -> none  [body(): lax.all_to_all(sums, ('dp', 'tensor'), split_axis=0, concat_axis=0, tiled...]
    ppermute x15, waiting for transfers between devices: 15.9 us -> 12.7 us  [exchange(): return lax.ppermute(value, axis, [(i, i ^ flip) for i in range(size)])]
    dynamic_slice x2 -> x0, local copies, waits for them, and re-layouts: 1.83 us -> none  [the longest x1 0.92 us: body(): own_keys = lax.dynamic_slice_in_dim(cache_keys, mine * share, share, 0)]
    pallas_call x4 -> x3, Pallas kernels: 5.27 us -> 3.91 us  [project(): pl.pallas_call(functools.partial(project_kernel, acc is not None, heads),...]
  transfers between devices with their start and end apart: 16 -> 15, of which waited for: 9 -> 8; matrix products, arithmetic and copies ran while one was open for 4% -> 1% of each run, Pallas kernels for 23% -> 35%
where the time goes in v3:
time: 79.8 us; the launch traced here: 79.6 us
  Pallas kernels  31.3 us (39%)
  starting transfers between devices  20.4 us (26%)
  waiting for transfers between devices  12.7 us (16%)
  blocking collectives  12.2 us (15%)
  local copies, waits for them, and re-layouts  1.42 us (2%)
  between operations  0.94 us (1%)
    ppermute x15, starting transfers between devices, exchange(): return lax.ppermute(value, axis, [(i, i ^ flip) for i in range(size)])  20.4 us
    pallas_call x1, Pallas kernels, forward(): pl.pallas_call(functools.partial(forward_kernel, order, n), grid_spec=spe...  15.1 us
    ppermute x15, waiting for transfers between devices, exchange(): return lax.ppermute(value, axis, [(i, i ^ flip) for i in range(size)])  12.7 us
    all_to_all x1, blocking collectives, body(): lax.all_to_all(sums, ('dp', 'tensor'), split_axis=0, concat_axis=0, tiled...  12.2 us
    pallas_call x2, Pallas kernels, key_grads(): pl.pallas_call(functools.partial(keys_kernel, head, orders, n), in_specs=...  4.7 us
    pallas_call x1, Pallas kernels, project_streamed(): pl.pallas_call(streamed_kernel, grid_spec=pltpu.PrefetchScalarGridSpec(nu...  4.02 us
    pallas_call x3, Pallas kernels, project(): pl.pallas_call(functools.partial(project_kernel, acc is not None, heads),...  3.91 us
    pallas_call x2, Pallas kernels, value_grads(): pl.pallas_call(functools.partial(values_kernel, head, orders, n), in_spec...  2.49 us
  transfers between devices with their start and end apart: 15, of which 8 were waited for; matrix products, arithmetic and copies ran while one was open for 1% of the time, Pallas kernels for 35%

profile of v3, /device:TPU:0, one launch (start us, length us, event | category | flops | bytes accessed | tf_op | source)
XLA Modules:
  0.0 79.6 jit_solution(5542627404828590224)
XLA Ops:
  0.7 0.5 collective-permute-start.1
  1.2 2.6 %collective-permute-start = (bf16[256,2048]{1,0:T(8,128)(2,1)}, bf16[256,2048]{1,0:T(8,128)(2,1)S(1)}, u32[]{:S(2)}, u32[]{:S(2)}) collective-permute-start(bf16[256,2048]{1,0:T(8,128)(2,1)} %g_ref), channel_id=1, source_target_pairs={{0,2},{1,3},{2,0},{3,1},{4,6},{5,7},{6,4},{7,5},{8,10},{9,11},{10,... | collective-permute-start | bytes 3145736 | tf_op jit(solution)/shard_map/ppermute | solution.py:362
  3.8 1.3 %copy-done.3 = bf16[256,2048]{1,0:T(8,128)(2,1)S(1)} copy-done((bf16[256,2048]{1,0:T(8,128)(2,1)S(1)}, bf16[256,2048]{1,0:T(8,128)(2,1)}, u32[]{:S(2)}) %copy-start.3) | copy-done | bytes 1048600
  5.0 4.0 %project_streamed.1.refs_0_ = f32[1024,256]{1,0:T(8,128)S(1)} custom-call(s32[1]{0:T(128)} %bitcast.1.shard_ref, bf16[1024,8192]{1,0:T(8,128)(2,1)} %w_ref.3, bf16[256,2048]{1,0:T(8,128)(2,1)S(1)} %copy-done.3), custom_call_target="tpu_custom_call" | custom-call | flops 1073741824 | bytes 4194304 | tf_op jit(solution)/shard_map/project_streamed/pallas_call | solution.py:166
  9.1 0.1 fusion.1.bias_ref
  9.2 15.1 %forward.1 = (bf16[2,2048,1024]{2,1,0:T(8,128)(2,1)S(1)}, bf16[256,1024]{1,0:T(8,128)(2,1)}, bf16[2,128,1024]{2,1,0:T(8,128)(2,1)S(1)}, bf16[1024,8192]{1,0:T(8,128)(2,1)S(1)}) custom-call(s32[1]{0:T(128)} %bitcast.me_ref, bf16[256,1024]{1,0:T(8,128)(2,1)S(1)} %copy-done.1, bf16[2048,256]{1,0:T(8,128)(2,1)S(1)} %copy-done.2, bf16[256,256]{1,0:T(8,128)(2,1)S(1)} %copy-done.4, ...), custom_call_target="tpu_custom_call" | custom-call | flops 2415919104 | bytes 8388608 | tf_op jit(solution)/shard_map/forward/pallas_call | solution.py:139
  24.3 0.0 collective-permute-done.1.g_ref
  24.3 1.3 %project.3.refs_0_ = f32[1024,256]{1,0:T(8,128)S(1)} custom-call(s32[1]{0:T(128)S(6)} %xor.10.shard_ref, bf16[1024,8192]{1,0:T(8,128)(2,1)S(1)} %get-tuple-element.27.w_ref, bf16[256,2048]{1,0:T(8,128)(2,1)S(1)} %collective-permute-done.1.g_ref, f32[1024,256]{1,0:T(8,128)S(1)} %project_streamed.1.refs_0_), custom_call_target="tpu_custom_call" | custom-call | flops 1073741824 | bytes 4194304 | tf_op jit(solution)/shard_map/project/pallas_call | solution.py:216
  25.6 2.1 %collective-permute-done.g_ref = bf16[256,2048]{1,0:T(8,128)(2,1)S(1)} collective-permute-done((bf16[256,2048]{1,0:T(8,128)(2,1)}, bf16[256,2048]{1,0:T(8,128)(2,1)S(1)}, u32[]{:S(2)}, u32[]{:S(2)}) %collective-permute-start) | collective-permute-done | bytes 1048608 | tf_op jit(solution)/shard_map/ppermute | solution.py:362
  27.7 0.0 collective-permute-start.2
  27.7 1.3 %project.4.refs_0_ = f32[1024,256]{1,0:T(8,128)S(1)} custom-call(s32[1]{0:T(128)S(6)} %xor.11.shard_ref, bf16[1024,8192]{1,0:T(8,128)(2,1)S(1)} %get-tuple-element.27.w_ref, bf16[256,2048]{1,0:T(8,128)(2,1)S(1)} %collective-permute-done.g_ref, f32[1024,256]{1,0:T(8,128)S(1)} %project.3.refs_0_), custom_call_target="tpu_custom_call" | custom-call | flops 1073741824 | bytes 4194304 | tf_op jit(solution)/shard_map/project/pallas_call | solution.py:216
  29.1 1.3 %collective-permute-done.2.g_ref = bf16[256,2048]{1,0:T(8,128)(2,1)S(1)} collective-permute-done((bf16[256,2048]{1,0:T(8,128)(2,1)S(1)}, bf16[256,2048]{1,0:T(8,128)(2,1)S(1)}, u32[]{:S(2)}, u32[]{:S(2)}) %collective-permute-start.2) | collective-permute-done | bytes 1048608 | tf_op jit(solution)/shard_map/ppermute | solution.py:362
  30.4 1.3 %project.5.da_ref = bf16[2,128,1024]{2,1,0:T(8,128)(2,1)S(1)} custom-call(s32[1]{0:T(128)S(6)} %xor.9.shard_ref, bf16[1024,8192]{1,0:T(8,128)(2,1)S(1)} %get-tuple-element.27.w_ref, bf16[256,2048]{1,0:T(8,128)(2,1)S(1)} %collective-permute-done.2.g_ref, f32[1024,256]{1,0:T(8,128)S(1)} %project.4.refs_0_), custom_call_target="tpu_custom_call" | custom-call | flops 1073741824 | bytes 4194304 | tf_op jit(solution)/shard_map/project/pallas_call | solution.py:216
  31.7 1.3 %value_grads.3 = bf16[2048,128]{1,0:T(8,128)(2,1)S(1)} custom-call(bf16[2,2048,1024]{2,1,0:T(8,128)(2,1)S(1)} %get-tuple-element.26.p_ref, bf16[2,128,1024]{2,1,0:T(8,128)(2,1)S(1)} %project.5.da_ref), custom_call_target="tpu_custom_call" | custom-call | flops 4194304 | bytes 524288 | tf_op jit(solution)/shard_map/value_grads/pallas_call | solution.py:248
  33.0 1.9 %collective-permute-start.12 = (bf16[1024,128]{1,0:T(8,128)(2,1)S(1)}, bf16[1024,128]{1,0:T(8,128)(2,1)S(1)}, u32[]{:S(2)}, u32[]{:S(2)}) collective-permute-start(bf16[1024,128]{1,0:T(8,128)(2,1)S(1)} %slice.94), channel_id=1, source_target_pairs={{0,8},{4,12},{8,0},{12,4},{16,24},{20,28},{24,16},{28,20},{1,9},{5... | collective-permute-start | bytes 786440 | tf_op jit(solution)/shard_map/ppermute | solution.py:362
  34.9 1.2 %value_grads.2 = bf16[2048,128]{1,0:T(8,128)(2,1)S(1)} custom-call(bf16[2,2048,1024]{2,1,0:T(8,128)(2,1)S(1)} %get-tuple-element.26.p_ref, bf16[2,128,1024]{2,1,0:T(8,128)(2,1)S(1)} %project.5.da_ref), custom_call_target="tpu_custom_call" | custom-call | flops 4194304 | bytes 524288 | tf_op jit(solution)/shard_map/value_grads/pallas_call | solution.py:248
  36.1 1.6 %collective-permute-start.6 = (bf16[1024,128]{1,0:T(8,128)(2,1)S(1)}, bf16[1024,128]{1,0:T(8,128)(2,1)S(1)}, u32[]{:S(2)}, u32[]{:S(2)}) collective-permute-start(bf16[1024,128]{1,0:T(8,128)(2,1)S(1)} %slice.85), channel_id=1, source_target_pairs={{0,4},{4,0},{8,12},{12,8},{16,20},{20,16},{24,28},{28,24},{1,5},{5... | collective-permute-start | bytes 786440 | tf_op jit(solution)/shard_map/ppermute | solution.py:362
  37.7 2.4 %key_grads.2 = bf16[2048,128]{1,0:T(8,128)(2,1)S(1)} custom-call(s32[1]{0:T(128)} %bitcast.me_ref, bf16[2,2048,1024]{2,1,0:T(8,128)(2,1)S(1)} %get-tuple-element.26.p_ref, bf16[2048,256]{1,0:T(8,128)(2,1)S(1)} %copy-done, bf16[2,128,1024]{2,1,0:T(8,128)(2,1)S(1)} %project.5.da_ref, bf16[2,128,1024]{2,1,0:T(8,128)(2,1)S(1)} %get-tuple-element.31.att_ref, ...), custom_call_target="tpu_custom_call" | custom-call | flops 8388608 | bytes 524288 | tf_op jit(solution)/shard_map/key_grads/pallas_call | solution.py:286
  40.1 0.5 collective-permute-start.3
  40.6 2.3 %key_grads.3 = bf16[2048,128]{1,0:T(8,128)(2,1)S(1)} custom-call(s32[1]{0:T(128)} %bitcast.me_ref, bf16[2,2048,1024]{2,1,0:T(8,128)(2,1)S(1)} %get-tuple-element.26.p_ref, bf16[2048,256]{1,0:T(8,128)(2,1)S(1)} %copy-done, bf16[2,128,1024]{2,1,0:T(8,128)(2,1)S(1)} %project.5.da_ref, bf16[2,128,1024]{2,1,0:T(8,128)(2,1)S(1)} %get-tuple-element.31.att_ref, ...), custom_call_target="tpu_custom_call" | custom-call | flops 8388608 | bytes 524288 | tf_op jit(solution)/shard_map/key_grads/pallas_call | solution.py:286
  43.0 0.0 collective-permute-done.12
  43.0 0.1 add_convert_fusion
  43.1 0.4 collective-permute-start.13
  43.5 0.8 collective-permute-done.6
  44.3 0.1 add_convert_fusion.1
  44.4 1.5 %collective-permute-start.10 = (bf16[512,128]{1,0:T(8,128)(2,1)S(1)}, bf16[512,128]{1,0:T(8,128)(2,1)S(1)}, u32[]{:S(2)}, u32[]{:S(2)}) collective-permute-start(bf16[512,128]{1,0:T(8,128)(2,1)S(1)} %slice.91), channel_id=1, source_target_pairs={{0,8},{4,12},{8,0},{12,4},{16,24},{20,28},{24,16},{28,20},{1,9},{5... | collective-permute-start | bytes 393224 | tf_op jit(solution)/shard_map/ppermute | solution.py:362
  45.9 1.1 %collective-permute-start.7 = (bf16[1024,128]{1,0:T(8,128)(2,1)S(1)}, bf16[1024,128]{1,0:T(8,128)(2,1)S(1)}, u32[]{:S(2)}, u32[]{:S(2)}) collective-permute-start(bf16[1024,128]{1,0:T(8,128)(2,1)S(1)} %slice.67), channel_id=1, source_target_pairs={{0,4},{4,0},{8,12},{12,8},{16,20},{20,16},{24,28},{28,24},{1,5},{5... | collective-permute-start | bytes 786440 | tf_op jit(solution)/shard_map/ppermute | solution.py:362
  47.0 2.4 %collective-permute-done.3 = bf16[1024,128]{1,0:T(8,128)(2,1)S(1)} collective-permute-done((bf16[1024,128]{1,0:T(8,128)(2,1)S(1)}, bf16[1024,128]{1,0:T(8,128)(2,1)S(1)}, u32[]{:S(2)}, u32[]{:S(2)}) %collective-permute-start.3) | collective-permute-done | bytes 262176 | tf_op jit(solution)/shard_map/ppermute | solution.py:362
  49.3 0.1 add_convert_fusion.3
  49.4 0.6 collective-permute-start.4
  50.1 0.0 collective-permute-done.13
  50.1 2.7 %collective-permute-start.14 = (bf16[256,128]{1,0:T(8,128)(2,1)S(1)}, bf16[256,128]{1,0:T(8,128)(2,1)S(1)}, u32[]{:S(2)}, u32[]{:S(2)}) collective-permute-start(bf16[256,128]{1,0:T(8,128)(2,1)S(1)} %slice.97), channel_id=1, source_target_pairs={{0,16},{4,20},{8,24},{12,28},{16,0},{20,4},{24,8},{28,12},{1,17},{... | collective-permute-start | bytes 196616 | tf_op jit(solution)/shard_map/ppermute | solution.py:362
  52.8 0.0 collective-permute-done.10
  52.8 0.7 collective-permute-start.11
  53.5 1.6 %collective-permute-done.7 = bf16[1024,128]{1,0:T(8,128)(2,1)S(1)} collective-permute-done((bf16[1024,128]{1,0:T(8,128)(2,1)S(1)}, bf16[1024,128]{1,0:T(8,128)(2,1)S(1)}, u32[]{:S(2)}, u32[]{:S(2)}) %collective-permute-start.7) | collective-permute-done | bytes 262176 | tf_op jit(solution)/shard_map/ppermute | solution.py:362
  55.1 0.1 add_convert_fusion.2
  55.2 1.4 %collective-permute-start.8 = (bf16[512,128]{1,0:T(8,128)(2,1)S(1)}, bf16[512,128]{1,0:T(8,128)(2,1)S(1)}, u32[]{:S(2)}, u32[]{:S(2)}) collective-permute-start(bf16[512,128]{1,0:T(8,128)(2,1)S(1)} %slice.87), channel_id=1, source_target_pairs={{0,8},{4,12},{8,0},{12,4},{16,24},{20,28},{24,16},{28,20},{1,9},{5... | collective-permute-start | bytes 393224 | tf_op jit(solution)/shard_map/ppermute | solution.py:362
  56.6 0.0 collective-permute-done.4
  56.6 2.6 %collective-permute-start.5 = (bf16[256,128]{1,0:T(8,128)(2,1)S(1)}, bf16[256,128]{1,0:T(8,128)(2,1)S(1)}, u32[]{:S(2)}, u32[]{:S(2)}) collective-permute-start(bf16[256,128]{1,0:T(8,128)(2,1)S(1)} %slice.84), channel_id=1, source_target_pairs={{0,16},{4,20},{8,24},{12,28},{16,0},{20,4},{24,8},{28,12},{1,17},{... | collective-permute-start | bytes 196616 | tf_op jit(solution)/shard_map/ppermute | solution.py:362
  59.3 1.6 %collective-permute-done.8 = bf16[512,128]{1,0:T(8,128)(2,1)S(1)} collective-permute-done((bf16[512,128]{1,0:T(8,128)(2,1)S(1)}, bf16[512,128]{1,0:T(8,128)(2,1)S(1)}, u32[]{:S(2)}, u32[]{:S(2)}) %collective-permute-start.8) | collective-permute-done | bytes 131104 | tf_op jit(solution)/shard_map/ppermute | solution.py:362
  61.0 2.3 %collective-permute-start.9 = (bf16[256,128]{1,0:T(8,128)(2,1)S(1)}, bf16[256,128]{1,0:T(8,128)(2,1)S(1)}, u32[]{:S(2)}, u32[]{:S(2)}) collective-permute-start(bf16[256,128]{1,0:T(8,128)(2,1)S(1)} %slice.88), channel_id=1, source_target_pairs={{0,16},{4,20},{8,24},{12,28},{16,0},{20,4},{24,8},{28,12},{1,17},{... | collective-permute-start | bytes 196616 | tf_op jit(solution)/shard_map/ppermute | solution.py:362
  63.3 0.0 collective-permute-done.14.refs_7_
  63.3 0.0 collective-permute-done.11.refs_5_
  63.3 0.7 collective-permute-done.5.refs_1_
  63.9 2.3 %collective-permute-done.9.refs_3_ = bf16[256,128]{1,0:T(8,128)(2,1)S(1)} collective-permute-done((bf16[256,128]{1,0:T(8,128)(2,1)S(1)}, bf16[256,128]{1,0:T(8,128)(2,1)S(1)}, u32[]{:S(2)}, u32[]{:S(2)}) %collective-permute-start.9) | collective-permute-done | bytes 65568 | tf_op jit(solution)/shard_map/ppermute | solution.py:362
  66.2 0.2 squares.1
  66.5 12.2 %all_to_all.11 = f32[32,1,128]{2,1,0:T(1,128)S(1)} all-to-all(f32[32,1,128]{2,1,0:T(1,128)S(1)} %bitcast.8), channel_id=1, replica_groups=mesh['dp'=8,'tensor'=4] {'dp','tensor'}, dimensions={0} | all-to-all | bytes 32768 | tf_op jit(solution)/shard_map/all_to_all | solution.py:442
  78.7 0.9 %update.1 = (f32[256,256]{1,0:T(8,128)}, f32[256,256]{1,0:T(8,128)}) custom-call(s32[1]{0:T(128)} %bitcast.me_ref, f32[32,128]{1,0:T(8,128)S(1)} %bitcast.7, bf16[2048,256]{1,0:T(8,128)(2,1)S(1)} %copy-done.2, bf16[2048,256]{1,0:T(8,128)(2,1)S(1)} %copy-done, f32[256,256]{1,0:T(8,128)S(1)} %get-tuple-element.35.grad_k_ref, ...), custom_call_target="tpu_custom_call" | custom-call | flops 262144 | bytes 1310720 | tf_op jit(solution)/shard_map/update/pallas_call | solution.py:344
  (29 shorter events, 0.3 us)
Async XLA Ops:
  0.6 8.6 %copy-start.2 = (bf16[2048,256]{1,0:T(8,128)(2,1)S(1)}, bf16[2048,256]{1,0:T(8,128)(2,1)}, u32[]{:S(2)}) copy-start(bf16[2048,256]{1,0:T(8,128)(2,1)} %keys_ref.1) | copy-start | bytes 3145732
  0.6 8.6 %copy-start = (bf16[2048,256]{1,0:T(8,128)(2,1)S(1)}, bf16[2048,256]{1,0:T(8,128)(2,1)}, u32[]{:S(2)}) copy-start(bf16[2048,256]{1,0:T(8,128)(2,1)} %vals_ref.1) | copy-start | bytes 3145732
  0.7 8.6 %copy-start.1 = (bf16[256,1024]{1,0:T(8,128)(2,1)S(1)}, bf16[256,1024]{1,0:T(8,128)(2,1)}, u32[]{:S(2)}) copy-start(bf16[256,1024]{1,0:T(8,128)(2,1)} %q_ref.5) | copy-start | bytes 1572868
  0.7 23.7 %collective-permute-start.1 = (bf16[256,2048]{1,0:T(8,128)(2,1)}, bf16[256,2048]{1,0:T(8,128)(2,1)S(1)}, u32[]{:S(2)}, u32[]{:S(2)}) collective-permute-start(bf16[256,2048]{1,0:T(8,128)(2,1)} %g_ref), channel_id=1, source_target_pairs={{0,1},{1,0},{2,3},{3,2},{4,5},{5,4},{6,7},{7,6},{8,9},{9,8},{10,11... | collective-permute-start | bytes 3145736 | tf_op jit(solution)/shard_map/ppermute | solution.py:362
  1.2 26.6 %collective-permute-start = (bf16[256,2048]{1,0:T(8,128)(2,1)}, bf16[256,2048]{1,0:T(8,128)(2,1)S(1)}, u32[]{:S(2)}, u32[]{:S(2)}) collective-permute-start(bf16[256,2048]{1,0:T(8,128)(2,1)} %g_ref), channel_id=1, source_target_pairs={{0,2},{1,3},{2,0},{3,1},{4,6},{5,7},{6,4},{7,5},{8,10},{9,11},{10,... | collective-permute-start | bytes 3145736 | tf_op jit(solution)/shard_map/ppermute | solution.py:362
  3.8 1.3 %copy-start.3 = (bf16[256,2048]{1,0:T(8,128)(2,1)S(1)}, bf16[256,2048]{1,0:T(8,128)(2,1)}, u32[]{:S(2)}) copy-start(bf16[256,2048]{1,0:T(8,128)(2,1)} %g_ref) | copy-start | bytes 3145732
  5.0 4.0 %copy-start.6 = (s32[1,256]{1,0:T(1,128)S(1)}, s32[1,256]{1,0:T(1,128)}, u32[]{:S(2)}) copy-start(s32[1,256]{1,0:T(1,128)} %param.15) | copy-start | bytes 3076
  5.0 4.2 %copy-start.4 = (bf16[256,256]{1,0:T(8,128)(2,1)S(1)}, bf16[256,256]{1,0:T(8,128)(2,1)}, u32[]{:S(2)}) copy-start(bf16[256,256]{1,0:T(8,128)(2,1)} %ks_ref.1) | copy-start | bytes 393220
  5.0 4.2 %copy-start.5 = (bf16[256,256]{1,0:T(8,128)(2,1)S(1)}, bf16[256,256]{1,0:T(8,128)(2,1)}, u32[]{:S(2)}) copy-start(bf16[256,256]{1,0:T(8,128)(2,1)} %vs_ref.1) | copy-start | bytes 393220
  27.7 2.7 %collective-permute-start.2 = (bf16[256,2048]{1,0:T(8,128)(2,1)S(1)}, bf16[256,2048]{1,0:T(8,128)(2,1)S(1)}, u32[]{:S(2)}, u32[]{:S(2)}) collective-permute-start(bf16[256,2048]{1,0:T(8,128)(2,1)S(1)} %collective-permute-done.g_ref), channel_id=1, source_target_pairs={{0,1},{1,0},{2,3},{3,2},{4,5},{5,4},{6,7},{7,6},{8,9},{9,8},{10,11... | collective-permute-start | bytes 3145736 | tf_op jit(solution)/shard_map/ppermute | solution.py:362
  33.0 10.0 %collective-permute-start.12 = (bf16[1024,128]{1,0:T(8,128)(2,1)S(1)}, bf16[1024,128]{1,0:T(8,128)(2,1)S(1)}, u32[]{:S(2)}, u32[]{:S(2)}) collective-permute-start(bf16[1024,128]{1,0:T(8,128)(2,1)S(1)} %slice.94), channel_id=1, source_target_pairs={{0,8},{4,12},{8,0},{12,4},{16,24},{20,28},{24,16},{28,20},{1,9},{5... | collective-permute-start | bytes 786440 | tf_op jit(solution)/shard_map/ppermute | solution.py:362
  36.1 8.1 %collective-permute-start.6 = (bf16[1024,128]{1,0:T(8,128)(2,1)S(1)}, bf16[1024,128]{1,0:T(8,128)(2,1)S(1)}, u32[]{:S(2)}, u32[]{:S(2)}) collective-permute-start(bf16[1024,128]{1,0:T(8,128)(2,1)S(1)} %slice.85), channel_id=1, source_target_pairs={{0,4},{4,0},{8,12},{12,8},{16,20},{20,16},{24,28},{28,24},{1,5},{5... | collective-permute-start | bytes 786440 | tf_op jit(solution)/shard_map/ppermute | solution.py:362
  40.1 9.3 %collective-permute-start.3 = (bf16[1024,128]{1,0:T(8,128)(2,1)S(1)}, bf16[1024,128]{1,0:T(8,128)(2,1)S(1)}, u32[]{:S(2)}, u32[]{:S(2)}) collective-permute-start(bf16[1024,128]{1,0:T(8,128)(2,1)S(1)} %slice.81), channel_id=1, source_target_pairs={{0,8},{4,12},{8,0},{12,4},{16,24},{20,28},{24,16},{28,20},{1,9},{5... | collective-permute-start | bytes 786440 | tf_op jit(solution)/shard_map/ppermute | solution.py:362
  43.1 7.0 %collective-permute-start.13 = (bf16[512,128]{1,0:T(8,128)(2,1)S(1)}, bf16[512,128]{1,0:T(8,128)(2,1)S(1)}, u32[]{:S(2)}, u32[]{:S(2)}) collective-permute-start(bf16[512,128]{1,0:T(8,128)(2,1)S(1)} %slice.96), channel_id=1, source_target_pairs={{0,4},{4,0},{8,12},{12,8},{16,20},{20,16},{24,28},{28,24},{1,5},{5... | collective-permute-start | bytes 393224 | tf_op jit(solution)/shard_map/ppermute | solution.py:362
  44.4 8.4 %collective-permute-start.10 = (bf16[512,128]{1,0:T(8,128)(2,1)S(1)}, bf16[512,128]{1,0:T(8,128)(2,1)S(1)}, u32[]{:S(2)}, u32[]{:S(2)}) collective-permute-start(bf16[512,128]{1,0:T(8,128)(2,1)S(1)} %slice.91), channel_id=1, source_target_pairs={{0,8},{4,12},{8,0},{12,4},{16,24},{20,28},{24,16},{28,20},{1,9},{5... | collective-permute-start | bytes 393224 | tf_op jit(solution)/shard_map/ppermute | solution.py:362
  45.9 9.3 %collective-permute-start.7 = (bf16[1024,128]{1,0:T(8,128)(2,1)S(1)}, bf16[1024,128]{1,0:T(8,128)(2,1)S(1)}, u32[]{:S(2)}, u32[]{:S(2)}) collective-permute-start(bf16[1024,128]{1,0:T(8,128)(2,1)S(1)} %slice.67), channel_id=1, source_target_pairs={{0,4},{4,0},{8,12},{12,8},{16,20},{20,16},{24,28},{28,24},{1,5},{5... | collective-permute-start | bytes 786440 | tf_op jit(solution)/shard_map/ppermute | solution.py:362
  49.4 7.2 %collective-permute-start.4 = (bf16[512,128]{1,0:T(8,128)(2,1)S(1)}, bf16[512,128]{1,0:T(8,128)(2,1)S(1)}, u32[]{:S(2)}, u32[]{:S(2)}) collective-permute-start(bf16[512,128]{1,0:T(8,128)(2,1)S(1)} %slice.83), channel_id=1, source_target_pairs={{0,4},{4,0},{8,12},{12,8},{16,20},{20,16},{24,28},{28,24},{1,5},{5... | collective-permute-start | bytes 393224 | tf_op jit(solution)/shard_map/ppermute | solution.py:362
  50.1 13.1 %collective-permute-start.14 = (bf16[256,128]{1,0:T(8,128)(2,1)S(1)}, bf16[256,128]{1,0:T(8,128)(2,1)S(1)}, u32[]{:S(2)}, u32[]{:S(2)}) collective-permute-start(bf16[256,128]{1,0:T(8,128)(2,1)S(1)} %slice.97), channel_id=1, source_target_pairs={{0,16},{4,20},{8,24},{12,28},{16,0},{20,4},{24,8},{28,12},{1,17},{... | collective-permute-start | bytes 196616 | tf_op jit(solution)/shard_map/ppermute | solution.py:362
  52.8 10.4 %collective-permute-start.11 = (bf16[256,128]{1,0:T(8,128)(2,1)S(1)}, bf16[256,128]{1,0:T(8,128)(2,1)S(1)}, u32[]{:S(2)}, u32[]{:S(2)}) collective-permute-start(bf16[256,128]{1,0:T(8,128)(2,1)S(1)} %slice.92), channel_id=1, source_target_pairs={{0,16},{4,20},{8,24},{12,28},{16,0},{20,4},{24,8},{28,12},{1,17},{... | collective-permute-start | bytes 196616 | tf_op jit(solution)/shard_map/ppermute | solution.py:362
  55.2 5.7 %collective-permute-start.8 = (bf16[512,128]{1,0:T(8,128)(2,1)S(1)}, bf16[512,128]{1,0:T(8,128)(2,1)S(1)}, u32[]{:S(2)}, u32[]{:S(2)}) collective-permute-start(bf16[512,128]{1,0:T(8,128)(2,1)S(1)} %slice.87), channel_id=1, source_target_pairs={{0,8},{4,12},{8,0},{12,4},{16,24},{20,28},{24,16},{28,20},{1,9},{5... | collective-permute-start | bytes 393224 | tf_op jit(solution)/shard_map/ppermute | solution.py:362
  56.6 7.3 %collective-permute-start.5 = (bf16[256,128]{1,0:T(8,128)(2,1)S(1)}, bf16[256,128]{1,0:T(8,128)(2,1)S(1)}, u32[]{:S(2)}, u32[]{:S(2)}) collective-permute-start(bf16[256,128]{1,0:T(8,128)(2,1)S(1)} %slice.84), channel_id=1, source_target_pairs={{0,16},{4,20},{8,24},{12,28},{16,0},{20,4},{24,8},{28,12},{1,17},{... | collective-permute-start | bytes 196616 | tf_op jit(solution)/shard_map/ppermute | solution.py:362
  61.0 5.2 %collective-permute-start.9 = (bf16[256,128]{1,0:T(8,128)(2,1)S(1)}, bf16[256,128]{1,0:T(8,128)(2,1)S(1)}, u32[]{:S(2)}, u32[]{:S(2)}) collective-permute-start(bf16[256,128]{1,0:T(8,128)(2,1)S(1)} %slice.88), channel_id=1, source_target_pairs={{0,16},{4,20},{8,24},{12,28},{16,0},{20,4},{24,8},{28,12},{1,17},{... | collective-permute-start | bytes 196616 | tf_op jit(solution)/shard_map/ppermute | solution.py:362

commit v4 on v3

--- a/solution.py
+++ b/solution.py
@@ -228,28 +228,30 @@
     )(*args)
 
 
-def row_pieces(slots, n, base, order):
+def row_pieces(slots, n, base, order, side):
     share = slots // n
     size = min(share, 256)
     for row in range(0, slots, size):
         away = block_at(row // share, base)
-        yield row, place_of(away, order) * share + row % share, size, away
-
-
-def values_kernel(head, orders, n, p_ref, da_ref, out_ref):
+        to = place_of(away, order) * share + row % share - side * (slots // 2)
+        if 0 <= to < slots // 2:
+            yield row, to, size, away
+
+
+def values_kernel(head, layout, n, p_ref, da_ref, out_ref):
     da = da_ref[head]
-    for row, to, size, _ in row_pieces(p_ref.shape[1], n, *orders):
+    for row, to, size, _ in row_pieces(p_ref.shape[1], n, *layout):
         out_ref[to : to + size, :] = mm(p_ref[head, row : row + size, :], da, NT).astype(BF16)
 
 
-def value_grads(head, probs, grad_att_t, orders, n):
+def value_grads(head, probs, grad_att_t, layout, n):
     _, slots, wide = probs.shape
     vmem = pl.BlockSpec(memory_space=pltpu.VMEM)
     return pl.pallas_call(
-        functools.partial(values_kernel, head, orders, n),
+        functools.partial(values_kernel, head, layout, n),
         in_specs=[vmem, vmem],
         out_specs=vmem,
-        out_shape=jax.ShapeDtypeStruct((slots, HD), BF16),
+        out_shape=jax.ShapeDtypeStruct((slots // 2, HD), BF16),
         compiler_params=pltpu.CompilerParams(vmem_limit_bytes=14 * MIB),
         cost_estimate=pl.CostEstimate(
             flops=2 * slots * wide, bytes_accessed=2 * slots * HD, transcendentals=0
@@ -258,7 +260,7 @@
     )(probs, grad_att_t)
 
 
-def keys_kernel(head, orders, n, me_ref, p_ref, v_ref, da_ref, att_ref, q_ref, out_ref):
+def keys_kernel(head, layout, n, me_ref, p_ref, v_ref, da_ref, att_ref, q_ref, out_ref):
     me = me_ref[0]
     slots = p_ref.shape[1]
     share = slots // n
@@ -270,7 +272,7 @@
     q = jnp.concatenate(
         [q_ref[:, first + j * HD : first + (j + 1) * HD] for j in range(group)], axis=0
     )
-    for row, to, size, away in row_pieces(slots, n, *orders):
+    for row, to, size, away in row_pieces(slots, n, *layout):
         start = pl.multiple_of((away ^ me) * share + row % share, size)
         values = v_ref[pl.ds(start, size), head * HD : (head + 1) * HD]
         grad_p = mm(values, da, NN)
@@ -280,14 +282,14 @@
         out_ref[to : to + size, :] = total.astype(BF16)
 
 
-def key_grads(head, me, probs, cache_v, grad_att_t, att_t, queries, orders, n):
+def key_grads(head, me, probs, cache_v, grad_att_t, att_t, queries, layout, n):
     _, slots, wide = probs.shape
     vmem = pl.BlockSpec(memory_space=pltpu.VMEM)
     return pl.pallas_call(
-        functools.partial(keys_kernel, head, orders, n),
+        functools.partial(keys_kernel, head, layout, n),
         in_specs=[pl.BlockSpec(memory_space=pltpu.SMEM)] + [vmem] * 5,
         out_specs=vmem,
-        out_shape=jax.ShapeDtypeStruct((slots, HD), BF16),
+        out_shape=jax.ShapeDtypeStruct((slots // 2, HD), BF16),
         compiler_params=pltpu.CompilerParams(vmem_limit_bytes=14 * MIB),
         cost_estimate=pl.CostEstimate(
             flops=4 * slots * wide, bytes_accessed=2 * slots * HD, transcendentals=0
@@ -360,12 +362,6 @@
 
 def exchange(value, axis, size, flip):
     return lax.ppermute(value, axis, [(i, i ^ flip) for i in range(size)])
-
-
-def first_halving(part, order, n):
-    if not order:
-        return part, jnp.zeros_like(part)
-    return part, exchange(part[part.shape[0] // 2 :], "dp", n, 1 << order[0])
 
 
 def next_halving(part, bit, n):
@@ -418,22 +414,26 @@
     for flip, got in zip(flips, later):
         acc = project(shard ^ (flip + 1), held, got, acc, group if flip == flips[-1] else 0)
 
-    def values(h, acc, order):
-        return value_grads(h, probs, acc, (base, order), n)
-
-    def keys(h, acc, order):
-        return key_grads(h, me, probs, cache_values, acc, att_t, queries, (base, order), n)
+    def values(h, acc, order, side):
+        return value_grads(h, probs, acc, (base, order, side), n)
+
+    def keys(h, acc, order, side):
+        return key_grads(h, me, probs, cache_values, acc, att_t, queries, (base, order, side), n)
 
     kernels = [functools.partial(values, h) for h in range(kv)]
     kernels += [functools.partial(keys, h) for h in range(kv)]
-    orders = ([base, other, other, base] if kv == 2 else [base] * len(kernels))
+    orders = [base, other, other, base] if kv == 2 else [base] * len(kernels)
+    got = []
+    for kernel, order in zip(kernels, orders):
+        sent = kernel(acc, order, 1)
+        acc, sent = lax.optimization_barrier((acc, sent))
+        got.append(exchange(sent, "dp", n, 1 << order[0]))
     parts = []
     for at, (kernel, order) in enumerate(zip(kernels, orders)):
-        final = at == len(kernels) - 1
-        grad = kernel(acc, order)
-        if final:
-            grad, parts[0] = in_order(grad, parts[0])
-        parts.append(first_halving(grad, order, n))
+        if at == 1:
+            acc, got[0] = lax.optimization_barrier((acc, got[0]))
+            parts[0] = (parts[0][0], got[0])
+        parts.append((kernel(acc, order, 0), got[at]))
     for step in range(1, len(base)):
         for at, order in enumerate(orders):
             parts[at] = next_halving(parts[at], order[step], n)

time: 79.8 us -> 78.1 us (0.979)
  starting transfers between devices: 20.4 us -> 18 us
  waiting for transfers between devices: 12.7 us -> 14.5 us
  blocking collectives: 12.2 us -> 10.6 us
    ppermute x15, starting transfers between devices: 20.4 us -> 18 us  [exchange(): return lax.ppermute(value, axis, [(i, i ^ flip) for i in range(size)])]
    ppermute x15, waiting for transfers between devices: 12.7 us -> 14.5 us  [exchange(): return lax.ppermute(value, axis, [(i, i ^ flip) for i in range(size)])]
    all_to_all x1, blocking collectives: 12.2 us -> 10.6 us  [body(): lax.all_to_all(sums, ('dp', 'tensor'), split_axis=0, concat_axis=0, tiled...]
    pallas_call x4 -> x8, Pallas kernels: 7.19 us -> 7.81 us  [the longest x4 5.02 us: key_grads(): pl.pallas_call(functools.partial(keys_kernel, head, layout, n), in_specs=...]
  transfers between devices with their start and end apart: 15 -> 15, of which waited for: 8 -> 9; matrix products, arithmetic and copies ran while one was open for 1% -> 1% of each run, Pallas kernels for 35% -> 37%
where the time goes in v4:
time: 78.1 us; the launch traced here: 77.9 us
  Pallas kernels  31.9 us (41%)
  starting transfers between devices  18 us (23%)
  waiting for transfers between devices  14.5 us (19%)
  blocking collectives  10.6 us (14%)
  local copies, waits for them, and re-layouts  1.35 us (2%)
  between operations  0.95 us (1%)
    ppermute x15, starting transfers between devices, exchange(): return lax.ppermute(value, axis, [(i, i ^ flip) for i in range(size)])  18 us
    pallas_call x1, Pallas kernels, forward(): pl.pallas_call(functools.partial(forward_kernel, order, n), grid_spec=spe...  15.1 us
    ppermute x15, waiting for transfers between devices, exchange(): return lax.ppermute(value, axis, [(i, i ^ flip) for i in range(size)])  14.5 us
    all_to_all x1, blocking collectives, body(): lax.all_to_all(sums, ('dp', 'tensor'), split_axis=0, concat_axis=0, tiled...  10.6 us
    pallas_call x4, Pallas kernels, key_grads(): pl.pallas_call(functools.partial(keys_kernel, head, layout, n), in_specs=...  5.02 us
    pallas_call x1, Pallas kernels, project_streamed(): pl.pallas_call(streamed_kernel, grid_spec=pltpu.PrefetchScalarGridSpec(nu...  4.02 us
    pallas_call x3, Pallas kernels, project(): pl.pallas_call(functools.partial(project_kernel, acc is not None, heads),...  3.89 us
    pallas_call x4, Pallas kernels, value_grads(): pl.pallas_call(functools.partial(values_kernel, head, layout, n), in_spec...  2.78 us
  transfers between devices with their start and end apart: 15, of which 9 were waited for; matrix products, arithmetic and copies ran while one was open for 1% of the time, Pallas kernels for 37%

profile of v4, /device:TPU:0, one launch (start us, length us, event | category | flops | bytes accessed | tf_op | source)
XLA Modules:
  0.0 77.9 jit_solution(2062490111699394800)
XLA Ops:
  0.7 0.5 collective-permute-start.1
  1.2 2.6 %collective-permute-start = (bf16[256,2048]{1,0:T(8,128)(2,1)}, bf16[256,2048]{1,0:T(8,128)(2,1)S(1)}, u32[]{:S(2)}, u32[]{:S(2)}) collective-permute-start(bf16[256,2048]{1,0:T(8,128)(2,1)} %g_ref), channel_id=1, source_target_pairs={{0,2},{1,3},{2,0},{3,1},{4,6},{5,7},{6,4},{7,5},{8,10},{9,11},{10,... | collective-permute-start | bytes 3145736 | tf_op jit(solution)/shard_map/ppermute | solution.py:364
  3.8 1.3 %copy-done.3 = bf16[256,2048]{1,0:T(8,128)(2,1)S(1)} copy-done((bf16[256,2048]{1,0:T(8,128)(2,1)S(1)}, bf16[256,2048]{1,0:T(8,128)(2,1)}, u32[]{:S(2)}) %copy-start.3) | copy-done | bytes 1048600
  5.0 4.0 %project_streamed.1.refs_0_ = f32[1024,256]{1,0:T(8,128)S(1)} custom-call(s32[1]{0:T(128)} %bitcast.1.shard_ref, bf16[1024,8192]{1,0:T(8,128)(2,1)} %w_ref.3, bf16[256,2048]{1,0:T(8,128)(2,1)S(1)} %copy-done.3), custom_call_target="tpu_custom_call" | custom-call | flops 1073741824 | bytes 4194304 | tf_op jit(solution)/shard_map/project_streamed/pallas_call | solution.py:166
  9.1 0.1 fusion.1.bias_ref
  9.2 15.1 %forward.1 = (bf16[2,2048,1024]{2,1,0:T(8,128)(2,1)S(1)}, bf16[256,1024]{1,0:T(8,128)(2,1)}, bf16[2,128,1024]{2,1,0:T(8,128)(2,1)S(1)}, bf16[1024,8192]{1,0:T(8,128)(2,1)S(1)}) custom-call(s32[1]{0:T(128)} %bitcast.me_ref, bf16[256,1024]{1,0:T(8,128)(2,1)S(1)} %copy-done.1, bf16[2048,256]{1,0:T(8,128)(2,1)S(1)} %copy-done.2, bf16[256,256]{1,0:T(8,128)(2,1)S(1)} %copy-done.4, ...), custom_call_target="tpu_custom_call" | custom-call | flops 2415919104 | bytes 8388608 | tf_op jit(solution)/shard_map/forward/pallas_call | solution.py:139
  24.3 0.0 collective-permute-done.1.g_ref
  24.3 1.3 %project.3.refs_0_ = f32[1024,256]{1,0:T(8,128)S(1)} custom-call(s32[1]{0:T(128)S(6)} %xor.10.shard_ref, bf16[1024,8192]{1,0:T(8,128)(2,1)S(1)} %get-tuple-element.35.w_ref, bf16[256,2048]{1,0:T(8,128)(2,1)S(1)} %collective-permute-done.1.g_ref, f32[1024,256]{1,0:T(8,128)S(1)} %project_streamed.1.refs_0_), custom_call_target="tpu_custom_call" | custom-call | flops 1073741824 | bytes 4194304 | tf_op jit(solution)/shard_map/project/pallas_call | solution.py:216
  25.6 2.1 %collective-permute-done.g_ref = bf16[256,2048]{1,0:T(8,128)(2,1)S(1)} collective-permute-done((bf16[256,2048]{1,0:T(8,128)(2,1)}, bf16[256,2048]{1,0:T(8,128)(2,1)S(1)}, u32[]{:S(2)}, u32[]{:S(2)}) %collective-permute-start) | collective-permute-done | bytes 1048608 | tf_op jit(solution)/shard_map/ppermute | solution.py:364
  27.7 1.3 %project.4.refs_0_ = f32[1024,256]{1,0:T(8,128)S(1)} custom-call(s32[1]{0:T(128)S(6)} %xor.11.shard_ref, bf16[1024,8192]{1,0:T(8,128)(2,1)S(1)} %get-tuple-element.35.w_ref, bf16[256,2048]{1,0:T(8,128)(2,1)S(1)} %collective-permute-done.g_ref, f32[1024,256]{1,0:T(8,128)S(1)} %project.3.refs_0_), custom_call_target="tpu_custom_call" | custom-call | flops 1073741824 | bytes 4194304 | tf_op jit(solution)/shard_map/project/pallas_call | solution.py:216
  29.1 1.3 %collective-permute-done.2.g_ref = bf16[256,2048]{1,0:T(8,128)(2,1)S(1)} collective-permute-done((bf16[256,2048]{1,0:T(8,128)(2,1)S(1)}, bf16[256,2048]{1,0:T(8,128)(2,1)S(1)}, u32[]{:S(2)}, u32[]{:S(2)}) %collective-permute-start.2) | collective-permute-done | bytes 1048608 | tf_op jit(solution)/shard_map/ppermute | solution.py:364
  30.4 1.3 %project.5.da_ref = bf16[2,128,1024]{2,1,0:T(8,128)(2,1)S(1)} custom-call(s32[1]{0:T(128)S(6)} %xor.9.shard_ref, bf16[1024,8192]{1,0:T(8,128)(2,1)S(1)} %get-tuple-element.35.w_ref, bf16[256,2048]{1,0:T(8,128)(2,1)S(1)} %collective-permute-done.2.g_ref, f32[1024,256]{1,0:T(8,128)S(1)} %project.4.refs_0_), custom_call_target="tpu_custom_call" | custom-call | flops 1073741824 | bytes 4194304 | tf_op jit(solution)/shard_map/project/pallas_call | solution.py:216
  31.7 0.7 value_grads.4
  32.4 1.8 %collective-permute-start.3 = (bf16[1024,128]{1,0:T(8,128)(2,1)S(1)}, bf16[1024,128]{1,0:T(8,128)(2,1)S(1)}, u32[]{:S(2)}, u32[]{:S(2)}) collective-permute-start(bf16[1024,128]{1,0:T(8,128)(2,1)S(1)} %value_grads.4), channel_id=1, source_target_pairs={{0,4},{4,0},{8,12},{12,8},{16,20},{20,16},{24,28},{28,24},{1,5},{5... | collective-permute-start | bytes 786440 | tf_op jit(solution)/shard_map/ppermute | solution.py:364
  34.2 0.7 value_grads.5
  34.9 1.6 %collective-permute-start.12 = (bf16[1024,128]{1,0:T(8,128)(2,1)S(1)}, bf16[1024,128]{1,0:T(8,128)(2,1)S(1)}, u32[]{:S(2)}, u32[]{:S(2)}) collective-permute-start(bf16[1024,128]{1,0:T(8,128)(2,1)S(1)} %value_grads.5), channel_id=1, source_target_pairs={{0,8},{4,12},{8,0},{12,4},{16,24},{20,28},{24,16},{28,20},{1,9},{5... | collective-permute-start | bytes 786440 | tf_op jit(solution)/shard_map/ppermute | solution.py:364
  36.5 1.3 %key_grads.4 = bf16[1024,128]{1,0:T(8,128)(2,1)S(1)} custom-call(s32[1]{0:T(128)} %bitcast.me_ref, bf16[2,2048,1024]{2,1,0:T(8,128)(2,1)S(1)} %get-tuple-element.34.p_ref, bf16[2048,256]{1,0:T(8,128)(2,1)S(1)} %copy-done, bf16[2,128,1024]{2,1,0:T(8,128)(2,1)S(1)} %project.5.da_ref, bf16[2,128,1024]{2,1,0:T(8,128)(2,1)S(1)} %get-tuple-element.41.att_ref, ...), custom_call_target="tpu_custom_call" | custom-call | flops 8388608 | bytes 524288 | tf_op jit(solution)/shard_map/key_grads/pallas_call | solution.py:288
  37.8 1.3 %key_grads.5 = bf16[1024,128]{1,0:T(8,128)(2,1)S(1)} custom-call(s32[1]{0:T(128)} %bitcast.me_ref, bf16[2,2048,1024]{2,1,0:T(8,128)(2,1)S(1)} %get-tuple-element.34.p_ref, bf16[2048,256]{1,0:T(8,128)(2,1)S(1)} %copy-done, bf16[2,128,1024]{2,1,0:T(8,128)(2,1)S(1)} %project.5.da_ref, bf16[2,128,1024]{2,1,0:T(8,128)(2,1)S(1)} %get-tuple-element.41.att_ref, ...), custom_call_target="tpu_custom_call" | custom-call | flops 8388608 | bytes 524288 | tf_op jit(solution)/shard_map/key_grads/pallas_call | solution.py:288
  39.1 0.6 collective-permute-start.7
  39.7 0.2 collective-permute-start.4
  39.9 0.7 value_grads.6
  40.6 0.2 collective-permute-done.3
  40.8 0.7 value_grads.7
  41.5 2.7 %collective-permute-done.12 = bf16[1024,128]{1,0:T(8,128)(2,1)S(1)} collective-permute-done((bf16[1024,128]{1,0:T(8,128)(2,1)S(1)}, bf16[1024,128]{1,0:T(8,128)(2,1)S(1)}, u32[]{:S(2)}, u32[]{:S(2)}) %collective-permute-start.12) | collective-permute-done | bytes 262176 | tf_op jit(solution)/shard_map/ppermute | solution.py:364
  44.2 0.1 add_convert_fusion
  44.3 0.1 collective-permute-start.13
  44.3 0.1 add_convert_fusion.1
  44.4 2.1 %collective-permute-start.10 = (bf16[512,128]{1,0:T(8,128)(2,1)S(1)}, bf16[512,128]{1,0:T(8,128)(2,1)S(1)}, u32[]{:S(2)}, u32[]{:S(2)}) collective-permute-start(bf16[512,128]{1,0:T(8,128)(2,1)S(1)} %slice.55), channel_id=1, source_target_pairs={{0,8},{4,12},{8,0},{12,4},{16,24},{20,28},{24,16},{28,20},{1,9},{5... | collective-permute-start | bytes 393224 | tf_op jit(solution)/shard_map/ppermute | solution.py:364
  46.6 1.3 %key_grads.7 = bf16[1024,128]{1,0:T(8,128)(2,1)S(1)} custom-call(s32[1]{0:T(128)} %bitcast.me_ref, bf16[2,2048,1024]{2,1,0:T(8,128)(2,1)S(1)} %get-tuple-element.34.p_ref, bf16[2048,256]{1,0:T(8,128)(2,1)S(1)} %copy-done, bf16[2,128,1024]{2,1,0:T(8,128)(2,1)S(1)} %project.5.da_ref, bf16[2,128,1024]{2,1,0:T(8,128)(2,1)S(1)} %get-tuple-element.41.att_ref, ...), custom_call_target="tpu_custom_call" | custom-call | flops 8388608 | bytes 524288 | tf_op jit(solution)/shard_map/key_grads/pallas_call | solution.py:288
  47.8 0.5 collective-permute-done.7
  48.3 0.1 add_convert_fusion.2
  48.4 0.8 %collective-permute-start.8 = (bf16[512,128]{1,0:T(8,128)(2,1)S(1)}, bf16[512,128]{1,0:T(8,128)(2,1)S(1)}, u32[]{:S(2)}, u32[]{:S(2)}) collective-permute-start(bf16[512,128]{1,0:T(8,128)(2,1)S(1)} %slice.52), channel_id=1, source_target_pairs={{0,8},{4,12},{8,0},{12,4},{16,24},{20,28},{24,16},{28,20},{1,9},{5... | collective-permute-start | bytes 393224 | tf_op jit(solution)/shard_map/ppermute | solution.py:364
  49.2 1.3 %key_grads.6 = bf16[1024,128]{1,0:T(8,128)(2,1)S(1)} custom-call(s32[1]{0:T(128)} %bitcast.me_ref, bf16[2,2048,1024]{2,1,0:T(8,128)(2,1)S(1)} %get-tuple-element.34.p_ref, bf16[2048,256]{1,0:T(8,128)(2,1)S(1)} %copy-done, bf16[2,128,1024]{2,1,0:T(8,128)(2,1)S(1)} %project.5.da_ref, bf16[2,128,1024]{2,1,0:T(8,128)(2,1)S(1)} %get-tuple-element.41.att_ref, ...), custom_call_target="tpu_custom_call" | custom-call | flops 8388608 | bytes 524288 | tf_op jit(solution)/shard_map/key_grads/pallas_call | solution.py:288
  50.5 0.0 collective-permute-done.4
  50.5 0.1 add_convert_fusion.3
  50.6 1.6 %collective-permute-start.5 = (bf16[512,128]{1,0:T(8,128)(2,1)S(1)}, bf16[512,128]{1,0:T(8,128)(2,1)S(1)}, u32[]{:S(2)}, u32[]{:S(2)}) collective-permute-start(bf16[512,128]{1,0:T(8,128)(2,1)S(1)} %slice.49), channel_id=1, source_target_pairs={{0,4},{4,0},{8,12},{12,8},{16,20},{20,16},{24,28},{28,24},{1,5},{5... | collective-permute-start | bytes 393224 | tf_op jit(solution)/shard_map/ppermute | solution.py:364
  52.2 2.7 %collective-permute-start.14 = (bf16[256,128]{1,0:T(8,128)(2,1)S(1)}, bf16[256,128]{1,0:T(8,128)(2,1)S(1)}, u32[]{:S(2)}, u32[]{:S(2)}) collective-permute-start(bf16[256,128]{1,0:T(8,128)(2,1)S(1)} %slice.59), channel_id=1, source_target_pairs={{0,16},{4,20},{8,24},{12,28},{16,0},{20,4},{24,8},{28,12},{1,17},{... | collective-permute-start | bytes 196616 | tf_op jit(solution)/shard_map/ppermute | solution.py:364
  54.9 0.0 collective-permute-done.10
  54.9 0.4 collective-permute-start.11
  55.4 2.7 %collective-permute-start.9 = (bf16[256,128]{1,0:T(8,128)(2,1)S(1)}, bf16[256,128]{1,0:T(8,128)(2,1)S(1)}, u32[]{:S(2)}, u32[]{:S(2)}) collective-permute-start(bf16[256,128]{1,0:T(8,128)(2,1)S(1)} %slice.53), channel_id=1, source_target_pairs={{0,16},{4,20},{8,24},{12,28},{16,0},{20,4},{24,8},{28,12},{1,17},{... | collective-permute-start | bytes 196616 | tf_op jit(solution)/shard_map/ppermute | solution.py:364
  58.2 0.3 collective-permute-start.6
  58.5 2.4 %collective-permute-done.14.refs_7_ = bf16[256,128]{1,0:T(8,128)(2,1)S(1)} collective-permute-done((bf16[256,128]{1,0:T(8,128)(2,1)S(1)}, bf16[256,128]{1,0:T(8,128)(2,1)S(1)}, u32[]{:S(2)}, u32[]{:S(2)}) %collective-permute-start.14) | collective-permute-done | bytes 65568 | tf_op jit(solution)/shard_map/ppermute | solution.py:364
  60.9 2.8 %collective-permute-done.11.refs_5_ = bf16[256,128]{1,0:T(8,128)(2,1)S(1)} collective-permute-done((bf16[256,128]{1,0:T(8,128)(2,1)S(1)}, bf16[256,128]{1,0:T(8,128)(2,1)S(1)}, u32[]{:S(2)}, u32[]{:S(2)}) %collective-permute-start.11) | collective-permute-done | bytes 65568 | tf_op jit(solution)/shard_map/ppermute | solution.py:364
  63.7 1.8 %collective-permute-done.9.refs_3_ = bf16[256,128]{1,0:T(8,128)(2,1)S(1)} collective-permute-done((bf16[256,128]{1,0:T(8,128)(2,1)S(1)}, bf16[256,128]{1,0:T(8,128)(2,1)S(1)}, u32[]{:S(2)}, u32[]{:S(2)}) %collective-permute-start.9) | collective-permute-done | bytes 65568 | tf_op jit(solution)/shard_map/ppermute | solution.py:364
  65.5 0.7 collective-permute-done.6.refs_1_
  66.2 0.2 squares.1
  66.4 10.6 %all_to_all.11 = f32[32,1,128]{2,1,0:T(1,128)S(1)} all-to-all(f32[32,1,128]{2,1,0:T(1,128)S(1)} %bitcast.8), channel_id=1, replica_groups=mesh['dp'=8,'tensor'=4] {'dp','tensor'}, dimensions={0} | all-to-all | bytes 32768 | tf_op jit(solution)/shard_map/all_to_all | solution.py:442
  77.0 0.9 %update.1 = (f32[256,256]{1,0:T(8,128)}, f32[256,256]{1,0:T(8,128)}) custom-call(s32[1]{0:T(128)} %bitcast.me_ref, f32[32,128]{1,0:T(8,128)S(1)} %bitcast.7, bf16[2048,256]{1,0:T(8,128)(2,1)S(1)} %copy-done.2, bf16[2048,256]{1,0:T(8,128)(2,1)S(1)} %copy-done, f32[256,256]{1,0:T(8,128)S(1)} %get-tuple-element.51.grad_k_ref, ...), custom_call_target="tpu_custom_call" | custom-call | flops 262144 | bytes 1310720 | tf_op jit(solution)/shard_map/update/pallas_call | solution.py:346
  (29 shorter events, 0.3 us)
Async XLA Ops:
  0.6 8.6 %copy-start.2 = (bf16[2048,256]{1,0:T(8,128)(2,1)S(1)}, bf16[2048,256]{1,0:T(8,128)(2,1)}, u32[]{:S(2)}) copy-start(bf16[2048,256]{1,0:T(8,128)(2,1)} %keys_ref.1) | copy-start | bytes 3145732
  0.6 8.6 %copy-start = (bf16[2048,256]{1,0:T(8,128)(2,1)S(1)}, bf16[2048,256]{1,0:T(8,128)(2,1)}, u32[]{:S(2)}) copy-start(bf16[2048,256]{1,0:T(8,128)(2,1)} %vals_ref.1) | copy-start | bytes 3145732
  0.7 8.6 %copy-start.1 = (bf16[256,1024]{1,0:T(8,128)(2,1)S(1)}, bf16[256,1024]{1,0:T(8,128)(2,1)}, u32[]{:S(2)}) copy-start(bf16[256,1024]{1,0:T(8,128)(2,1)} %q_ref.9) | copy-start | bytes 1572868
  0.7 23.7 %collective-permute-start.1 = (bf16[256,2048]{1,0:T(8,128)(2,1)}, bf16[256,2048]{1,0:T(8,128)(2,1)S(1)}, u32[]{:S(2)}, u32[]{:S(2)}) collective-permute-start(bf16[256,2048]{1,0:T(8,128)(2,1)} %g_ref), channel_id=1, source_target_pairs={{0,1},{1,0},{2,3},{3,2},{4,5},{5,4},{6,7},{7,6},{8,9},{9,8},{10,11... | collective-permute-start | bytes 3145736 | tf_op jit(solution)/shard_map/ppermute | solution.py:364
  1.2 26.6 %collective-permute-start = (bf16[256,2048]{1,0:T(8,128)(2,1)}, bf16[256,2048]{1,0:T(8,128)(2,1)S(1)}, u32[]{:S(2)}, u32[]{:S(2)}) collective-permute-start(bf16[256,2048]{1,0:T(8,128)(2,1)} %g_ref), channel_id=1, source_target_pairs={{0,2},{1,3},{2,0},{3,1},{4,6},{5,7},{6,4},{7,5},{8,10},{9,11},{10,... | collective-permute-start | bytes 3145736 | tf_op jit(solution)/shard_map/ppermute | solution.py:364
  3.8 1.3 %copy-start.3 = (bf16[256,2048]{1,0:T(8,128)(2,1)S(1)}, bf16[256,2048]{1,0:T(8,128)(2,1)}, u32[]{:S(2)}) copy-start(bf16[256,2048]{1,0:T(8,128)(2,1)} %g_ref) | copy-start | bytes 3145732
  5.0 4.0 %copy-start.6 = (s32[1,256]{1,0:T(1,128)S(1)}, s32[1,256]{1,0:T(1,128)}, u32[]{:S(2)}) copy-start(s32[1,256]{1,0:T(1,128)} %param.15) | copy-start | bytes 3076
  5.0 4.2 %copy-start.4 = (bf16[256,256]{1,0:T(8,128)(2,1)S(1)}, bf16[256,256]{1,0:T(8,128)(2,1)}, u32[]{:S(2)}) copy-start(bf16[256,256]{1,0:T(8,128)(2,1)} %ks_ref.1) | copy-start | bytes 393220
  5.0 4.2 %copy-start.5 = (bf16[256,256]{1,0:T(8,128)(2,1)S(1)}, bf16[256,256]{1,0:T(8,128)(2,1)}, u32[]{:S(2)}) copy-start(bf16[256,256]{1,0:T(8,128)(2,1)} %vs_ref.1) | copy-start | bytes 393220
  27.7 2.7 %collective-permute-start.2 = (bf16[256,2048]{1,0:T(8,128)(2,1)S(1)}, bf16[256,2048]{1,0:T(8,128)(2,1)S(1)}, u32[]{:S(2)}, u32[]{:S(2)}) collective-permute-start(bf16[256,2048]{1,0:T(8,128)(2,1)S(1)} %collective-permute-done.g_ref), channel_id=1, source_target_pairs={{0,1},{1,0},{2,3},{3,2},{4,5},{5,4},{6,7},{7,6},{8,9},{9,8},{10,11... | collective-permute-start | bytes 3145736 | tf_op jit(solution)/shard_map/ppermute | solution.py:364
  32.4 8.4 %collective-permute-start.3 = (bf16[1024,128]{1,0:T(8,128)(2,1)S(1)}, bf16[1024,128]{1,0:T(8,128)(2,1)S(1)}, u32[]{:S(2)}, u32[]{:S(2)}) collective-permute-start(bf16[1024,128]{1,0:T(8,128)(2,1)S(1)} %value_grads.4), channel_id=1, source_target_pairs={{0,4},{4,0},{8,12},{12,8},{16,20},{20,16},{24,28},{28,24},{1,5},{5... | collective-permute-start | bytes 786440 | tf_op jit(solution)/shard_map/ppermute | solution.py:364
  34.9 9.3 %collective-permute-start.12 = (bf16[1024,128]{1,0:T(8,128)(2,1)S(1)}, bf16[1024,128]{1,0:T(8,128)(2,1)S(1)}, u32[]{:S(2)}, u32[]{:S(2)}) collective-permute-start(bf16[1024,128]{1,0:T(8,128)(2,1)S(1)} %value_grads.5), channel_id=1, source_target_pairs={{0,8},{4,12},{8,0},{12,4},{16,24},{20,28},{24,16},{28,20},{1,9},{5... | collective-permute-start | bytes 786440 | tf_op jit(solution)/shard_map/ppermute | solution.py:364
  39.1 9.2 %collective-permute-start.7 = (bf16[1024,128]{1,0:T(8,128)(2,1)S(1)}, bf16[1024,128]{1,0:T(8,128)(2,1)S(1)}, u32[]{:S(2)}, u32[]{:S(2)}) collective-permute-start(bf16[1024,128]{1,0:T(8,128)(2,1)S(1)} %key_grads.5), channel_id=1, source_target_pairs={{0,4},{4,0},{8,12},{12,8},{16,20},{20,16},{24,28},{28,24},{1,5},{5... | collective-permute-start | bytes 786440 | tf_op jit(solution)/shard_map/ppermute | solution.py:364
  39.7 10.8 %collective-permute-start.4 = (bf16[1024,128]{1,0:T(8,128)(2,1)S(1)}, bf16[1024,128]{1,0:T(8,128)(2,1)S(1)}, u32[]{:S(2)}, u32[]{:S(2)}) collective-permute-start(bf16[1024,128]{1,0:T(8,128)(2,1)S(1)} %key_grads.4), channel_id=1, source_target_pairs={{0,8},{4,12},{8,0},{12,4},{16,24},{20,28},{24,16},{28,20},{1,9},{5... | collective-permute-start | bytes 786440 | tf_op jit(solution)/shard_map/ppermute | solution.py:364
  44.3 7.9 %collective-permute-start.13 = (bf16[512,128]{1,0:T(8,128)(2,1)S(1)}, bf16[512,128]{1,0:T(8,128)(2,1)S(1)}, u32[]{:S(2)}, u32[]{:S(2)}) collective-permute-start(bf16[512,128]{1,0:T(8,128)(2,1)S(1)} %slice.58), channel_id=1, source_target_pairs={{0,4},{4,0},{8,12},{12,8},{16,20},{20,16},{24,28},{28,24},{1,5},{5... | collective-permute-start | bytes 393224 | tf_op jit(solution)/shard_map/ppermute | solution.py:364
  44.4 10.4 %collective-permute-start.10 = (bf16[512,128]{1,0:T(8,128)(2,1)S(1)}, bf16[512,128]{1,0:T(8,128)(2,1)S(1)}, u32[]{:S(2)}, u32[]{:S(2)}) collective-permute-start(bf16[512,128]{1,0:T(8,128)(2,1)S(1)} %slice.55), channel_id=1, source_target_pairs={{0,8},{4,12},{8,0},{12,4},{16,24},{20,28},{24,16},{28,20},{1,9},{5... | collective-permute-start | bytes 393224 | tf_op jit(solution)/shard_map/ppermute | solution.py:364
  48.4 6.9 %collective-permute-start.8 = (bf16[512,128]{1,0:T(8,128)(2,1)S(1)}, bf16[512,128]{1,0:T(8,128)(2,1)S(1)}, u32[]{:S(2)}, u32[]{:S(2)}) collective-permute-start(bf16[512,128]{1,0:T(8,128)(2,1)S(1)} %slice.52), channel_id=1, source_target_pairs={{0,8},{4,12},{8,0},{12,4},{16,24},{20,28},{24,16},{28,20},{1,9},{5... | collective-permute-start | bytes 393224 | tf_op jit(solution)/shard_map/ppermute | solution.py:364
  50.6 7.5 %collective-permute-start.5 = (bf16[512,128]{1,0:T(8,128)(2,1)S(1)}, bf16[512,128]{1,0:T(8,128)(2,1)S(1)}, u32[]{:S(2)}, u32[]{:S(2)}) collective-permute-start(bf16[512,128]{1,0:T(8,128)(2,1)S(1)} %slice.49), channel_id=1, source_target_pairs={{0,4},{4,0},{8,12},{12,8},{16,20},{20,16},{24,28},{28,24},{1,5},{5... | collective-permute-start | bytes 393224 | tf_op jit(solution)/shard_map/ppermute | solution.py:364
  52.2 8.6 %collective-permute-start.14 = (bf16[256,128]{1,0:T(8,128)(2,1)S(1)}, bf16[256,128]{1,0:T(8,128)(2,1)S(1)}, u32[]{:S(2)}, u32[]{:S(2)}) collective-permute-start(bf16[256,128]{1,0:T(8,128)(2,1)S(1)} %slice.59), channel_id=1, source_target_pairs={{0,16},{4,20},{8,24},{12,28},{16,0},{20,4},{24,8},{28,12},{1,17},{... | collective-permute-start | bytes 196616 | tf_op jit(solution)/shard_map/ppermute | solution.py:364
  54.9 8.8 %collective-permute-start.11 = (bf16[256,128]{1,0:T(8,128)(2,1)S(1)}, bf16[256,128]{1,0:T(8,128)(2,1)S(1)}, u32[]{:S(2)}, u32[]{:S(2)}) collective-permute-start(bf16[256,128]{1,0:T(8,128)(2,1)S(1)} %slice.56), channel_id=1, source_target_pairs={{0,16},{4,20},{8,24},{12,28},{16,0},{20,4},{24,8},{28,12},{1,17},{... | collective-permute-start | bytes 196616 | tf_op jit(solution)/shard_map/ppermute | solution.py:364
  55.4 10.1 %collective-permute-start.9 = (bf16[256,128]{1,0:T(8,128)(2,1)S(1)}, bf16[256,128]{1,0:T(8,128)(2,1)S(1)}, u32[]{:S(2)}, u32[]{:S(2)}) collective-permute-start(bf16[256,128]{1,0:T(8,128)(2,1)S(1)} %slice.53), channel_id=1, source_target_pairs={{0,16},{4,20},{8,24},{12,28},{16,0},{20,4},{24,8},{28,12},{1,17},{... | collective-permute-start | bytes 196616 | tf_op jit(solution)/shard_map/ppermute | solution.py:364
  58.2 8.0 %collective-permute-start.6 = (bf16[256,128]{1,0:T(8,128)(2,1)S(1)}, bf16[256,128]{1,0:T(8,128)(2,1)S(1)}, u32[]{:S(2)}, u32[]{:S(2)}) collective-permute-start(bf16[256,128]{1,0:T(8,128)(2,1)S(1)} %slice.50), channel_id=1, source_target_pairs={{0,16},{4,20},{8,24},{12,28},{16,0},{20,4},{24,8},{28,12},{1,17},{... | collective-permute-start | bytes 196616 | tf_op jit(solution)/shard_map/ppermute | solution.py:364

commit v5 on v4

--- a/solution.py
+++ b/solution.py
@@ -29,7 +29,7 @@
 
 def bit_orders(n):
     first = list(range(n.bit_length() - 1))
-    return first, first[1::-1] + first[2:]
+    return first, first[1::-1] + first[2:], first[:1] + first[2:0:-1] + first[3:]
 
 
 def place_of(rel, order):
@@ -391,7 +391,7 @@
     length = queries.shape[0]
     kv = cache_keys.shape[1] // HD
     group = queries.shape[1] // HD // kv
-    base, other = bit_orders(n)
+    base, other, third = bit_orders(n)
 
     flips = [2 * s for s in range(1, t // 2)]
     far = [exchange(out_grad, "tensor", t, flip) for flip in flips]
@@ -422,7 +422,7 @@
 
     kernels = [functools.partial(values, h) for h in range(kv)]
     kernels += [functools.partial(keys, h) for h in range(kv)]
-    orders = [base, other, other, base] if kv == 2 else [base] * len(kernels)
+    orders = [third, other, other, base] if kv == 2 else [base] * len(kernels)
     got = []
     for kernel, order in zip(kernels, orders):
         sent = kernel(acc, order, 1)

time: 78.1 us -> 76.9 us (0.985)
  waiting for transfers between devices: 14.5 us -> 10.7 us
  starting transfers between devices: 18 us -> 19.5 us
  blocking collectives: 10.6 us -> 11.7 us
    ppermute x15, waiting for transfers between devices: 14.5 us -> 10.7 us  [exchange(): return lax.ppermute(value, axis, [(i, i ^ flip) for i in range(size)])]
    ppermute x15, starting transfers between devices: 18 us -> 19.5 us  [exchange(): return lax.ppermute(value, axis, [(i, i ^ flip) for i in range(size)])]
    all_to_all x1, blocking collectives: 10.6 us -> 11.7 us  [body(): lax.all_to_all(sums, ('dp', 'tensor'), split_axis=0, concat_axis=0, tiled...]
  transfers between devices with their start and end apart: 15 -> 15, of which waited for: 9 -> 8; matrix products, arithmetic and copies ran while one was open for 1% -> 1% of each run, Pallas kernels for 37% -> 38%
where the time goes in v5:
time: 76.9 us; the launch traced here: 76.7 us
  Pallas kernels  31.9 us (41%)
  starting transfers between devices  19.5 us (25%)
  blocking collectives  11.7 us (15%)
  waiting for transfers between devices  10.7 us (14%)
  local copies, waits for them, and re-layouts  1.35 us (2%)
  between operations  0.95 us (1%)
    ppermute x15, starting transfers between devices, exchange(): return lax.ppermute(value, axis, [(i, i ^ flip) for i in range(size)])  19.5 us
    pallas_call x1, Pallas kernels, forward(): pl.pallas_call(functools.partial(forward_kernel, order, n), grid_spec=spe...  15.1 us
    all_to_all x1, blocking collectives, body(): lax.all_to_all(sums, ('dp', 'tensor'), split_axis=0, concat_axis=0, tiled...  11.7 us
    ppermute x15, waiting for transfers between devices, exchange(): return lax.ppermute(value, axis, [(i, i ^ flip) for i in range(size)])  10.7 us
    pallas_call x4, Pallas kernels, key_grads(): pl.pallas_call(functools.partial(keys_kernel, head, layout, n), in_specs=...  5.03 us
    pallas_call x1, Pallas kernels, project_streamed(): pl.pallas_call(streamed_kernel, grid_spec=pltpu.PrefetchScalarGridSpec(nu...  4.02 us
    pallas_call x3, Pallas kernels, project(): pl.pallas_call(functools.partial(project_kernel, acc is not None, heads),...  3.89 us
    pallas_call x4, Pallas kernels, value_grads(): pl.pallas_call(functools.partial(values_kernel, head, layout, n), in_spec...  2.78 us
  transfers between devices with their start and end apart: 15, of which 8 were waited for; matrix products, arithmetic and copies ran while one was open for 1% of the time, Pallas kernels for 38%

profile of v5, /device:TPU:0, one launch (start us, length us, event | category | flops | bytes accessed | tf_op | source)
XLA Modules:
  0.0 76.7 jit_solution(11971704761195144612)
XLA Ops:
  0.7 0.5 collective-permute-start.1
  1.2 2.6 %collective-permute-start = (bf16[256,2048]{1,0:T(8,128)(2,1)}, bf16[256,2048]{1,0:T(8,128)(2,1)S(1)}, u32[]{:S(2)}, u32[]{:S(2)}) collective-permute-start(bf16[256,2048]{1,0:T(8,128)(2,1)} %g_ref), channel_id=1, source_target_pairs={{0,2},{1,3},{2,0},{3,1},{4,6},{5,7},{6,4},{7,5},{8,10},{9,11},{10,... | collective-permute-start | bytes 3145736 | tf_op jit(solution)/shard_map/ppermute | solution.py:364
  3.8 1.3 %copy-done.3 = bf16[256,2048]{1,0:T(8,128)(2,1)S(1)} copy-done((bf16[256,2048]{1,0:T(8,128)(2,1)S(1)}, bf16[256,2048]{1,0:T(8,128)(2,1)}, u32[]{:S(2)}) %copy-start.3) | copy-done | bytes 1048600
  5.0 4.0 %project_streamed.1.refs_0_ = f32[1024,256]{1,0:T(8,128)S(1)} custom-call(s32[1]{0:T(128)} %bitcast.1.shard_ref, bf16[1024,8192]{1,0:T(8,128)(2,1)} %w_ref.3, bf16[256,2048]{1,0:T(8,128)(2,1)S(1)} %copy-done.3), custom_call_target="tpu_custom_call" | custom-call | flops 1073741824 | bytes 4194304 | tf_op jit(solution)/shard_map/project_streamed/pallas_call | solution.py:166
  9.1 0.1 fusion.1.bias_ref
  9.2 15.1 %forward.1 = (bf16[2,2048,1024]{2,1,0:T(8,128)(2,1)S(1)}, bf16[256,1024]{1,0:T(8,128)(2,1)}, bf16[2,128,1024]{2,1,0:T(8,128)(2,1)S(1)}, bf16[1024,8192]{1,0:T(8,128)(2,1)S(1)}) custom-call(s32[1]{0:T(128)} %bitcast.me_ref, bf16[256,1024]{1,0:T(8,128)(2,1)S(1)} %copy-done.1, bf16[2048,256]{1,0:T(8,128)(2,1)S(1)} %copy-done.2, bf16[256,256]{1,0:T(8,128)(2,1)S(1)} %copy-done.4, ...), custom_call_target="tpu_custom_call" | custom-call | flops 2415919104 | bytes 8388608 | tf_op jit(solution)/shard_map/forward/pallas_call | solution.py:139
  24.3 0.0 collective-permute-done.1.g_ref
  24.3 1.3 %project.3.refs_0_ = f32[1024,256]{1,0:T(8,128)S(1)} custom-call(s32[1]{0:T(128)S(6)} %xor.10.shard_ref, bf16[1024,8192]{1,0:T(8,128)(2,1)S(1)} %get-tuple-element.35.w_ref, bf16[256,2048]{1,0:T(8,128)(2,1)S(1)} %collective-permute-done.1.g_ref, f32[1024,256]{1,0:T(8,128)S(1)} %project_streamed.1.refs_0_), custom_call_target="tpu_custom_call" | custom-call | flops 1073741824 | bytes 4194304 | tf_op jit(solution)/shard_map/project/pallas_call | solution.py:216
  25.6 2.1 %collective-permute-done.g_ref = bf16[256,2048]{1,0:T(8,128)(2,1)S(1)} collective-permute-done((bf16[256,2048]{1,0:T(8,128)(2,1)}, bf16[256,2048]{1,0:T(8,128)(2,1)S(1)}, u32[]{:S(2)}, u32[]{:S(2)}) %collective-permute-start) | collective-permute-done | bytes 1048608 | tf_op jit(solution)/shard_map/ppermute | solution.py:364
  27.7 1.3 %project.4.refs_0_ = f32[1024,256]{1,0:T(8,128)S(1)} custom-call(s32[1]{0:T(128)S(6)} %xor.11.shard_ref, bf16[1024,8192]{1,0:T(8,128)(2,1)S(1)} %get-tuple-element.35.w_ref, bf16[256,2048]{1,0:T(8,128)(2,1)S(1)} %collective-permute-done.g_ref, f32[1024,256]{1,0:T(8,128)S(1)} %project.3.refs_0_), custom_call_target="tpu_custom_call" | custom-call | flops 1073741824 | bytes 4194304 | tf_op jit(solution)/shard_map/project/pallas_call | solution.py:216
  29.1 1.3 %collective-permute-done.2.g_ref = bf16[256,2048]{1,0:T(8,128)(2,1)S(1)} collective-permute-done((bf16[256,2048]{1,0:T(8,128)(2,1)S(1)}, bf16[256,2048]{1,0:T(8,128)(2,1)S(1)}, u32[]{:S(2)}, u32[]{:S(2)}) %collective-permute-start.2) | collective-permute-done | bytes 1048608 | tf_op jit(solution)/shard_map/ppermute | solution.py:364
  30.4 1.3 %project.5.da_ref = bf16[2,128,1024]{2,1,0:T(8,128)(2,1)S(1)} custom-call(s32[1]{0:T(128)S(6)} %xor.9.shard_ref, bf16[1024,8192]{1,0:T(8,128)(2,1)S(1)} %get-tuple-element.35.w_ref, bf16[256,2048]{1,0:T(8,128)(2,1)S(1)} %collective-permute-done.2.g_ref, f32[1024,256]{1,0:T(8,128)S(1)} %project.4.refs_0_), custom_call_target="tpu_custom_call" | custom-call | flops 1073741824 | bytes 4194304 | tf_op jit(solution)/shard_map/project/pallas_call | solution.py:216
  31.7 0.7 value_grads.4
  32.4 1.8 %collective-permute-start.3 = (bf16[1024,128]{1,0:T(8,128)(2,1)S(1)}, bf16[1024,128]{1,0:T(8,128)(2,1)S(1)}, u32[]{:S(2)}, u32[]{:S(2)}) collective-permute-start(bf16[1024,128]{1,0:T(8,128)(2,1)S(1)} %value_grads.4), channel_id=1, source_target_pairs={{0,4},{4,0},{8,12},{12,8},{16,20},{20,16},{24,28},{28,24},{1,5},{5... | collective-permute-start | bytes 786440 | tf_op jit(solution)/shard_map/ppermute | solution.py:364
  34.2 0.7 value_grads.5
  34.9 1.6 %collective-permute-start.12 = (bf16[1024,128]{1,0:T(8,128)(2,1)S(1)}, bf16[1024,128]{1,0:T(8,128)(2,1)S(1)}, u32[]{:S(2)}, u32[]{:S(2)}) collective-permute-start(bf16[1024,128]{1,0:T(8,128)(2,1)S(1)} %value_grads.5), channel_id=1, source_target_pairs={{0,8},{4,12},{8,0},{12,4},{16,24},{20,28},{24,16},{28,20},{1,9},{5... | collective-permute-start | bytes 786440 | tf_op jit(solution)/shard_map/ppermute | solution.py:364
  36.5 1.3 %key_grads.4 = bf16[1024,128]{1,0:T(8,128)(2,1)S(1)} custom-call(s32[1]{0:T(128)} %bitcast.me_ref, bf16[2,2048,1024]{2,1,0:T(8,128)(2,1)S(1)} %get-tuple-element.34.p_ref, bf16[2048,256]{1,0:T(8,128)(2,1)S(1)} %copy-done, bf16[2,128,1024]{2,1,0:T(8,128)(2,1)S(1)} %project.5.da_ref, bf16[2,128,1024]{2,1,0:T(8,128)(2,1)S(1)} %get-tuple-element.41.att_ref, ...), custom_call_target="tpu_custom_call" | custom-call | flops 8388608 | bytes 524288 | tf_op jit(solution)/shard_map/key_grads/pallas_call | solution.py:288
  37.8 1.3 %key_grads.5 = bf16[1024,128]{1,0:T(8,128)(2,1)S(1)} custom-call(s32[1]{0:T(128)} %bitcast.me_ref, bf16[2,2048,1024]{2,1,0:T(8,128)(2,1)S(1)} %get-tuple-element.34.p_ref, bf16[2048,256]{1,0:T(8,128)(2,1)S(1)} %copy-done, bf16[2,128,1024]{2,1,0:T(8,128)(2,1)S(1)} %project.5.da_ref, bf16[2,128,1024]{2,1,0:T(8,128)(2,1)S(1)} %get-tuple-element.41.att_ref, ...), custom_call_target="tpu_custom_call" | custom-call | flops 8388608 | bytes 524288 | tf_op jit(solution)/shard_map/key_grads/pallas_call | solution.py:288
  39.1 0.6 collective-permute-start.7
  39.7 0.2 collective-permute-start.4
  39.9 0.7 value_grads.6
  40.6 0.2 collective-permute-done.3
  40.8 0.7 value_grads.7
  41.5 2.7 %collective-permute-done.12 = bf16[1024,128]{1,0:T(8,128)(2,1)S(1)} collective-permute-done((bf16[1024,128]{1,0:T(8,128)(2,1)S(1)}, bf16[1024,128]{1,0:T(8,128)(2,1)S(1)}, u32[]{:S(2)}, u32[]{:S(2)}) %collective-permute-start.12) | collective-permute-done | bytes 262176 | tf_op jit(solution)/shard_map/ppermute | solution.py:364
  44.2 0.1 add_convert_fusion
  44.3 0.1 collective-permute-start.13
  44.3 0.1 add_convert_fusion.1
  44.4 2.6 %collective-permute-start.10 = (bf16[512,128]{1,0:T(8,128)(2,1)S(1)}, bf16[512,128]{1,0:T(8,128)(2,1)S(1)}, u32[]{:S(2)}, u32[]{:S(2)}) collective-permute-start(bf16[512,128]{1,0:T(8,128)(2,1)S(1)} %slice.55), channel_id=1, source_target_pairs={{0,16},{4,20},{8,24},{12,28},{16,0},{20,4},{24,8},{28,12},{1,17},{... | collective-permute-start | bytes 393224 | tf_op jit(solution)/shard_map/ppermute | solution.py:364
  47.1 1.3 %key_grads.7 = bf16[1024,128]{1,0:T(8,128)(2,1)S(1)} custom-call(s32[1]{0:T(128)} %bitcast.me_ref, bf16[2,2048,1024]{2,1,0:T(8,128)(2,1)S(1)} %get-tuple-element.34.p_ref, bf16[2048,256]{1,0:T(8,128)(2,1)S(1)} %copy-done, bf16[2,128,1024]{2,1,0:T(8,128)(2,1)S(1)} %project.5.da_ref, bf16[2,128,1024]{2,1,0:T(8,128)(2,1)S(1)} %get-tuple-element.41.att_ref, ...), custom_call_target="tpu_custom_call" | custom-call | flops 8388608 | bytes 524288 | tf_op jit(solution)/shard_map/key_grads/pallas_call | solution.py:288
  48.3 0.0 collective-permute-done.7
  48.4 0.1 add_convert_fusion.2
  48.5 2.1 %collective-permute-start.8 = (bf16[512,128]{1,0:T(8,128)(2,1)S(1)}, bf16[512,128]{1,0:T(8,128)(2,1)S(1)}, u32[]{:S(2)}, u32[]{:S(2)}) collective-permute-start(bf16[512,128]{1,0:T(8,128)(2,1)S(1)} %slice.52), channel_id=1, source_target_pairs={{0,8},{4,12},{8,0},{12,4},{16,24},{20,28},{24,16},{28,20},{1,9},{5... | collective-permute-start | bytes 393224 | tf_op jit(solution)/shard_map/ppermute | solution.py:364
  50.6 1.3 %key_grads.6 = bf16[1024,128]{1,0:T(8,128)(2,1)S(1)} custom-call(s32[1]{0:T(128)} %bitcast.me_ref, bf16[2,2048,1024]{2,1,0:T(8,128)(2,1)S(1)} %get-tuple-element.34.p_ref, bf16[2048,256]{1,0:T(8,128)(2,1)S(1)} %copy-done, bf16[2,128,1024]{2,1,0:T(8,128)(2,1)S(1)} %project.5.da_ref, bf16[2,128,1024]{2,1,0:T(8,128)(2,1)S(1)} %get-tuple-element.41.att_ref, ...), custom_call_target="tpu_custom_call" | custom-call | flops 8388608 | bytes 524288 | tf_op jit(solution)/shard_map/key_grads/pallas_call | solution.py:288
  51.9 0.6 collective-permute-done.4
  52.5 0.1 add_convert_fusion.3
  52.6 0.9 %collective-permute-start.5 = (bf16[512,128]{1,0:T(8,128)(2,1)S(1)}, bf16[512,128]{1,0:T(8,128)(2,1)S(1)}, u32[]{:S(2)}, u32[]{:S(2)}) collective-permute-start(bf16[512,128]{1,0:T(8,128)(2,1)S(1)} %slice.49), channel_id=1, source_target_pairs={{0,4},{4,0},{8,12},{12,8},{16,20},{20,16},{24,28},{28,24},{1,5},{5... | collective-permute-start | bytes 393224 | tf_op jit(solution)/shard_map/ppermute | solution.py:364
  53.5 0.0 collective-permute-done.13
  53.6 1.3 %collective-permute-start.14 = (bf16[256,128]{1,0:T(8,128)(2,1)S(1)}, bf16[256,128]{1,0:T(8,128)(2,1)S(1)}, u32[]{:S(2)}, u32[]{:S(2)}) collective-permute-start(bf16[256,128]{1,0:T(8,128)(2,1)S(1)} %slice.59), channel_id=1, source_target_pairs={{0,16},{4,20},{8,24},{12,28},{16,0},{20,4},{24,8},{28,12},{1,17},{... | collective-permute-start | bytes 196616 | tf_op jit(solution)/shard_map/ppermute | solution.py:364
  54.9 0.0 collective-permute-done.10
  54.9 2.0 %collective-permute-start.11 = (bf16[256,128]{1,0:T(8,128)(2,1)S(1)}, bf16[256,128]{1,0:T(8,128)(2,1)S(1)}, u32[]{:S(2)}, u32[]{:S(2)}) collective-permute-start(bf16[256,128]{1,0:T(8,128)(2,1)S(1)} %slice.56), channel_id=1, source_target_pairs={{0,8},{4,12},{8,0},{12,4},{16,24},{20,28},{24,16},{28,20},{1,9},{5... | collective-permute-start | bytes 196616 | tf_op jit(solution)/shard_map/ppermute | solution.py:364
  57.0 1.1 %collective-permute-start.9 = (bf16[256,128]{1,0:T(8,128)(2,1)S(1)}, bf16[256,128]{1,0:T(8,128)(2,1)S(1)}, u32[]{:S(2)}, u32[]{:S(2)}) collective-permute-start(bf16[256,128]{1,0:T(8,128)(2,1)S(1)} %slice.53), channel_id=1, source_target_pairs={{0,16},{4,20},{8,24},{12,28},{16,0},{20,4},{24,8},{28,12},{1,17},{... | collective-permute-start | bytes 196616 | tf_op jit(solution)/shard_map/ppermute | solution.py:364
  58.2 2.0 %collective-permute-start.6 = (bf16[256,128]{1,0:T(8,128)(2,1)S(1)}, bf16[256,128]{1,0:T(8,128)(2,1)S(1)}, u32[]{:S(2)}, u32[]{:S(2)}) collective-permute-start(bf16[256,128]{1,0:T(8,128)(2,1)S(1)} %slice.50), channel_id=1, source_target_pairs={{0,16},{4,20},{8,24},{12,28},{16,0},{20,4},{24,8},{28,12},{1,17},{... | collective-permute-start | bytes 196616 | tf_op jit(solution)/shard_map/ppermute | solution.py:364
  60.1 0.6 collective-permute-done.14.refs_7_
  60.7 2.4 %collective-permute-done.9.refs_3_ = bf16[256,128]{1,0:T(8,128)(2,1)S(1)} collective-permute-done((bf16[256,128]{1,0:T(8,128)(2,1)S(1)}, bf16[256,128]{1,0:T(8,128)(2,1)S(1)}, u32[]{:S(2)}, u32[]{:S(2)}) %collective-permute-start.9) | collective-permute-done | bytes 65568 | tf_op jit(solution)/shard_map/ppermute | solution.py:364
  63.1 0.7 collective-permute-done.6.refs_1_
  63.8 0.2 squares.1
  64.1 11.7 %all_to_all.11 = f32[32,1,128]{2,1,0:T(1,128)S(1)} all-to-all(f32[32,1,128]{2,1,0:T(1,128)S(1)} %bitcast.8), channel_id=1, replica_groups=mesh['dp'=8,'tensor'=4] {'dp','tensor'}, dimensions={0} | all-to-all | bytes 32768 | tf_op jit(solution)/shard_map/all_to_all | solution.py:442
  75.8 0.9 %update.1 = (f32[256,256]{1,0:T(8,128)}, f32[256,256]{1,0:T(8,128)}) custom-call(s32[1]{0:T(128)} %bitcast.me_ref, f32[32,128]{1,0:T(8,128)S(1)} %bitcast.7, bf16[2048,256]{1,0:T(8,128)(2,1)S(1)} %copy-done.2, bf16[2048,256]{1,0:T(8,128)(2,1)S(1)} %copy-done, f32[256,256]{1,0:T(8,128)S(1)} %get-tuple-element.51.grad_k_ref, ...), custom_call_target="tpu_custom_call" | custom-call | flops 262144 | bytes 1310720 | tf_op jit(solution)/shard_map/update/pallas_call | solution.py:346
  (29 shorter events, 0.3 us)
Async XLA Ops:
  0.6 8.6 %copy-start.2 = (bf16[2048,256]{1,0:T(8,128)(2,1)S(1)}, bf16[2048,256]{1,0:T(8,128)(2,1)}, u32[]{:S(2)}) copy-start(bf16[2048,256]{1,0:T(8,128)(2,1)} %keys_ref.1) | copy-start | bytes 3145732
  0.6 8.6 %copy-start = (bf16[2048,256]{1,0:T(8,128)(2,1)S(1)}, bf16[2048,256]{1,0:T(8,128)(2,1)}, u32[]{:S(2)}) copy-start(bf16[2048,256]{1,0:T(8,128)(2,1)} %vals_ref.1) | copy-start | bytes 3145732
  0.7 8.6 %copy-start.1 = (bf16[256,1024]{1,0:T(8,128)(2,1)S(1)}, bf16[256,1024]{1,0:T(8,128)(2,1)}, u32[]{:S(2)}) copy-start(bf16[256,1024]{1,0:T(8,128)(2,1)} %q_ref.9) | copy-start | bytes 1572868
  0.7 23.7 %collective-permute-start.1 = (bf16[256,2048]{1,0:T(8,128)(2,1)}, bf16[256,2048]{1,0:T(8,128)(2,1)S(1)}, u32[]{:S(2)}, u32[]{:S(2)}) collective-permute-start(bf16[256,2048]{1,0:T(8,128)(2,1)} %g_ref), channel_id=1, source_target_pairs={{0,1},{1,0},{2,3},{3,2},{4,5},{5,4},{6,7},{7,6},{8,9},{9,8},{10,11... | collective-permute-start | bytes 3145736 | tf_op jit(solution)/shard_map/ppermute | solution.py:364
  1.2 26.6 %collective-permute-start = (bf16[256,2048]{1,0:T(8,128)(2,1)}, bf16[256,2048]{1,0:T(8,128)(2,1)S(1)}, u32[]{:S(2)}, u32[]{:S(2)}) collective-permute-start(bf16[256,2048]{1,0:T(8,128)(2,1)} %g_ref), channel_id=1, source_target_pairs={{0,2},{1,3},{2,0},{3,1},{4,6},{5,7},{6,4},{7,5},{8,10},{9,11},{10,... | collective-permute-start | bytes 3145736 | tf_op jit(solution)/shard_map/ppermute | solution.py:364
  3.8 1.3 %copy-start.3 = (bf16[256,2048]{1,0:T(8,128)(2,1)S(1)}, bf16[256,2048]{1,0:T(8,128)(2,1)}, u32[]{:S(2)}) copy-start(bf16[256,2048]{1,0:T(8,128)(2,1)} %g_ref) | copy-start | bytes 3145732
  5.0 4.0 %copy-start.6 = (s32[1,256]{1,0:T(1,128)S(1)}, s32[1,256]{1,0:T(1,128)}, u32[]{:S(2)}) copy-start(s32[1,256]{1,0:T(1,128)} %param.15) | copy-start | bytes 3076
  5.0 4.2 %copy-start.4 = (bf16[256,256]{1,0:T(8,128)(2,1)S(1)}, bf16[256,256]{1,0:T(8,128)(2,1)}, u32[]{:S(2)}) copy-start(bf16[256,256]{1,0:T(8,128)(2,1)} %ks_ref.1) | copy-start | bytes 393220
  5.0 4.2 %copy-start.5 = (bf16[256,256]{1,0:T(8,128)(2,1)S(1)}, bf16[256,256]{1,0:T(8,128)(2,1)}, u32[]{:S(2)}) copy-start(bf16[256,256]{1,0:T(8,128)(2,1)} %vs_ref.1) | copy-start | bytes 393220
  27.7 2.7 %collective-permute-start.2 = (bf16[256,2048]{1,0:T(8,128)(2,1)S(1)}, bf16[256,2048]{1,0:T(8,128)(2,1)S(1)}, u32[]{:S(2)}, u32[]{:S(2)}) collective-permute-start(bf16[256,2048]{1,0:T(8,128)(2,1)S(1)} %collective-permute-done.g_ref), channel_id=1, source_target_pairs={{0,1},{1,0},{2,3},{3,2},{4,5},{5,4},{6,7},{7,6},{8,9},{9,8},{10,11... | collective-permute-start | bytes 3145736 | tf_op jit(solution)/shard_map/ppermute | solution.py:364
  32.4 8.4 %collective-permute-start.3 = (bf16[1024,128]{1,0:T(8,128)(2,1)S(1)}, bf16[1024,128]{1,0:T(8,128)(2,1)S(1)}, u32[]{:S(2)}, u32[]{:S(2)}) collective-permute-start(bf16[1024,128]{1,0:T(8,128)(2,1)S(1)} %value_grads.4), channel_id=1, source_target_pairs={{0,4},{4,0},{8,12},{12,8},{16,20},{20,16},{24,28},{28,24},{1,5},{5... | collective-permute-start | bytes 786440 | tf_op jit(solution)/shard_map/ppermute | solution.py:364
  34.9 9.3 %collective-permute-start.12 = (bf16[1024,128]{1,0:T(8,128)(2,1)S(1)}, bf16[1024,128]{1,0:T(8,128)(2,1)S(1)}, u32[]{:S(2)}, u32[]{:S(2)}) collective-permute-start(bf16[1024,128]{1,0:T(8,128)(2,1)S(1)} %value_grads.5), channel_id=1, source_target_pairs={{0,8},{4,12},{8,0},{12,4},{16,24},{20,28},{24,16},{28,20},{1,9},{5... | collective-permute-start | bytes 786440 | tf_op jit(solution)/shard_map/ppermute | solution.py:364
  39.1 9.3 %collective-permute-start.7 = (bf16[1024,128]{1,0:T(8,128)(2,1)S(1)}, bf16[1024,128]{1,0:T(8,128)(2,1)S(1)}, u32[]{:S(2)}, u32[]{:S(2)}) collective-permute-start(bf16[1024,128]{1,0:T(8,128)(2,1)S(1)} %key_grads.5), channel_id=1, source_target_pairs={{0,4},{4,0},{8,12},{12,8},{16,20},{20,16},{24,28},{28,24},{1,5},{5... | collective-permute-start | bytes 786440 | tf_op jit(solution)/shard_map/ppermute | solution.py:364
  39.7 12.8 %collective-permute-start.4 = (bf16[1024,128]{1,0:T(8,128)(2,1)S(1)}, bf16[1024,128]{1,0:T(8,128)(2,1)S(1)}, u32[]{:S(2)}, u32[]{:S(2)}) collective-permute-start(bf16[1024,128]{1,0:T(8,128)(2,1)S(1)} %key_grads.4), channel_id=1, source_target_pairs={{0,8},{4,12},{8,0},{12,4},{16,24},{20,28},{24,16},{28,20},{1,9},{5... | collective-permute-start | bytes 786440 | tf_op jit(solution)/shard_map/ppermute | solution.py:364
  44.3 9.3 %collective-permute-start.13 = (bf16[512,128]{1,0:T(8,128)(2,1)S(1)}, bf16[512,128]{1,0:T(8,128)(2,1)S(1)}, u32[]{:S(2)}, u32[]{:S(2)}) collective-permute-start(bf16[512,128]{1,0:T(8,128)(2,1)S(1)} %slice.58), channel_id=1, source_target_pairs={{0,4},{4,0},{8,12},{12,8},{16,20},{20,16},{24,28},{28,24},{1,5},{5... | collective-permute-start | bytes 393224 | tf_op jit(solution)/shard_map/ppermute | solution.py:364
  44.4 10.4 %collective-permute-start.10 = (bf16[512,128]{1,0:T(8,128)(2,1)S(1)}, bf16[512,128]{1,0:T(8,128)(2,1)S(1)}, u32[]{:S(2)}, u32[]{:S(2)}) collective-permute-start(bf16[512,128]{1,0:T(8,128)(2,1)S(1)} %slice.55), channel_id=1, source_target_pairs={{0,16},{4,20},{8,24},{12,28},{16,0},{20,4},{24,8},{28,12},{1,17},{... | collective-permute-start | bytes 393224 | tf_op jit(solution)/shard_map/ppermute | solution.py:364
  48.5 8.5 %collective-permute-start.8 = (bf16[512,128]{1,0:T(8,128)(2,1)S(1)}, bf16[512,128]{1,0:T(8,128)(2,1)S(1)}, u32[]{:S(2)}, u32[]{:S(2)}) collective-permute-start(bf16[512,128]{1,0:T(8,128)(2,1)S(1)} %slice.52), channel_id=1, source_target_pairs={{0,8},{4,12},{8,0},{12,4},{16,24},{20,28},{24,16},{28,20},{1,9},{5... | collective-permute-start | bytes 393224 | tf_op jit(solution)/shard_map/ppermute | solution.py:364
  52.6 5.5 %collective-permute-start.5 = (bf16[512,128]{1,0:T(8,128)(2,1)S(1)}, bf16[512,128]{1,0:T(8,128)(2,1)S(1)}, u32[]{:S(2)}, u32[]{:S(2)}) collective-permute-start(bf16[512,128]{1,0:T(8,128)(2,1)S(1)} %slice.49), channel_id=1, source_target_pairs={{0,4},{4,0},{8,12},{12,8},{16,20},{20,16},{24,28},{28,24},{1,5},{5... | collective-permute-start | bytes 393224 | tf_op jit(solution)/shard_map/ppermute | solution.py:364
  53.6 7.1 %collective-permute-start.14 = (bf16[256,128]{1,0:T(8,128)(2,1)S(1)}, bf16[256,128]{1,0:T(8,128)(2,1)S(1)}, u32[]{:S(2)}, u32[]{:S(2)}) collective-permute-start(bf16[256,128]{1,0:T(8,128)(2,1)S(1)} %slice.59), channel_id=1, source_target_pairs={{0,16},{4,20},{8,24},{12,28},{16,0},{20,4},{24,8},{28,12},{1,17},{... | collective-permute-start | bytes 196616 | tf_op jit(solution)/shard_map/ppermute | solution.py:364
  54.9 5.8 %collective-permute-start.11 = (bf16[256,128]{1,0:T(8,128)(2,1)S(1)}, bf16[256,128]{1,0:T(8,128)(2,1)S(1)}, u32[]{:S(2)}, u32[]{:S(2)}) collective-permute-start(bf16[256,128]{1,0:T(8,128)(2,1)S(1)} %slice.56), channel_id=1, source_target_pairs={{0,8},{4,12},{8,0},{12,4},{16,24},{20,28},{24,16},{28,20},{1,9},{5... | collective-permute-start | bytes 196616 | tf_op jit(solution)/shard_map/ppermute | solution.py:364
  57.0 6.1 %collective-permute-start.9 = (bf16[256,128]{1,0:T(8,128)(2,1)S(1)}, bf16[256,128]{1,0:T(8,128)(2,1)S(1)}, u32[]{:S(2)}, u32[]{:S(2)}) collective-permute-start(bf16[256,128]{1,0:T(8,128)(2,1)S(1)} %slice.53), channel_id=1, source_target_pairs={{0,16},{4,20},{8,24},{12,28},{16,0},{20,4},{24,8},{28,12},{1,17},{... | collective-permute-start | bytes 196616 | tf_op jit(solution)/shard_map/ppermute | solution.py:364
  58.2 5.7 %collective-permute-start.6 = (bf16[256,128]{1,0:T(8,128)(2,1)S(1)}, bf16[256,128]{1,0:T(8,128)(2,1)S(1)}, u32[]{:S(2)}, u32[]{:S(2)}) collective-permute-start(bf16[256,128]{1,0:T(8,128)(2,1)S(1)} %slice.50), channel_id=1, source_target_pairs={{0,16},{4,20},{8,24},{12,28},{16,0},{20,4},{24,8},{28,12},{1,17},{... | collective-permute-start | bytes 196616 | tf_op jit(solution)/shard_map/ppermute | solution.py:364
